TPU v7x, 128 devices: a whole 4x4x4 slice. The times are simulated.
128 devices in a mesh: terms: 8 (over x, core), sect: 16 (over y, z).
Axes of the slice: x: 4, y: 4, z: 4, core: 2. Of those that a mesh axis runs over, the one named last changes fastest.
Arguments:
- wavefunction: bfloat16 [32, 32, 128, 128], P('sect'), may hold values from -6 to 6
- left_operator: bfloat16 [192, 32, 128, 128], P('terms', 'sect'), may hold values from -0.5 to 0.5
- right_operator: bfloat16 [192, 32, 128, 128], P('terms', 'sect'), may hold values from -0.0390625 to 0.0390625
- allowed: int32 [32, 32], replicated, may hold values from 0 to 1, as said below
- block_units: int32 [32], replicated, may hold values from 1 to 8
Outputs:
- sigma: bfloat16 [32, 32, 128, 128], P('terms', 'sect')
Inputs may be any that keep to these rules, and one draw needn't show every extreme that they name: Each sector carries a charge of 0 or 1; allowed[l, m] is 1 exactly where the charges of l and m add to one common parity, so every row and every column holds at least one 1.
All inputs are finite; a program needn't handle non-finite values.
Results may differ from a plain program's by a relative error of at most 0.0049.
Values may be sent and summed in bfloat16 or wider, within the bound.
No kernel may reach another device: no remote copies, remote signals or barrier semaphores. Data moves between devices by JAX's collectives and lax.ppermute only.
A program may use at most 128 MiB of HBM per device.

v0:
```python
import jax
import jax.numpy as jnp
from jax import lax
from jax.sharding import PartitionSpec as P


def valid_rows(unit_counts, block_width):
    positions = jnp.arange(block_width, dtype=jnp.int32)
    limits = unit_counts * (block_width // 8)
    return (positions[None, :] < limits[:, None]).astype(jnp.bfloat16)


def shards(wavefunction, left_operator, right_operator, allowed, block_units):
    sec_dev = wavefunction.shape[0]
    sectors = wavefunction.shape[1]
    block_width = wavefunction.shape[2]
    sect_pos = lax.axis_index("sect")
    term_pos = lax.axis_index("terms")
    groups = lax.axis_size("terms")
    row_valid = valid_rows(block_units, block_width)
    own_rows = lax.dynamic_slice_in_dim(row_valid, sect_pos * sec_dev, sec_dev, 0)
    own_allowed = lax.dynamic_slice_in_dim(allowed, sect_pos * sec_dev, sec_dev, 0).astype(
        jnp.bfloat16
    )
    weights = (
        own_allowed[:, :, None, None] * own_rows[:, None, :, None] * row_valid[None, :, None, :]
    )
    masked = wavefunction * weights
    blocks = lax.all_gather(right_operator, "sect", axis=1, tiled=True)
    pieces = []
    for row in range(sec_dev):
        contracted = jnp.einsum(
            "kab,mbc->kmac", left_operator[:, row], masked[row], preferred_element_type=jnp.float32
        ).astype(jnp.bfloat16)
        pieces.append(
            jnp.einsum("kmac,kmdc->mad", contracted, blocks, preferred_element_type=jnp.float32)
        )
    rows_partial = jnp.stack(pieces, axis=0)
    partial_value = lax.all_to_all(rows_partial, "sect", split_axis=1, concat_axis=0, tiled=True)
    share_rows = sectors // groups
    summed = lax.psum(partial_value, "terms")
    owned = lax.dynamic_slice_in_dim(summed, term_pos * share_rows, share_rows, 0)
    out_allowed = lax.dynamic_slice(
        allowed, (term_pos * share_rows, sect_pos * sec_dev), (share_rows, sec_dev)
    ).astype(jnp.float32)
    left_valid = lax.dynamic_slice_in_dim(row_valid, term_pos * share_rows, share_rows, 0).astype(
        jnp.float32
    )
    right_valid = own_rows.astype(jnp.float32)
    out_weights = (
        out_allowed[:, :, None, None] * left_valid[:, None, :, None] * right_valid[None, :, None, :]
    )
    return (owned * out_weights).astype(jnp.bfloat16)


def solution(mesh):
    return jax.shard_map(
        shards,
        mesh=mesh,
        in_specs=(
            P("sect", None, None, None),
            P("terms", "sect", None, None),
            P("terms", "sect", None, None),
            P(),
            P(),
        ),
        out_specs=P("terms", "sect", None, None),
        check_vma=False,
    )
```

profile of v0, /device:TPU:7, one launch (start us, length us, event | category | flops | bytes accessed | tf_op | source)
XLA Modules:
  0.0 341.9 jit_solution(4118679197222673489)
XLA Ops:
  6.5 0.0 copy-start.2
  6.5 0.0 copy-start
  6.5 0.0 all-gather.2.cloned.1.call-start
  6.5 2.9 copy.8
  9.5 0.0 all-gather.2.cloned.1.call-update
  9.5 0.0 all-reduce.2.cloned.1.call-start
  9.6 0.7 dynamic-slice_convert_fusion.2
  10.3 0.0 copy-done.2
  10.3 0.1 fusion.24
  10.4 0.1 broadcast_multiply_fusion
  10.4 0.0 copy-done
  10.4 2.2 multiply_multiply_fusion
  12.7 0.0 copy-start.1
  12.7 153.6 %all-gather.2.cloned.1.call-done = bf16[24,32,128,128]{3,2,0,1:T(8,128)(2,1)} async-done(((bf16[24,2,128,128]{3,2,0,1:T(8,128)(2,1)}), bf16[24,32,128,128]{3,2,0,1:T(8,128)(2,1)}) %all-gather.2.cloned.1.call-update) | async-done | bytes 25165840 | tf_op jit(solution)/shard_map/all_gather | solution.py:29
  166.3 17.5 %fusion.13 = f32[1,32,128,128]{3,2,1,0:T(8,128)} fusion(bf16[24,32,128,128]{3,2,0,1:T(8,128)(2,1)} %all-gather.2.cloned.1.call-done, bf16[2,32,128,128]{3,2,1,0:T(8,128)(2,1)} %multiply_multiply_fusion, bf16[24,2,128,128]{3,2,1,0:T(8,128)(2,1)} %param.6), kind=kOutput, calls=%fused_computation.11 | convolution fusion | flops 6455033856 | bytes 29097984 | tf_op jit(solution)/shard_map/kmac,kmdc->mad/dot_general | solution.py:36
  183.8 0.0 copy-done.1
  183.8 17.4 %fusion.10 = f32[1,32,128,128]{3,2,1,0:T(8,128)} fusion(bf16[24,32,128,128]{3,2,0,1:T(8,128)(2,1)} %all-gather.2.cloned.1.call-done, bf16[2,32,128,128]{3,2,1,0:T(8,128)(2,1)S(1)} %copy-done.1, bf16[24,2,128,128]{3,2,1,0:T(8,128)(2,1)} %param.6), kind=kOutput, calls=%fused_computation.10 | convolution fusion | flops 6455033856 | bytes 29097984 | tf_op jit(solution)/shard_map/kmac,kmdc->mad/dot_general | solution.py:36
  201.2 2.5 pad_maximum_fusion
  203.7 0.5 copy.9
  204.2 54.1 %all_to_all.18 = f32[2,32,128,128]{3,2,0,1:T(8,128)S(1)} all-to-all(f32[2,32,128,128]{3,2,0,1:T(8,128)S(1)} %copy.9), channel_id=1, replica_groups=mesh['terms'=8,'sect'=16] {'sect'}, dimensions={1} | all-to-all | bytes 8388608 | tf_op jit(solution)/shard_map/all_to_all | solution.py:39
  258.3 2.3 copy.10
  260.6 0.0 all-reduce.2.cloned.1.call-update
  260.6 0.8 dynamic-slice_convert_fusion
  261.4 0.1 broadcast_multiply_fusion.1
  261.4 71.7 %all-reduce.2.cloned.1.call-done = f32[32,2,128,128]{3,2,1,0:T(8,128)} async-done(((f32[32,2,128,128]{3,2,1,0:T(8,128)}), f32[32,2,128,128]{3,2,1,0:T(8,128)}) %all-reduce.2.cloned.1.call-update) | async-done | bytes 4194320 | tf_op jit(solution)/shard_map/psum | solution.py:41
  333.1 1.9 multiply_convert_fusion
  (3 shorter events, 0.0 us)
Async XLA Ops:
  6.5 3.7 %copy-start.2 = (s32[32]{0:T(128)S(1)}, s32[32]{0:T(128)}, u32[]{:S(2)}) copy-start(s32[32]{0:T(128)} %param.9) | copy-start | bytes 388
  6.5 3.9 %copy-start = (bf16[2,32,128,128]{3,2,1,0:T(8,128)(2,1)S(1)}, bf16[2,32,128,128]{3,2,1,0:T(8,128)(2,1)}, u32[]{:S(2)}) copy-start(bf16[2,32,128,128]{3,2,1,0:T(8,128)(2,1)} %param.5) | copy-start | bytes 6291460
  6.5 159.8 %all-gather.2.cloned.1.call-start = ((), (), s32[]{:S(2)}) async-start(), calls=%async_computation.1 | async-start | bytes 26738688 | tf_op jit(solution)/shard_map/all_gather | solution.py:29
  9.5 323.6 %all-reduce.2.cloned.1.call-start = ((), (), s32[]{:S(2)}) async-start(), calls=%async_computation.2 | async-start | bytes 8388608 | tf_op jit(solution)/shard_map/psum | solution.py:41
  12.7 171.1 %copy-start.1 = (bf16[2,32,128,128]{3,2,1,0:T(8,128)(2,1)S(1)}, bf16[2,32,128,128]{3,2,1,0:T(8,128)(2,1)}, u32[]{:S(2)}) copy-start(bf16[2,32,128,128]{3,2,1,0:T(8,128)(2,1)} %multiply_multiply_fusion) | copy-start | bytes 6291460
Sparse Core Ops, SparseCore 0:
  9.6 156.6 all-gather.1
  260.7 72.3 all-reduce.1
where the time goes:
time: 343 us; the launch traced here: 342 us
  waiting for transfers between devices  225 us (66%)
  blocking collectives  54.1 us (16%)
  matrix products  34.9 us (10%)
  between operations  13.4 us (4%)
  other arithmetic  8.36 us (2%)
  local copies, waits for them, and re-layouts  5.7 us (2%)
    all_gather x1, waiting for transfers between devices, shards(): blocks = lax.all_gather(right_operator, 'sect', axis=1, tiled=True)  154 us
    psum x1, waiting for transfers between devices, shards(): summed = lax.psum(partial_value, 'terms')  71.7 us
    all_to_all x1, blocking collectives, shards(): lax.all_to_all(rows_partial, 'sect', split_axis=1, concat_axis=0, tiled=T...  54.1 us
    dot_general x2, matrix products, shards(): jnp.einsum('kmac,kmdc->mad', contracted, blocks, preferred_element_type=j...  34.9 us
  transfers between devices with their start and end apart: 2, of which 2 were waited for; matrix products, arithmetic and copies ran while one was open for 1% of the time, Pallas kernels for 0%

commit v1 on v0

v1 whole, which is shorter than its diff:
```python
import functools

import jax
import jax.numpy as jnp
from jax import lax
from jax.experimental import pallas as pl
from jax.experimental.pallas import tpu as pltpu
from jax.sharding import Mesh
from jax.sharding import PartitionSpec as P

B = 128
UNIT = B // 8


def shifted(size, step):
    return [(i, (i + step) % size) for i in range(size)]


def products_kernel(
    terms, half, pos, allowed, units, l0, l1, l3, l2a, l2b, r0, r1, r3, r2a, r2b, w, keep, send,
    ls, rs, t, lists, counts, sems,
):
    y, z, x, c = pos[0], pos[1], pos[2], pos[3]
    copies = []

    def fetch(src, dst):
        copy = pltpu.make_async_copy(src, dst, sems.at[len(copies)])
        copy.start()
        copies.append(copy)

    for i in range(2):
        for store, pieces in ((ls, (l0, l1, l2a, l2b, l3)), (rs, (r0, r1, r2a, r2b, r3))):
            p0, p1, p2a, p2b, p3 = pieces
            fetch(p0.at[:, i], store.at[0 + i])
            fetch(p1.at[:, i], store.at[2 + i])
            fetch(p3.at[:, i], store.at[6 + i])
            fetch(p2a.at[:, i], store.at[4 + i, pl.ds(0, half)])
            fetch(p2b.at[:, i], store.at[4 + i, pl.ds(half, terms - half)])

    def left_sector(slot):
        return 8 * lax.rem(y + 4 - slot // 2, 4) + 2 * z + lax.rem(slot, 2)

    def right_local(slot):
        return 2 * lax.rem(z + 4 - slot // 2, 4) + lax.rem(slot, 2)

    for cls in range(2):
        counts[cls] = 0
        counts[2 + cls] = 0

    @pl.loop(0, 8)
    def _(slot):
        cls = allowed[left_sector(slot), 0]
        n = counts[cls]
        lists[8 * cls + n] = slot
        counts[cls] = n + 1
        cls = (allowed[0, 8 * y + right_local(slot)] == allowed[0, 0]).astype(jnp.int32)
        n = counts[2 + cls]
        lists[16 + 8 * cls + n] = slot
        counts[2 + cls] = n + 1

    for copy in copies:
        copy.wait()

    row = lax.broadcasted_iota(jnp.int32, (B, B), 0)
    col = lax.broadcasted_iota(jnp.int32, (B, B), 1)

    def item(lefts, rights):
        nm = len(rights)
        locals_ = [right_local(m) for m in rights]
        for a, l in enumerate(lefts):
            rows = units[left_sector(l)] * UNIT
            blocks = []
            for q in locals_:
                inside = (row < rows) & (col < units[8 * y + q] * UNIT)
                block = w[q, l].astype(jnp.float32)
                blocks.append(jnp.where(inside, block, 0.0).astype(jnp.bfloat16))
            wide = blocks[0] if nm == 1 else jnp.concatenate(blocks, axis=1)
            part = jnp.dot(
                ls[l].reshape(terms * B, B), wide, preferred_element_type=jnp.float32
            ).astype(jnp.bfloat16).reshape(terms, B, nm * B)
            for k in range(terms):
                for b in range(nm):
                    t[b, a * B : (a + 1) * B, k * B : (k + 1) * B] = part[k][:, b * B : (b + 1) * B]
        for b, m in enumerate(rights):
            right = rs[m]
            wide = jnp.concatenate([right[k] for k in range(terms)], axis=1)
            total = lax.dot_general(
                t[b, : len(lefts) * B], wide, (((1,), (1,)), ((), ())),
                preferred_element_type=jnp.float32,
            ).astype(jnp.bfloat16)
            zq = locals_[b] // 2
            e, j = lax.rem(zq, 2), lax.rem(locals_[b], 2)
            mine = zq // 2 == c
            for a, l in enumerate(lefts):
                to = lax.rem(y + 4 - l // 2 + 4 - x, 4)
                i = lax.rem(l, 2)
                block = total[a * B : (a + 1) * B]

                @pl.when(mine)
                def _():
                    keep[to, e, i, j] = block

                @pl.when(jnp.logical_not(mine))
                def _():
                    send[to, e, i, j] = block

    @pl.loop(0, 2)
    def _(cls):
        nl, nm = counts[cls], counts[2 + cls]
        lb, mb = 8 * cls, 16 + 8 * cls

        @pl.loop(0, nl // 2)
        def _(a):
            pair = [lists[lb + 2 * a], lists[lb + 2 * a + 1]]

            @pl.loop(0, nm // 2)
            def _(b):
                item(pair, [lists[mb + 2 * b], lists[mb + 2 * b + 1]])

            @pl.when(lax.rem(nm, 2) == 1)
            def _():
                item(pair, [lists[mb + nm - 1]])

        @pl.when(lax.rem(nl, 2) == 1)
        def _():
            one = [lists[lb + nl - 1]]

            @pl.loop(0, nm // 2)
            def _(b):
                item(one, [lists[mb + 2 * b], lists[mb + 2 * b + 1]])

            @pl.when(lax.rem(nm, 2) == 1)
            def _():
                item(one, [lists[mb + nm - 1]])


def products(pos, allowed, units, lefts, rights, w):
    terms = lefts[0].shape[0]
    half = lefts[3].shape[0]
    smem = pl.BlockSpec(memory_space=pltpu.SMEM)
    anywhere = pl.BlockSpec(memory_space=pl.ANY)
    vmem = pl.BlockSpec(memory_space=pltpu.VMEM)
    out = jax.ShapeDtypeStruct((4, 2, 2, 2, B, B), jnp.bfloat16)
    return pl.pallas_call(
        functools.partial(products_kernel, terms, half),
        out_shape=(out, out),
        in_specs=[smem] * 3 + [anywhere] * 10 + [vmem],
        out_specs=(vmem, vmem),
        scratch_shapes=[
            pltpu.VMEM((8, terms, B, B), jnp.bfloat16),
            pltpu.VMEM((8, terms, B, B), jnp.bfloat16),
            pltpu.VMEM((2, 2 * B, terms * B), jnp.bfloat16),
            pltpu.SMEM((32,), jnp.int32),
            pltpu.SMEM((4,), jnp.int32),
            pltpu.SemaphoreType.DMA((20,)),
        ],
        compiler_params=pltpu.CompilerParams(vmem_limit_bytes=36 * 2**20),
        cost_estimate=pl.CostEstimate(
            flops=64 * terms * 4 * B**3, bytes_accessed=16 * 2**20, transcendentals=0
        ),
    )(pos, allowed, units, *lefts, *rights, w)


def ring(own, axis):
    half = own.shape[0] // 2
    prev = lax.ppermute(own, axis, shifted(4, 1))
    nxt = lax.ppermute(own, axis, shifted(4, -1))
    far_a = lax.ppermute(prev[:half], axis, shifted(4, 1))
    far_b = lax.ppermute(nxt[half:], axis, shifted(4, -1))
    return prev, nxt, far_a, far_b


def shards(wavefunction, left_operator, right_operator, allowed, block_units):
    x, c = lax.axis_index("x"), lax.axis_index("core")
    y, z = lax.axis_index("y"), lax.axis_index("z")
    q = 2 * x + c
    moved = []
    for d in range(4):
        piece = lax.dynamic_slice_in_dim(wavefunction, 8 * ((y + d) % 4) + q, 1, 1)[:, 0]
        moved.append(lax.ppermute(piece, "y", shifted(4, d)) if d else piece)
    w = lax.all_gather(jnp.concatenate(moved, axis=0), ("x", "core"), axis=0, tiled=False)
    lefts = (left_operator, *ring(left_operator, "y"))
    rights = (right_operator, *ring(right_operator, "z"))
    pos = jnp.stack([y, z, x, c]).astype(jnp.int32)
    keep, send = products(pos, allowed, block_units, lefts, rights, w)
    other = lax.ppermute(send, "core", shifted(2, 1))
    total = keep[0].astype(jnp.float32) + other[0].astype(jnp.float32)
    for d in range(1, 4):
        chip = (keep[d].astype(jnp.float32) + other[d].astype(jnp.float32)).astype(jnp.bfloat16)
        total = total + lax.ppermute(chip, "x", shifted(4, d)).astype(jnp.float32)
    lsec = 8 * x + 2 * z + jnp.arange(2)
    msec = (8 * y + 4 * c + jnp.arange(4)).reshape(2, 2)
    inside = jnp.arange(B)[None, :] < block_units[:, None] * UNIT
    mask = (
        (allowed[lsec[None, :, None], msec[:, None, :]] == 1)[..., None, None]
        & inside[lsec][None, :, None, :, None]
        & inside[msec][:, None, :, None, :]
    )
    final = jnp.where(mask, total, 0.0).astype(jnp.bfloat16)
    got = []
    for s in range(2):
        perm = [
            (cc * 4 + zz, (zz // 2) * 4 + 2 * cc + (s ^ (zz & 1)))
            for cc in range(2)
            for zz in range(4)
        ]
        piece = lax.dynamic_index_in_dim(final, s ^ (z & 1), 0, keepdims=False)
        got.append(lax.ppermute(piece, ("core", "z"), perm))
    odd = (z & 1) == 1
    first = jnp.where(odd, got[1], got[0])
    second = jnp.where(odd, got[0], got[1])
    return jnp.concatenate([first, second], axis=0)


def solution(mesh):
    fine = Mesh(mesh.devices.reshape(4, 2, 4, 4), ("x", "core", "y", "z"))
    return jax.shard_map(
        shards,
        mesh=fine,
        in_specs=(
            P(("y", "z"), None, None, None),
            P(("x", "core"), ("y", "z"), None, None),
            P(("x", "core"), ("y", "z"), None, None),
            P(),
            P(),
        ),
        out_specs=P(("x", "core"), ("y", "z"), None, None),
        check_vma=False,
    )
```

time: 343 us -> 162 us (0.47)
  waiting for transfers between devices: 225 us -> 64.6 us
  blocking collectives: 54.1 us -> 0 us
  matrix products: 34.9 us -> 0 us
  starting transfers between devices: 0.04 us -> 31.1 us
  Pallas kernels: 0 us -> 31 us
  local copies, waits for them, and re-layouts: 5.7 us -> 19 us
  other arithmetic: 8.36 us -> 3.3 us
    all_gather x1, waiting for transfers between devices: 154 us -> 0.01 us  [shards(): lax.all_gather(jnp.concatenate(moved, axis=0), ('x', 'core'), axis=0, til...]
    psum x1 -> x0, waiting for transfers between devices: 71.7 us -> none  [shards(): summed = lax.psum(partial_value, 'terms')]
    ppermute x0 -> x17, waiting for transfers between devices: none -> 64.6 us  [the longest x2 28.9 us: ring(): prev = lax.ppermute(own, axis, shifted(4, 1))]
    all_to_all x1 -> x0, blocking collectives: 54.1 us -> none  [shards(): lax.all_to_all(rows_partial, 'sect', split_axis=1, concat_axis=0, tiled=T...]
    dot_general x2 -> x0, matrix products: 34.9 us -> none  [shards(): jnp.einsum('kmac,kmdc->mad', contracted, blocks, preferred_element_type=j...]
    ppermute x0 -> x17, starting transfers between devices: none -> 31.1 us  [the longest x2 6.72 us: shards(): got.append(lax.ppermute(piece, ('core', 'z'), perm))]
    pallas_call x0 -> x1, Pallas kernels: none -> 31 us  [products(): pl.pallas_call(functools.partial(products_kernel, terms, half), out_shape...]
    unnamed x7 -> x26, local copies, waits for them, and re-layouts: 2.96 us -> 11.9 us
  transfers between devices with their start and end apart: 2 -> 18, of which waited for: 2 -> 12; matrix products, arithmetic and copies ran while one was open for 1% -> 4% of each run, Pallas kernels for 0% -> 0%
where the time goes in v1:
time: 162 us
  waiting for transfers between devices  64.6 us (40%)
  starting transfers between devices  31.1 us (19%)
  Pallas kernels  31 us (19%)
  local copies, waits for them, and re-layouts  19 us (12%)
  between operations  13.5 us (8%)
  other arithmetic  3.3 us (2%)
    pallas_call x1, Pallas kernels, products(): pl.pallas_call(functools.partial(products_kernel, terms, half), out_shape...  31 us
    ppermute x2, waiting for transfers between devices, ring(): prev = lax.ppermute(own, axis, shifted(4, 1))  28.9 us
    ppermute x3, waiting for transfers between devices, shards(): total = total + lax.ppermute(chip, 'x', shifted(4, d)).astype(jnp.float32)  12 us
    unnamed x26, local copies, waits for them, and re-layouts  11.9 us
    ppermute x2, waiting for transfers between devices, ring(): far_a = lax.ppermute(prev[:half], axis, shifted(4, 1))  11.5 us
    ppermute x2, starting transfers between devices, shards(): got.append(lax.ppermute(piece, ('core', 'z'), perm))  6.72 us
    ppermute x2, waiting for transfers between devices, shards(): got.append(lax.ppermute(piece, ('core', 'z'), perm))  5.86 us
    ppermute x2, starting transfers between devices, ring(): nxt = lax.ppermute(own, axis, shifted(4, -1))  4.78 us
  transfers between devices with their start and end apart: 18, of which 12 were waited for; matrix products, arithmetic and copies ran while one was open for 4% of the time, Pallas kernels for 0%

profile of v1, /device:TPU:7, one launch (start us, length us, event | category | flops | bytes accessed | tf_op | source)
XLA Modules:
  0.0 162.4 jit_solution(16783556828073063388)
XLA Ops:
  6.5 1.0 dynamic-slice_bitcast_fusion.5
  7.5 2.8 %collective-permute-start.10 = (bf16[2,128,128]{2,1,0:T(8,128)(2,1)S(1)}, bf16[2,128,128]{2,1,0:T(8,128)(2,1)S(1)}, u32[]{:S(2)}, u32[]{:S(2)}) collective-permute-start(bf16[2,128,128]{2,1,0:T(8,128)(2,1)S(1)} %get-tuple-element.14), channel_id=1, source_target_pairs={{0,12},{4,0},{8,4},{12,8},{1,13},{5,1},{9,5},{13,9},{2,14},{6,2},{... | collective-permute-start | bytes 196616 | tf_op jit(solution)/shard_map/ppermute | solution.py:180
  10.3 1.6 %collective-permute-start.9 = (bf16[2,128,128]{2,1,0:T(8,128)(2,1)S(1)}, bf16[2,128,128]{2,1,0:T(8,128)(2,1)S(1)}, u32[]{:S(2)}, u32[]{:S(2)}) collective-permute-start(bf16[2,128,128]{2,1,0:T(8,128)(2,1)S(1)} %get-tuple-element.15), channel_id=1, source_target_pairs={{0,8},{4,12},{8,0},{12,4},{1,9},{5,13},{9,1},{13,5},{2,10},{6,14},... | collective-permute-start | bytes 196616 | tf_op jit(solution)/shard_map/ppermute | solution.py:180
  11.9 3.2 %collective-permute-done.8 = bf16[2,128,128]{2,1,0:T(8,128)(2,1)S(1)} collective-permute-done((bf16[2,128,128]{2,1,0:T(8,128)(2,1)S(1)}, bf16[2,128,128]{2,1,0:T(8,128)(2,1)S(1)}, u32[]{:S(2)}, u32[]{:S(2)}) %collective-permute-start.8) | collective-permute-done | bytes 65568 | tf_op jit(solution)/shard_map/ppermute | solution.py:180
  15.1 0.4 collective-permute-done.9
  15.5 0.7 pad_maximum_fusion
  16.4 2.7 %collective-permute-start.1 = (bf16[24,2,128,128]{3,2,1,0:T(8,128)(2,1)}, bf16[24,2,128,128]{3,2,1,0:T(8,128)(2,1)S(1)}, u32[]{:S(2)}, u32[]{:S(2)}) collective-permute-start(bf16[24,2,128,128]{3,2,1,0:T(8,128)(2,1)} %l0.1), channel_id=1, source_target_pairs={{0,12},{4,0},{8,4},{12,8},{1,13},{5,1},{9,5},{13,9},{2,14},{6,2},{... | collective-permute-start | bytes 4718600 | tf_op jit(solution)/shard_map/ppermute | solution.py:167
  19.0 1.6 %collective-permute-start.4 = (bf16[24,2,128,128]{3,2,1,0:T(8,128)(2,1)}, bf16[24,2,128,128]{3,2,1,0:T(8,128)(2,1)S(1)}, u32[]{:S(2)}, u32[]{:S(2)}) collective-permute-start(bf16[24,2,128,128]{3,2,1,0:T(8,128)(2,1)} %r0.1), channel_id=1, source_target_pairs={{0,1},{1,2},{2,3},{3,0},{4,5},{5,6},{6,7},{7,4},{8,9},{9,10},{10,1... | collective-permute-start | bytes 4718600 | tf_op jit(solution)/shard_map/ppermute | solution.py:166
  20.7 2.1 %collective-permute-start.5 = (bf16[24,2,128,128]{3,2,1,0:T(8,128)(2,1)}, bf16[24,2,128,128]{3,2,1,0:T(8,128)(2,1)S(1)}, u32[]{:S(2)}, u32[]{:S(2)}) collective-permute-start(bf16[24,2,128,128]{3,2,1,0:T(8,128)(2,1)} %r0.1), channel_id=1, source_target_pairs={{0,3},{1,0},{2,1},{3,2},{4,7},{5,4},{6,5},{7,6},{8,11},{9,8},{10,9... | collective-permute-start | bytes 4718600 | tf_op jit(solution)/shard_map/ppermute | solution.py:167
  22.8 28.9 %collective-permute-done.l1 = bf16[24,2,128,128]{3,2,1,0:T(8,128)(2,1)S(1)} collective-permute-done((bf16[24,2,128,128]{3,2,1,0:T(8,128)(2,1)}, bf16[24,2,128,128]{3,2,1,0:T(8,128)(2,1)S(1)}, u32[]{:S(2)}, u32[]{:S(2)}) %collective-permute-start) | collective-permute-done | bytes 1572896 | tf_op jit(solution)/shard_map/ppermute | solution.py:166
  51.7 1.0 slice.54
  52.7 1.1 slice.55
  53.7 2.7 %collective-permute-start.3 = (bf16[12,2,128,128]{3,2,1,0:T(8,128)(2,1)}, bf16[12,2,128,128]{3,2,1,0:T(8,128)(2,1)S(1)}, u32[]{:S(2)}, u32[]{:S(2)}) collective-permute-start(bf16[12,2,128,128]{3,2,1,0:T(8,128)(2,1)} %slice.55), channel_id=1, source_target_pairs={{0,12},{4,0},{8,4},{12,8},{1,13},{5,1},{9,5},{13,9},{2,14},{6,2},{... | collective-permute-start | bytes 2359304 | tf_op jit(solution)/shard_map/ppermute | solution.py:169
  56.4 1.0 slice.56
  57.5 1.6 %collective-permute-start.6 = (bf16[12,2,128,128]{3,2,1,0:T(8,128)(2,1)}, bf16[12,2,128,128]{3,2,1,0:T(8,128)(2,1)}, u32[]{:S(2)}, u32[]{:S(2)}) collective-permute-start(bf16[12,2,128,128]{3,2,1,0:T(8,128)(2,1)} %slice.56), channel_id=1, source_target_pairs={{0,1},{1,2},{2,3},{3,0},{4,5},{5,6},{6,7},{7,4},{8,9},{9,10},{10,1... | collective-permute-start | bytes 2359304 | tf_op jit(solution)/shard_map/ppermute | solution.py:168
  59.1 0.9 slice.57
  60.0 1.2 copy-done.5
  61.2 2.1 %collective-permute-start.7 = (bf16[12,2,128,128]{3,2,1,0:T(8,128)(2,1)}, bf16[12,2,128,128]{3,2,1,0:T(8,128)(2,1)}, u32[]{:S(2)}, u32[]{:S(2)}) collective-permute-start(bf16[12,2,128,128]{3,2,1,0:T(8,128)(2,1)} %slice.57), channel_id=1, source_target_pairs={{0,3},{1,0},{2,1},{3,2},{4,7},{5,4},{6,5},{7,6},{8,11},{9,8},{10,9... | collective-permute-start | bytes 2359304 | tf_op jit(solution)/shard_map/ppermute | solution.py:169
  63.4 6.9 %collective-permute-done.2.l2a = bf16[12,2,128,128]{3,2,1,0:T(8,128)(2,1)S(1)} collective-permute-done((bf16[12,2,128,128]{3,2,1,0:T(8,128)(2,1)}, bf16[12,2,128,128]{3,2,1,0:T(8,128)(2,1)S(1)}, u32[]{:S(2)}, u32[]{:S(2)}) %collective-permute-start.2) | collective-permute-done | bytes 786464 | tf_op jit(solution)/shard_map/ppermute | solution.py:168
  70.4 0.9 copy-done.10
  71.3 4.6 %collective-permute-done.6.r2a = bf16[12,2,128,128]{3,2,1,0:T(8,128)(2,1)} collective-permute-done((bf16[12,2,128,128]{3,2,1,0:T(8,128)(2,1)}, bf16[12,2,128,128]{3,2,1,0:T(8,128)(2,1)}, u32[]{:S(2)}, u32[]{:S(2)}) %collective-permute-start.6) | collective-permute-done | bytes 786464 | tf_op jit(solution)/shard_map/ppermute | solution.py:168
  75.9 1.3 collective-permute-done.7.r2b
  77.2 1.4 copy-done.2
  78.6 1.4 copy-done.4
  80.0 1.4 copy-done.6
  81.4 1.6 copy-done.7
  83.0 1.4 copy-done.8
  84.4 1.4 copy-done.9
  85.8 1.1 copy-done.11
  86.9 31.0 %shard_map.55 = (bf16[4,2,2,2,128,128]{5,4,3,2,1,0:T(8,128)(2,1)S(1)}, bf16[4,2,2,2,128,128]{5,4,3,2,1,0:T(8,128)(2,1)}) custom-call(s32[4]{0:T(128)S(1)} %pad_add_fusion.pos, s32[32,32]{1,0:T(8,128)S(1)} %copy-done, s32[32]{0:T(128)S(1)} %copy-done.12, bf16[24,2,128,128]{3,2,1,0:T(8,128)(2,1)S(1)} %copy-done.8, ...), custom_call_target="tpu_custom_call" | custom-call | flops 12884901888 | bytes 16777216 | tf_op jit(solution)/shard_map/pallas_call | solution.py:144
  117.9 4.6 %collective-permute-start.11 = (bf16[4,2,2,2,128,128]{5,4,3,2,1,0:T(8,128)(2,1)}, bf16[4,2,2,2,128,128]{5,4,3,2,1,0:T(8,128)(2,1)S(1)}, u32[]{:S(2)}, u32[]{:S(2)}) collective-permute-start(bf16[4,2,2,2,128,128]{5,4,3,2,1,0:T(8,128)(2,1)} %get-tuple-element.8), channel_id=1, source_target_pairs={{0,16},{16,0},{1,17},{17,1},{2,18},{18,2},{3,19},{19,3},{4,20},{20... | collective-permute-start | bytes 3145736 | tf_op jit(solution)/shard_map/ppermute | solution.py:186
  122.6 0.1 reshape.100
  122.7 0.6 gather_fusion
  123.5 1.5 collective-permute-done.11
  125.0 0.3 fusion.4
  125.3 0.3 collective-permute-start.12
  125.6 2.1 %collective-permute-start.13 = (bf16[2,2,2,128,128]{4,3,2,1,0:T(8,128)(2,1)S(1)}, bf16[2,2,2,128,128]{4,3,2,1,0:T(8,128)(2,1)S(1)}, u32[]{:S(2)}, u32[]{:S(2)}) collective-permute-start(bf16[2,2,2,128,128]{4,3,2,1,0:T(8,128)(2,1)S(1)} %get-tuple-element.11), channel_id=1, source_target_pairs={{0,64},{32,96},{64,0},{96,32},{1,65},{33,97},{65,1},{97,33},{2,66}... | collective-permute-start | bytes 786440 | tf_op jit(solution)/shard_map/ppermute | solution.py:190
  127.8 0.6 gather_fusion.1
  128.4 0.6 gather_fusion.2
  129.0 3.9 %collective-permute-done.12 = bf16[2,2,2,128,128]{4,3,2,1,0:T(8,128)(2,1)S(1)} collective-permute-done((bf16[2,2,2,128,128]{4,3,2,1,0:T(8,128)(2,1)S(1)}, bf16[2,2,2,128,128]{4,3,2,1,0:T(8,128)(2,1)S(1)}, u32[]{:S(2)}, u32[]{:S(2)}) %collective-permute-start.12) | collective-permute-done | bytes 262176 | tf_op jit(solution)/shard_map/ppermute | solution.py:190
  132.9 1.4 collective-permute-done.13
  134.3 6.7 %collective-permute-done.14 = bf16[2,2,2,128,128]{4,3,2,1,0:T(8,128)(2,1)} collective-permute-done((bf16[2,2,2,128,128]{4,3,2,1,0:T(8,128)(2,1)S(1)}, bf16[2,2,2,128,128]{4,3,2,1,0:T(8,128)(2,1)}, u32[]{:S(2)}, u32[]{:S(2)}) %collective-permute-start.14) | collective-permute-done | bytes 262176 | tf_op jit(solution)/shard_map/ppermute | solution.py:190
  141.0 1.2 fusion.3
  142.3 4.8 %collective-permute-start.15 = (bf16[2,2,128,128]{3,2,1,0:T(8,128)(2,1)S(1)}, bf16[2,2,128,128]{3,2,1,0:T(8,128)(2,1)S(1)}, u32[]{:S(2)}, u32[]{:S(2)}) collective-permute-start(bf16[2,2,128,128]{3,2,1,0:T(8,128)(2,1)S(1)} %get-tuple-element.18), channel_id=1, source_target_pairs={{0,1},{1,0},{2,17},{3,16},{16,3},{17,2},{18,19},{19,18},{4,5},{5,4... | collective-permute-start | bytes 393224 | tf_op jit(solution)/shard_map/ppermute | solution.py:208
  147.1 1.9 %collective-permute-start.16 = (bf16[2,2,128,128]{3,2,1,0:T(8,128)(2,1)S(1)}, bf16[2,2,128,128]{3,2,1,0:T(8,128)(2,1)S(1)}, u32[]{:S(2)}, u32[]{:S(2)}) collective-permute-start(bf16[2,2,128,128]{3,2,1,0:T(8,128)(2,1)S(1)} %get-tuple-element.19), channel_id=1, source_target_pairs={{0,0},{1,1},{2,16},{3,17},{16,2},{17,3},{18,18},{19,19},{4,4},{5,5... | collective-permute-start | bytes 393224 | tf_op jit(solution)/shard_map/ppermute | solution.py:208
  149.0 0.7 collective-permute-done.15
  149.7 5.1 %collective-permute-done.16 = bf16[2,2,128,128]{3,2,1,0:T(8,128)(2,1)S(1)} collective-permute-done((bf16[2,2,128,128]{3,2,1,0:T(8,128)(2,1)S(1)}, bf16[2,2,128,128]{3,2,1,0:T(8,128)(2,1)S(1)}, u32[]{:S(2)}, u32[]{:S(2)}) %collective-permute-start.16) | collective-permute-done | bytes 131104 | tf_op jit(solution)/shard_map/ppermute | solution.py:208
  154.9 0.7 pad_maximum_fusion.1
  (46 shorter events, 0.8 us)
Async XLA Ops:
  6.5 70.6 %all-gather.3.cloned.1.call-start = ((), (), s32[]{:S(2)}) async-start(), calls=%async_computation | async-start | bytes 2359296 | tf_op jit(solution)/shard_map/all_gather | solution.py:181
  7.5 4.5 %collective-permute-start.10 = (bf16[2,128,128]{2,1,0:T(8,128)(2,1)S(1)}, bf16[2,128,128]{2,1,0:T(8,128)(2,1)S(1)}, u32[]{:S(2)}, u32[]{:S(2)}) collective-permute-start(bf16[2,128,128]{2,1,0:T(8,128)(2,1)S(1)} %get-tuple-element.14), channel_id=1, source_target_pairs={{0,12},{4,0},{8,4},{12,8},{1,13},{5,1},{9,5},{13,9},{2,14},{6,2},{... | collective-permute-start | bytes 196616 | tf_op jit(solution)/shard_map/ppermute | solution.py:180
  10.3 4.8 %collective-permute-start.8 = (bf16[2,128,128]{2,1,0:T(8,128)(2,1)S(1)}, bf16[2,128,128]{2,1,0:T(8,128)(2,1)S(1)}, u32[]{:S(2)}, u32[]{:S(2)}) collective-permute-start(bf16[2,128,128]{2,1,0:T(8,128)(2,1)S(1)} %get-tuple-element.13), channel_id=1, source_target_pairs={{0,4},{4,8},{8,12},{12,0},{1,5},{5,9},{9,13},{13,1},{2,6},{6,10},{... | collective-permute-start | bytes 196616 | tf_op jit(solution)/shard_map/ppermute | solution.py:180
  10.3 5.2 %collective-permute-start.9 = (bf16[2,128,128]{2,1,0:T(8,128)(2,1)S(1)}, bf16[2,128,128]{2,1,0:T(8,128)(2,1)S(1)}, u32[]{:S(2)}, u32[]{:S(2)}) collective-permute-start(bf16[2,128,128]{2,1,0:T(8,128)(2,1)S(1)} %get-tuple-element.15), channel_id=1, source_target_pairs={{0,8},{4,12},{8,0},{12,4},{1,9},{5,13},{9,1},{13,5},{2,10},{6,14},... | collective-permute-start | bytes 196616 | tf_op jit(solution)/shard_map/ppermute | solution.py:180
  16.3 35.4 %collective-permute-start = (bf16[24,2,128,128]{3,2,1,0:T(8,128)(2,1)}, bf16[24,2,128,128]{3,2,1,0:T(8,128)(2,1)S(1)}, u32[]{:S(2)}, u32[]{:S(2)}) collective-permute-start(bf16[24,2,128,128]{3,2,1,0:T(8,128)(2,1)} %l0.1), channel_id=1, source_target_pairs={{0,4},{4,8},{8,12},{12,0},{1,5},{5,9},{9,13},{13,1},{2,6},{6,10},{... | collective-permute-start | bytes 4718600 | tf_op jit(solution)/shard_map/ppermute | solution.py:166
  16.4 36.3 %collective-permute-start.1 = (bf16[24,2,128,128]{3,2,1,0:T(8,128)(2,1)}, bf16[24,2,128,128]{3,2,1,0:T(8,128)(2,1)S(1)}, u32[]{:S(2)}, u32[]{:S(2)}) collective-permute-start(bf16[24,2,128,128]{3,2,1,0:T(8,128)(2,1)} %l0.1), channel_id=1, source_target_pairs={{0,12},{4,0},{8,4},{12,8},{1,13},{5,1},{9,5},{13,9},{2,14},{6,2},{... | collective-permute-start | bytes 4718600 | tf_op jit(solution)/shard_map/ppermute | solution.py:167
  19.0 37.4 %collective-permute-start.4 = (bf16[24,2,128,128]{3,2,1,0:T(8,128)(2,1)}, bf16[24,2,128,128]{3,2,1,0:T(8,128)(2,1)S(1)}, u32[]{:S(2)}, u32[]{:S(2)}) collective-permute-start(bf16[24,2,128,128]{3,2,1,0:T(8,128)(2,1)} %r0.1), channel_id=1, source_target_pairs={{0,1},{1,2},{2,3},{3,0},{4,5},{5,6},{6,7},{7,4},{8,9},{9,10},{10,1... | collective-permute-start | bytes 4718600 | tf_op jit(solution)/shard_map/ppermute | solution.py:166
  20.7 38.4 %collective-permute-start.5 = (bf16[24,2,128,128]{3,2,1,0:T(8,128)(2,1)}, bf16[24,2,128,128]{3,2,1,0:T(8,128)(2,1)S(1)}, u32[]{:S(2)}, u32[]{:S(2)}) collective-permute-start(bf16[24,2,128,128]{3,2,1,0:T(8,128)(2,1)} %r0.1), channel_id=1, source_target_pairs={{0,3},{1,0},{2,1},{3,2},{4,7},{5,4},{6,5},{7,6},{8,11},{9,8},{10,9... | collective-permute-start | bytes 4718600 | tf_op jit(solution)/shard_map/ppermute | solution.py:167
  52.7 17.6 %collective-permute-start.2 = (bf16[12,2,128,128]{3,2,1,0:T(8,128)(2,1)}, bf16[12,2,128,128]{3,2,1,0:T(8,128)(2,1)S(1)}, u32[]{:S(2)}, u32[]{:S(2)}) collective-permute-start(bf16[12,2,128,128]{3,2,1,0:T(8,128)(2,1)} %slice.54), channel_id=1, source_target_pairs={{0,4},{4,8},{8,12},{12,0},{1,5},{5,9},{9,13},{13,1},{2,6},{6,10},{... | collective-permute-start | bytes 2359304 | tf_op jit(solution)/shard_map/ppermute | solution.py:168
  52.7 4.8 %copy-start.1 = (bf16[24,2,128,128]{3,2,1,0:T(8,128)(2,1)}, bf16[24,2,128,128]{3,2,1,0:T(8,128)(2,1)S(1)}, u32[]{:S(2)}) copy-start(bf16[24,2,128,128]{3,2,1,0:T(8,128)(2,1)S(1)} %collective-permute-done.1.l3) | copy-start | bytes 4718596
  53.7 23.4 %copy-start = (s32[32,32]{1,0:T(8,128)S(1)}, s32[32,32]{1,0:T(8,128)}, u32[]{:S(2)}) copy-start(s32[32,32]{1,0:T(8,128)} %allowed.1) | copy-start | bytes 12292
  53.7 23.4 %copy-start.12 = (s32[32]{0:T(128)S(1)}, s32[32]{0:T(128)}, u32[]{:S(2)}) copy-start(s32[32]{0:T(128)} %units.1) | copy-start | bytes 388
  53.7 16.6 %collective-permute-start.3 = (bf16[12,2,128,128]{3,2,1,0:T(8,128)(2,1)}, bf16[12,2,128,128]{3,2,1,0:T(8,128)(2,1)S(1)}, u32[]{:S(2)}, u32[]{:S(2)}) collective-permute-start(bf16[12,2,128,128]{3,2,1,0:T(8,128)(2,1)} %slice.55), channel_id=1, source_target_pairs={{0,12},{4,0},{8,4},{12,8},{1,13},{5,1},{9,5},{13,9},{2,14},{6,2},{... | collective-permute-start | bytes 2359304 | tf_op jit(solution)/shard_map/ppermute | solution.py:169
  56.4 3.6 %copy-start.3 = (bf16[24,2,128,128]{3,2,1,0:T(8,128)(2,1)}, bf16[24,2,128,128]{3,2,1,0:T(8,128)(2,1)S(1)}, u32[]{:S(2)}) copy-start(bf16[24,2,128,128]{3,2,1,0:T(8,128)(2,1)S(1)} %collective-permute-done.4.r1) | copy-start | bytes 4718596
  57.5 18.4 %collective-permute-start.6 = (bf16[12,2,128,128]{3,2,1,0:T(8,128)(2,1)}, bf16[12,2,128,128]{3,2,1,0:T(8,128)(2,1)}, u32[]{:S(2)}, u32[]{:S(2)}) collective-permute-start(bf16[12,2,128,128]{3,2,1,0:T(8,128)(2,1)} %slice.56), channel_id=1, source_target_pairs={{0,1},{1,2},{2,3},{3,0},{4,5},{5,6},{6,7},{7,4},{8,9},{9,10},{10,1... | collective-permute-start | bytes 2359304 | tf_op jit(solution)/shard_map/ppermute | solution.py:168
  60.0 1.2 copy-start.5
  61.2 15.9 %collective-permute-start.7 = (bf16[12,2,128,128]{3,2,1,0:T(8,128)(2,1)}, bf16[12,2,128,128]{3,2,1,0:T(8,128)(2,1)}, u32[]{:S(2)}, u32[]{:S(2)}) collective-permute-start(bf16[12,2,128,128]{3,2,1,0:T(8,128)(2,1)} %slice.57), channel_id=1, source_target_pairs={{0,3},{1,0},{2,1},{3,2},{4,7},{5,4},{6,5},{7,6},{8,11},{9,8},{10,9... | collective-permute-start | bytes 2359304 | tf_op jit(solution)/shard_map/ppermute | solution.py:169
  70.4 0.9 copy-start.10
  77.2 1.4 copy-start.2
  78.6 1.4 copy-start.4
  80.0 1.4 copy-start.6
  81.4 1.6 copy-start.7
  83.0 1.4 copy-start.8
  84.4 1.4 copy-start.9
  85.8 1.1 copy-start.11
  117.9 7.1 %collective-permute-start.11 = (bf16[4,2,2,2,128,128]{5,4,3,2,1,0:T(8,128)(2,1)}, bf16[4,2,2,2,128,128]{5,4,3,2,1,0:T(8,128)(2,1)S(1)}, u32[]{:S(2)}, u32[]{:S(2)}) collective-permute-start(bf16[4,2,2,2,128,128]{5,4,3,2,1,0:T(8,128)(2,1)} %get-tuple-element.8), channel_id=1, source_target_pairs={{0,16},{16,0},{1,17},{17,1},{2,18},{18,2},{3,19},{19,3},{4,20},{20... | collective-permute-start | bytes 3145736 | tf_op jit(solution)/shard_map/ppermute | solution.py:186
  125.3 7.6 %collective-permute-start.12 = (bf16[2,2,2,128,128]{4,3,2,1,0:T(8,128)(2,1)S(1)}, bf16[2,2,2,128,128]{4,3,2,1,0:T(8,128)(2,1)S(1)}, u32[]{:S(2)}, u32[]{:S(2)}) collective-permute-start(bf16[2,2,2,128,128]{4,3,2,1,0:T(8,128)(2,1)S(1)} %get-tuple-element.9), channel_id=1, source_target_pairs={{0,32},{32,64},{64,96},{96,0},{1,33},{33,65},{65,97},{97,1},{2,34}... | collective-permute-start | bytes 786440 | tf_op jit(solution)/shard_map/ppermute | solution.py:190
  125.6 8.7 %collective-permute-start.13 = (bf16[2,2,2,128,128]{4,3,2,1,0:T(8,128)(2,1)S(1)}, bf16[2,2,2,128,128]{4,3,2,1,0:T(8,128)(2,1)S(1)}, u32[]{:S(2)}, u32[]{:S(2)}) collective-permute-start(bf16[2,2,2,128,128]{4,3,2,1,0:T(8,128)(2,1)S(1)} %get-tuple-element.11), channel_id=1, source_target_pairs={{0,64},{32,96},{64,0},{96,32},{1,65},{33,97},{65,1},{97,33},{2,66}... | collective-permute-start | bytes 786440 | tf_op jit(solution)/shard_map/ppermute | solution.py:190
  127.7 13.3 %collective-permute-start.14 = (bf16[2,2,2,128,128]{4,3,2,1,0:T(8,128)(2,1)S(1)}, bf16[2,2,2,128,128]{4,3,2,1,0:T(8,128)(2,1)}, u32[]{:S(2)}, u32[]{:S(2)}) collective-permute-start(bf16[2,2,2,128,128]{4,3,2,1,0:T(8,128)(2,1)S(1)} %get-tuple-element.10), channel_id=1, source_target_pairs={{0,96},{32,0},{64,32},{96,64},{1,97},{33,1},{65,33},{97,65},{2,98}... | collective-permute-start | bytes 786440 | tf_op jit(solution)/shard_map/ppermute | solution.py:190
  142.3 7.5 %collective-permute-start.15 = (bf16[2,2,128,128]{3,2,1,0:T(8,128)(2,1)S(1)}, bf16[2,2,128,128]{3,2,1,0:T(8,128)(2,1)S(1)}, u32[]{:S(2)}, u32[]{:S(2)}) collective-permute-start(bf16[2,2,128,128]{3,2,1,0:T(8,128)(2,1)S(1)} %get-tuple-element.18), channel_id=1, source_target_pairs={{0,1},{1,0},{2,17},{3,16},{16,3},{17,2},{18,19},{19,18},{4,5},{5,4... | collective-permute-start | bytes 393224 | tf_op jit(solution)/shard_map/ppermute | solution.py:208
  147.1 7.8 %collective-permute-start.16 = (bf16[2,2,128,128]{3,2,1,0:T(8,128)(2,1)S(1)}, bf16[2,2,128,128]{3,2,1,0:T(8,128)(2,1)S(1)}, u32[]{:S(2)}, u32[]{:S(2)}) collective-permute-start(bf16[2,2,128,128]{3,2,1,0:T(8,128)(2,1)S(1)} %get-tuple-element.19), channel_id=1, source_target_pairs={{0,0},{1,1},{2,16},{3,17},{16,2},{17,3},{18,18},{19,19},{4,4},{5,5... | collective-permute-start | bytes 393224 | tf_op jit(solution)/shard_map/ppermute | solution.py:208
Sparse Core Ops, SparseCore 0:
  16.4 27.4 all-gather.2

commit v2 on v1

v2 whole, which is shorter than its diff:
```python
import functools

import jax
import jax.numpy as jnp
from jax import lax
from jax.experimental import pallas as pl
from jax.experimental.pallas import tpu as pltpu
from jax.sharding import Mesh
from jax.sharding import PartitionSpec as P

B = 128
UNIT = B // 8
CHUNK = 4


def shifted(size, step):
    return [(i, (i + step) % size) for i in range(size)]


def products_kernel(late, terms, pos, allowed, units, *refs):
    half = terms // 2
    pieces = 5 if late else 3
    lefts, refs = refs[:pieces], refs[pieces:]
    rights, refs = refs[:pieces], refs[pieces:]
    wave, refs = (refs[:1], refs[1:]) if late else (refs[:8], refs[8:])
    if late:
        refs = refs[2:]
    keep, send, *refs = refs
    if not late:
        wave_out, *refs = refs
    ls, rs, w, t, sums, lists, counts, seen, started, sems, out_sems = refs
    y, z, x, c = pos[0], pos[1], pos[2], pos[3]
    whole = []

    def fetch(src, dst, sem):
        copy = pltpu.make_async_copy(src, dst, sem)
        copy.start()
        return copy

    if late:
        new = 2 * lax.rem(z + 2, 4)
        whole.append(
            fetch(wave[0].at[:, pl.ds(6, 2)], w.at[:, pl.ds(6, 2)], sems.at[16])
        )
        whole.append(
            fetch(
                wave[0].at[pl.ds(new, 2), pl.ds(0, 6)],
                w.at[pl.ds(new, 2), pl.ds(0, 6)],
                sems.at[17],
            )
        )
    else:
        for at in range(8):
            chip = lax.rem(x + 4 - at % 4, 4)
            whole.append(fetch(wave[at], w.at[2 * chip + (c ^ (at // 4))], sems.at[16 + at]))
    order = (6, 7, 0, 1, 2, 3, 4, 5) if late else range(6)
    for slot in order:
        for side, (store, parts) in enumerate(((ls, lefts), (rs, rights))):
            sem = sems.at[8 * side + slot]
            i = slot % 2
            if slot < 6:
                fetch(parts[slot // 2].at[:, i], store.at[slot], sem)
            else:
                for part in range(2):
                    fetch(
                        parts[3 + part].at[:, i], store.at[slot, pl.ds(half * part, half)], sem
                    )
    for at in range(16):
        seen[at] = 0

    def ready(side, store, slot):
        at = 8 * side + slot

        @pl.when(seen[at] == 0)
        def _():
            pltpu.make_async_copy(store.at[slot], store.at[slot], sems.at[at]).wait()
            seen[at] = 1

    def shift_of(slot):
        pair = slot // 2
        return jnp.where(pair == 0, 0, jnp.where(pair == 1, 3, pair - 1))

    def left_sector(slot):
        return 8 * lax.rem(y + shift_of(slot), 4) + 2 * z + lax.rem(slot, 2)

    def right_local(slot):
        return 2 * lax.rem(z + shift_of(slot), 4) + lax.rem(slot, 2)

    for at in range(8):
        counts[at] = 0

    def enlist(slot):
        cls = allowed[left_sector(slot), 0]
        n = counts[cls]
        lists[8 * cls + n] = slot
        counts[cls] = n + 1
        cls = (allowed[0, 8 * y + right_local(slot)] == allowed[0, 0]).astype(jnp.int32)
        n = counts[2 + cls]
        lists[16 + 8 * cls + n] = slot
        counts[2 + cls] = n + 1

    if late:
        pl.loop(6, 8)(enlist)
        for at in range(4):
            counts[4 + at] = counts[at]
    pl.loop(0, 6)(enlist)
    if not late:
        for at in range(4):
            counts[4 + at] = counts[at]

    for copy in whole:
        copy.wait()

    if not late:
        row = lax.broadcasted_iota(jnp.int32, (B, B), 0)
        col = lax.broadcasted_iota(jnp.int32, (B, B), 1)

        @pl.loop(0, 8)
        def _(q):
            columns = (col < units[8 * y + q] * UNIT).astype(jnp.float32)
            for l in range(8):
                rows = (row < units[left_sector(l)] * UNIT).astype(jnp.float32)
                w[q, l] = w[q, l] * (rows * columns).astype(jnp.bfloat16)

        passed = fetch(w, wave_out, sems.at[16])
    else:
        counts[8] = 0

    def out_copy(other, to, e, i, j):
        return [
            pltpu.make_async_copy(
                sums.at[other, to, e, i, j],
                out.at[to, e, i, j],
                out_sems.at[(((other * 4 + to) * 2 + e) * 2 + i) * 2 + j],
            )
            for out in (keep, send)
        ]

    def item(left_slots, right_slots):
        nl, nm = len(left_slots), len(right_slots)
        locals_ = [right_local(m) for m in right_slots]
        for l in left_slots:
            ready(0, ls, l)
        for m in right_slots:
            ready(1, rs, m)
        for a, l in enumerate(left_slots):
            blocks = [w[q, l] for q in locals_]
            wide = blocks[0] if nm == 1 else jnp.concatenate(blocks, axis=1)
            for k0 in range(0, terms, CHUNK):
                n = min(CHUNK, terms - k0)
                part = jnp.dot(
                    ls[l, k0 : k0 + n].reshape(n * B, B), wide, preferred_element_type=jnp.float32
                ).astype(jnp.bfloat16).reshape(n, B, nm * B)
                for k in range(n):
                    for b in range(nm):
                        t[b, a * B : (a + 1) * B, (k0 + k) * B : (k0 + k + 1) * B] = part[k][
                            :, b * B : (b + 1) * B
                        ]
        for b, m in enumerate(right_slots):
            right = rs[m]
            wide = jnp.concatenate([right[k] for k in range(terms)], axis=1)
            total = lax.dot_general(
                t[b, : nl * B], wide, (((1,), (1,)), ((), ())), preferred_element_type=jnp.float32
            ).astype(jnp.bfloat16)
            owner = locals_[b] // 2
            e, j = lax.rem(owner, 2), lax.rem(locals_[b], 2)
            other = (owner // 2) ^ c
            for a, l in enumerate(left_slots):
                to = lax.rem(y + shift_of(l) + 4 - x, 4)
                sums[other, to, e, lax.rem(l, 2), j] = total[a * B : (a + 1) * B]
            if late:
                for l in left_slots:
                    to = lax.rem(y + shift_of(l) + 4 - x, 4)
                    kept, sent = out_copy(other, to, e, lax.rem(l, 2), j)
                    pl.when(other == 0)(kept.start)
                    pl.when(other == 1)(sent.start)
                    n = counts[8]
                    started[n] = (((other * 4 + to) * 2 + e) * 2 + lax.rem(l, 2)) * 2 + j
                    counts[8] = n + 1

    def rectangle(cls, l0, nl, m0, nm):
        lb, mb = 8 * cls + l0, 16 + 8 * cls + m0

        @pl.loop(0, nl // 2)
        def _(a):
            pair = [lists[lb + 2 * a], lists[lb + 2 * a + 1]]

            @pl.loop(0, nm // 2)
            def _(b):
                item(pair, [lists[mb + 2 * b], lists[mb + 2 * b + 1]])

            @pl.when(lax.rem(nm, 2) == 1)
            def _():
                item(pair, [lists[mb + nm - 1]])

        @pl.when(lax.rem(nl, 2) == 1)
        def _():
            one = [lists[lb + nl - 1]]

            @pl.loop(0, nm // 2)
            def _(b):
                item(one, [lists[mb + 2 * b], lists[mb + 2 * b + 1]])

            @pl.when(lax.rem(nm, 2) == 1)
            def _():
                item(one, [lists[mb + nm - 1]])

    @pl.loop(0, 4 if late else 2)
    def _(turn):
        cls = lax.rem(turn, 2)
        old = turn // 2
        new_l, all_l = counts[4 + cls], counts[cls]
        new_m, all_m = counts[6 + cls], counts[2 + cls]
        rectangle(
            cls,
            jnp.where(old == 1, new_l, 0),
            jnp.where(old == 1, all_l - new_l, new_l),
            0,
            jnp.where(old == 1, new_m, all_m),
        )

    for slot in order:
        ready(0, ls, slot)
        ready(1, rs, slot)
    if late:

        @pl.loop(0, counts[8])
        def _(n):
            pltpu.make_async_copy(
                sums.at[0, 0, 0, 0, 0], keep.at[0, 0, 0, 0], out_sems.at[started[n]]
            ).wait()
    else:
        done = [fetch(sums.at[0], keep, sems.at[24]), fetch(sums.at[1], send, sems.at[25])]
        for copy in (*done, passed):
            copy.wait()


def products(pos, allowed, units, lefts, rights, wave, before=()):
    terms = lefts[0].shape[0]
    smem = pl.BlockSpec(memory_space=pltpu.SMEM)
    hbm = pl.BlockSpec(memory_space=pl.ANY)
    out = jax.ShapeDtypeStruct((4, 2, 2, 2, B, B), jnp.bfloat16)
    masked = jax.ShapeDtypeStruct((8, 8, B, B), jnp.bfloat16)
    late = bool(before)
    n_in = 3 + 2 * len(lefts) + len(wave)
    return pl.pallas_call(
        functools.partial(products_kernel, late, terms),
        out_shape=(out, out) if late else (out, out, masked),
        in_specs=[smem] * 3 + [hbm] * (n_in - 3 + len(before)),
        out_specs=(hbm,) * (2 if late else 3),
        input_output_aliases={n_in: 0, n_in + 1: 1} if late else {},
        scratch_shapes=[
            pltpu.VMEM((8, terms, B, B), jnp.bfloat16),
            pltpu.VMEM((8, terms, B, B), jnp.bfloat16),
            pltpu.VMEM((8, 8, B, B), jnp.bfloat16),
            pltpu.VMEM((2, 2 * B, terms * B), jnp.bfloat16),
            pltpu.VMEM((2, 4, 2, 2, 2, B, B), jnp.bfloat16),
            pltpu.SMEM((32,), jnp.int32),
            pltpu.SMEM((9,), jnp.int32),
            pltpu.SMEM((16,), jnp.int32),
            pltpu.SMEM((64,), jnp.int32),
            pltpu.SemaphoreType.DMA((26,)),
            pltpu.SemaphoreType.DMA((64,)),
        ],
        compiler_params=pltpu.CompilerParams(vmem_limit_bytes=58 * 2**20),
        cost_estimate=pl.CostEstimate(
            flops=32 * terms * 4 * B**3, bytes_accessed=14 * 2**20, transcendentals=0
        ),
    )(pos, allowed, units, *lefts, *rights, *wave, *before)


def ring_near(own, axis):
    return lax.ppermute(own, axis, shifted(4, 1)), lax.ppermute(own, axis, shifted(4, -1))


def far_half(near):
    half = near[0].shape[0] // 2
    return near[0][:half], near[1][half:]


def ring_far(halves, axis):
    return (
        lax.ppermute(halves[0], axis, shifted(4, 1)),
        lax.ppermute(halves[1], axis, shifted(4, -1)),
    )


def swapped(size, bit):
    return [(i, i ^ bit) for i in range(size)]


def gather_wave(wavefunction, y, q, operators):
    def toward(owner):
        return lax.dynamic_slice_in_dim(wavefunction, 8 * owner + q, 1, 1)[:, 0]

    moved = [lax.ppermute(toward((y + d) % 4), "y", shifted(4, d)) for d in (1, 3, 2)]
    left, right = operators
    first, right = lax.optimization_barrier((moved[0], right))
    moved, left = lax.optimization_barrier(([first] + moved[1:], left))
    operators = left, right
    mine = jnp.concatenate([toward(y)] + moved)
    row = [mine] + [lax.ppermute(mine, "x", shifted(4, d)) for d in (1, 2, 3)]
    return row, operators


def share_wave(row):
    return (*row, *(lax.ppermute(part, "core", swapped(2, 1)) for part in row))


def add_cores(keep, send):
    other = lax.ppermute(send, "core", shifted(2, 1))
    both = [keep[d].astype(jnp.float32) + other[d].astype(jnp.float32) for d in range(4)]
    return both[0], [part.astype(jnp.bfloat16) for part in both[1:]]


def add_send(chips):
    return [lax.ppermute(part, "x", shifted(4, d + 1)) for d, part in enumerate(chips)]


def add_chips(own, chips):
    return (own + sum(part.astype(jnp.float32) for part in chips)).astype(jnp.bfloat16)


def shards(wavefunction, left_operator, right_operator, allowed, block_units):
    x, c = lax.axis_index("x"), lax.axis_index("core")
    y, z = lax.axis_index("y"), lax.axis_index("z")
    q = 2 * x + c
    row, (left_operator, right_operator) = gather_wave(
        wavefunction, y, q, (left_operator, right_operator)
    )
    near_l, near_r = ring_near(left_operator, "y"), ring_near(right_operator, "z")
    row, *near_l = lax.optimization_barrier((row, *near_l))
    wave = share_wave(row)
    lefts, rights = (left_operator, *near_l), (right_operator, *near_r)
    pos = jnp.stack([y, z, x, c]).astype(jnp.int32)
    far_l, far_r = far_half(near_l), far_half(near_r)
    *sums, masked = products(pos, allowed, block_units, lefts, rights, wave)
    lefts = (*lefts, *ring_far(far_l, "y"))
    rights = (*rights, *ring_far(far_r, "z"))
    keep, send = products(pos, allowed, block_units, lefts, rights, (masked,), sums)
    own, chips = add_cores(keep, send)
    final = add_chips(own, add_send(chips))

    got = []
    for s in range(2):
        perm = [
            (cc * 4 + zz, (zz // 2) * 4 + 2 * cc + (s ^ (zz & 1)))
            for cc in range(2)
            for zz in range(4)
        ]
        piece = lax.dynamic_index_in_dim(final, s ^ (z & 1), 0, keepdims=False)
        got.append(lax.ppermute(piece, ("core", "z"), perm))
    odd = (z & 1) == 1
    first = jnp.where(odd, got[1], got[0])
    second = jnp.where(odd, got[0], got[1])
    out = jnp.concatenate([first, second], axis=0)
    l0, m0 = 8 * x + 4 * c, 8 * y + 2 * z
    pairs = lax.dynamic_slice(allowed, (l0, m0), (4, 2))
    inside = jnp.arange(B)[None, :] < block_units[:, None] * UNIT
    mask = (
        (pairs == 1)[:, :, None, None]
        & lax.dynamic_slice_in_dim(inside, l0, 4, 0)[:, None, :, None]
        & lax.dynamic_slice_in_dim(inside, m0, 2, 0)[None, :, None, :]
    )
    return jnp.where(mask, out, jnp.bfloat16(0))


def solution(mesh):
    fine = Mesh(mesh.devices.reshape(4, 2, 4, 4), ("x", "core", "y", "z"))
    return jax.shard_map(
        shards,
        mesh=fine,
        in_specs=(
            P(("y", "z"), None, None, None),
            P(("x", "core"), ("y", "z"), None, None),
            P(("x", "core"), ("y", "z"), None, None),
            P(),
            P(),
        ),
        out_specs=P(("x", "core"), ("y", "z"), None, None),
        check_vma=False,
    )
```

time: 162 us -> 124 us (0.77)
  local copies, waits for them, and re-layouts: 19 us -> 2.59 us
  waiting for transfers between devices: 64.6 us -> 50 us
  between operations: 13.5 us -> 0.26 us
  starting transfers between devices: 31.1 us -> 34.7 us
  other arithmetic: 3.3 us -> 4.98 us
    ppermute x15 -> x22, waiting for transfers between devices: 58.7 us -> 44.3 us  [the longest x3 17.8 us: gather_wave(): row = [mine] + [lax.ppermute(mine, 'x', shifted(4, d)) for d in (1, 2, 3)]]
    unnamed x26 -> x22, local copies, waits for them, and re-layouts: 11.9 us -> 1.38 us
    ppermute x15 -> x22, starting transfers between devices: 24.4 us -> 28.6 us  [the longest x4 6.92 us: share_wave(): return (*row, *(lax.ppermute(part, 'core', swapped(2, 1)) for part in row))]
    slice x4, local copies, waits for them, and re-layouts: 4.04 us -> 0.21 us  [far_half(): return (near[0][:half], near[1][half:])]
    gather x4 -> x0, local copies, waits for them, and re-layouts: 1.79 us -> none  [the longest x1 0.64 us: shards(): allowed[lsec[None, :, None], msec[:, None, :]] == 1]
    pallas_call x1 -> x2, Pallas kernels: 31 us -> 31.3 us  [products(): pl.pallas_call(functools.partial(products_kernel, late, terms), out_shape...]
  transfers between devices with their start and end apart: 18 -> 24, of which waited for: 12 -> 11; matrix products, arithmetic and copies ran while one was open for 4% -> 1% of each run, Pallas kernels for 0% -> 13%
where the time goes in v2:
time: 124 us
  waiting for transfers between devices  50 us (40%)
  starting transfers between devices  34.7 us (28%)
  Pallas kernels  31.3 us (25%)
  other arithmetic  4.98 us (4%)
  local copies, waits for them, and re-layouts  2.59 us (2%)
    pallas_call x2, Pallas kernels, products(): pl.pallas_call(functools.partial(products_kernel, late, terms), out_shape...  31.3 us
    ppermute x3, waiting for transfers between devices, gather_wave(): row = [mine] + [lax.ppermute(mine, 'x', shifted(4, d)) for d in (1, 2, 3)]  17.8 us
    ppermute x3, waiting for transfers between devices, add_send(): lax.ppermute(part, 'x', shifted(4, d + 1))  12.4 us
    ppermute x2, waiting for transfers between devices, ring_near(): lax.ppermute(own, axis, shifted(4, 1))  8.51 us
    ppermute x4, starting transfers between devices, share_wave(): return (*row, *(lax.ppermute(part, 'core', swapped(2, 1)) for part in row))  6.92 us
    ppermute x2, starting transfers between devices, shards(): got.append(lax.ppermute(piece, ('core', 'z'), perm))  6.19 us
    ppermute x2, waiting for transfers between devices, shards(): got.append(lax.ppermute(piece, ('core', 'z'), perm))  5.78 us
    ppermute x2, starting transfers between devices, ring_far(): lax.ppermute(halves[1], axis, shifted(4, -1))  4.75 us
  transfers between devices with their start and end apart: 24, of which 11 were waited for; matrix products, arithmetic and copies ran while one was open for 1% of the time, Pallas kernels for 13%

profile of v2, /device:TPU:7, one launch (start us, length us, event | category | flops | bytes accessed | tf_op | source)
XLA Modules:
  0.0 123.9 jit_solution(15418016135232462820)
XLA Ops:
  0.0 1.0 dynamic-slice_bitcast_fusion.2
  1.0 1.4 %collective-permute-start = (bf16[2,128,128]{2,1,0:T(8,128)(2,1)S(1)}, bf16[2,128,128]{2,1,0:T(8,128)(2,1)S(1)}, u32[]{:S(2)}, u32[]{:S(2)}) collective-permute-start(bf16[2,128,128]{2,1,0:T(8,128)(2,1)S(1)} %get-tuple-element.44), channel_id=1, source_target_pairs={{0,4},{4,8},{8,12},{12,0},{1,5},{5,9},{9,13},{13,1},{2,6},{6,10},{... | collective-permute-start | bytes 196616 | tf_op jit(solution)/shard_map/ppermute | solution.py:296
  2.3 1.5 %collective-permute-start.1 = (bf16[2,128,128]{2,1,0:T(8,128)(2,1)S(1)}, bf16[2,128,128]{2,1,0:T(8,128)(2,1)S(1)}, u32[]{:S(2)}, u32[]{:S(2)}) collective-permute-start(bf16[2,128,128]{2,1,0:T(8,128)(2,1)S(1)} %get-tuple-element.43), channel_id=1, source_target_pairs={{0,12},{4,0},{8,4},{12,8},{1,13},{5,1},{9,5},{13,9},{2,14},{6,2},{... | collective-permute-start | bytes 196616 | tf_op jit(solution)/shard_map/ppermute | solution.py:296
  3.8 1.6 %collective-permute-start.2 = (bf16[2,128,128]{2,1,0:T(8,128)(2,1)S(1)}, bf16[2,128,128]{2,1,0:T(8,128)(2,1)S(1)}, u32[]{:S(2)}, u32[]{:S(2)}) collective-permute-start(bf16[2,128,128]{2,1,0:T(8,128)(2,1)S(1)} %get-tuple-element.45), channel_id=1, source_target_pairs={{0,8},{4,12},{8,0},{12,4},{1,9},{5,13},{9,1},{13,5},{2,10},{6,14},... | collective-permute-start | bytes 196616 | tf_op jit(solution)/shard_map/ppermute | solution.py:296
  5.4 3.0 %collective-permute-done.2 = bf16[2,128,128]{2,1,0:T(8,128)(2,1)S(1)} collective-permute-done((bf16[2,128,128]{2,1,0:T(8,128)(2,1)S(1)}, bf16[2,128,128]{2,1,0:T(8,128)(2,1)S(1)}, u32[]{:S(2)}, u32[]{:S(2)}) %collective-permute-start.2) | collective-permute-done | bytes 65568 | tf_op jit(solution)/shard_map/ppermute | solution.py:296
  8.5 0.3 collective-permute-start.6
  8.7 2.4 %collective-permute-start.7 = (bf16[24,2,128,128]{3,2,1,0:T(8,128)(2,1)}, bf16[24,2,128,128]{3,2,1,0:T(8,128)(2,1)S(1)}, u32[]{:S(2)}, u32[]{:S(2)}) collective-permute-start(bf16[24,2,128,128]{3,2,1,0:T(8,128)(2,1)} %refs_0_.1), channel_id=1, source_target_pairs={{0,12},{4,0},{8,4},{12,8},{1,13},{5,1},{9,5},{13,9},{2,14},{6,2},{... | collective-permute-start | bytes 4718600 | tf_op jit(solution)/shard_map/ppermute | solution.py:273
  11.1 1.6 %collective-permute-start.10 = (bf16[24,2,128,128]{3,2,1,0:T(8,128)(2,1)}, bf16[24,2,128,128]{3,2,1,0:T(8,128)(2,1)S(1)}, u32[]{:S(2)}, u32[]{:S(2)}) collective-permute-start(bf16[24,2,128,128]{3,2,1,0:T(8,128)(2,1)} %refs_5_), channel_id=1, source_target_pairs={{0,1},{1,2},{2,3},{3,0},{4,5},{5,6},{6,7},{7,4},{8,9},{9,10},{10,1... | collective-permute-start | bytes 4718600 | tf_op jit(solution)/shard_map/ppermute | solution.py:273
  12.8 2.1 %collective-permute-start.11 = (bf16[24,2,128,128]{3,2,1,0:T(8,128)(2,1)}, bf16[24,2,128,128]{3,2,1,0:T(8,128)(2,1)S(1)}, u32[]{:S(2)}, u32[]{:S(2)}) collective-permute-start(bf16[24,2,128,128]{3,2,1,0:T(8,128)(2,1)} %refs_5_), channel_id=1, source_target_pairs={{0,3},{1,0},{2,1},{3,2},{4,7},{5,4},{6,5},{7,6},{8,11},{9,8},{10,9... | collective-permute-start | bytes 4718600 | tf_op jit(solution)/shard_map/ppermute | solution.py:273
  15.0 0.3 collective-permute-start.3
  15.2 5.3 %collective-permute-done.3.refs_7_ = bf16[8,128,128]{2,1,0:T(8,128)(2,1)S(1)} collective-permute-done((bf16[8,128,128]{2,1,0:T(8,128)(2,1)S(1)}, bf16[8,128,128]{2,1,0:T(8,128)(2,1)S(1)}, u32[]{:S(2)}, u32[]{:S(2)}) %collective-permute-start.3) | collective-permute-done | bytes 262176 | tf_op jit(solution)/shard_map/ppermute | solution.py:302
  20.5 1.1 collective-permute-start.4
  21.7 5.6 %collective-permute-done.4.refs_8_ = bf16[8,128,128]{2,1,0:T(8,128)(2,1)S(1)} collective-permute-done((bf16[8,128,128]{2,1,0:T(8,128)(2,1)S(1)}, bf16[8,128,128]{2,1,0:T(8,128)(2,1)S(1)}, u32[]{:S(2)}, u32[]{:S(2)}) %collective-permute-start.4) | collective-permute-done | bytes 262176 | tf_op jit(solution)/shard_map/ppermute | solution.py:302
  27.3 0.8 collective-permute-start.5
  28.1 6.9 %collective-permute-done.5.refs_9_ = bf16[8,128,128]{2,1,0:T(8,128)(2,1)} collective-permute-done((bf16[8,128,128]{2,1,0:T(8,128)(2,1)S(1)}, bf16[8,128,128]{2,1,0:T(8,128)(2,1)}, u32[]{:S(2)}, u32[]{:S(2)}) %collective-permute-start.5) | collective-permute-done | bytes 262176 | tf_op jit(solution)/shard_map/ppermute | solution.py:302
  35.0 8.5 %collective-permute-done.6.refs_1_ = bf16[24,2,128,128]{3,2,1,0:T(8,128)(2,1)S(1)} collective-permute-done((bf16[24,2,128,128]{3,2,1,0:T(8,128)(2,1)}, bf16[24,2,128,128]{3,2,1,0:T(8,128)(2,1)S(1)}, u32[]{:S(2)}, u32[]{:S(2)}) %collective-permute-start.6) | collective-permute-done | bytes 1572896 | tf_op jit(solution)/shard_map/ppermute | solution.py:273
  43.5 3.2 %collective-permute-start.14 = (bf16[8,128,128]{2,1,0:T(8,128)(2,1)S(1)}, bf16[8,128,128]{2,1,0:T(8,128)(2,1)S(1)}, u32[]{:S(2)}, u32[]{:S(2)}) collective-permute-start(bf16[8,128,128]{2,1,0:T(8,128)(2,1)S(1)} %pad_maximum_fusion.refs_6_), channel_id=1, source_target_pairs={{0,16},{16,0},{1,17},{17,1},{2,18},{18,2},{3,19},{19,3},{4,20},{20... | collective-permute-start | bytes 786440 | tf_op jit(solution)/shard_map/ppermute | solution.py:307
  46.8 0.1 collective-permute-start.15
  46.9 0.4 collective-permute-start.16
  47.3 3.2 %collective-permute-start.17 = (bf16[8,128,128]{2,1,0:T(8,128)(2,1)}, bf16[8,128,128]{2,1,0:T(8,128)(2,1)}, u32[]{:S(2)}, u32[]{:S(2)}) collective-permute-start(bf16[8,128,128]{2,1,0:T(8,128)(2,1)} %collective-permute-done.5.refs_9_), channel_id=1, source_target_pairs={{0,16},{16,0},{1,17},{17,1},{2,18},{18,2},{3,19},{19,3},{4,20},{20... | collective-permute-start | bytes 786440 | tf_op jit(solution)/shard_map/ppermute | solution.py:307
  50.5 0.1 slice.37
  50.6 0.1 slice.48
  50.7 0.1 collective-permute-start.8
  50.8 0.1 slice.49
  50.8 2.7 %collective-permute-start.9 = (bf16[12,2,128,128]{3,2,1,0:T(8,128)(2,1)S(1)}, bf16[12,2,128,128]{3,2,1,0:T(8,128)(2,1)}, u32[]{:S(2)}, u32[]{:S(2)}) collective-permute-start(bf16[12,2,128,128]{3,2,1,0:T(8,128)(2,1)S(1)} %slice.37), channel_id=1, source_target_pairs={{0,12},{4,0},{8,4},{12,8},{1,13},{5,1},{9,5},{13,9},{2,14},{6,2},{... | collective-permute-start | bytes 2359304 | tf_op jit(solution)/shard_map/ppermute | solution.py:284
  53.6 0.6 copy-done.8
  54.3 0.7 copy-done.9
  55.0 2.0 %collective-permute-start.13 = (bf16[12,2,128,128]{3,2,1,0:T(8,128)(2,1)S(1)}, bf16[12,2,128,128]{3,2,1,0:T(8,128)(2,1)}, u32[]{:S(2)}, u32[]{:S(2)}) collective-permute-start(bf16[12,2,128,128]{3,2,1,0:T(8,128)(2,1)S(1)} %slice.49), channel_id=1, source_target_pairs={{0,3},{1,0},{2,1},{3,2},{4,7},{5,4},{6,5},{7,6},{8,11},{9,8},{10,9... | collective-permute-start | bytes 2359304 | tf_op jit(solution)/shard_map/ppermute | solution.py:284
  57.0 0.6 pad_add_fusion.pos
  57.7 16.3 %shard_map.55 = (bf16[4,2,2,2,128,128]{5,4,3,2,1,0:T(8,128)(2,1)}, bf16[4,2,2,2,128,128]{5,4,3,2,1,0:T(8,128)(2,1)}, bf16[8,8,128,128]{3,2,1,0:T(8,128)(2,1)}) custom-call(s32[4]{0:T(128)} %pad_add_fusion.pos, s32[32,32]{1,0:T(8,128)} %allowed.3, s32[32]{0:T(128)} %units.3, bf16[24,2,128,128]{3,2,1,0:T(8,128)(2,1)} %refs_0_.1, ...), custom_call_target="tpu_custom_call" | custom-call | flops 6442450944 | bytes 14680064 | tf_op jit(solution)/shard_map/pallas_call | solution.py:246
  74.0 15.0 %shard_map.56 = (bf16[4,2,2,2,128,128]{5,4,3,2,1,0:T(8,128)(2,1)}, bf16[4,2,2,2,128,128]{5,4,3,2,1,0:T(8,128)(2,1)}) custom-call(s32[4]{0:T(128)} %pad_add_fusion.pos, s32[32,32]{1,0:T(8,128)} %allowed.3, s32[32]{0:T(128)} %units.3, bf16[24,2,128,128]{3,2,1,0:T(8,128)(2,1)} %refs_0_.1, ...), custom_call_target="tpu_custom_call", output_to_operand_aliasing={{0}: (14, {}), {1}: (15, {})} | custom-call | flops 6442450944 | bytes 14680064 | tf_op jit(solution)/shard_map/pallas_call | solution.py:246
  89.0 1.3 %collective-permute-start.18 = (bf16[4,2,2,2,128,128]{5,4,3,2,1,0:T(8,128)(2,1)}, bf16[4,2,2,2,128,128]{5,4,3,2,1,0:T(8,128)(2,1)S(1)}, u32[]{:S(2)}, u32[]{:S(2)}) collective-permute-start(bf16[4,2,2,2,128,128]{5,4,3,2,1,0:T(8,128)(2,1)} %get-tuple-element.38), channel_id=1, source_target_pairs={{0,16},{16,0},{1,17},{17,1},{2,18},{18,2},{3,19},{19,3},{4,20},{20... | collective-permute-start | bytes 3145736 | tf_op jit(solution)/shard_map/ppermute | solution.py:311
  90.3 2.5 %collective-permute-done.18 = bf16[4,2,2,2,128,128]{5,4,3,2,1,0:T(8,128)(2,1)S(1)} collective-permute-done((bf16[4,2,2,2,128,128]{5,4,3,2,1,0:T(8,128)(2,1)}, bf16[4,2,2,2,128,128]{5,4,3,2,1,0:T(8,128)(2,1)S(1)}, u32[]{:S(2)}, u32[]{:S(2)}) %collective-permute-start.18) | collective-permute-done | bytes 1048608 | tf_op jit(solution)/shard_map/ppermute | solution.py:311
  92.8 1.3 %fusion.1 = (bf16[2,2,2,128,128]{4,3,2,1,0:T(8,128)(2,1)S(1)}, bf16[2,2,2,128,128]{4,3,2,1,0:T(8,128)(2,1)S(1)}, bf16[2,2,2,128,128]{4,3,2,1,0:T(8,128)(2,1)S(1)}) fusion(bf16[4,2,2,2,128,128]{5,4,3,2,1,0:T(8,128)(2,1)S(1)} %collective-permute-done.18, bf16[4,2,2,2,128,128]{5,4,3,2,1,0:T(8,128)(2,1)} %get-tuple-element.37), kind=kLoop, calls=%fused_computation.6 | loop fusion | flops 1572864 | bytes 2359296 | tf_op jit(solution)/shard_map/convert_element_type | solution.py:313
  94.1 0.3 collective-permute-start.19
  94.4 2.1 %collective-permute-start.20 = (bf16[2,2,2,128,128]{4,3,2,1,0:T(8,128)(2,1)S(1)}, bf16[2,2,2,128,128]{4,3,2,1,0:T(8,128)(2,1)S(1)}, u32[]{:S(2)}, u32[]{:S(2)}) collective-permute-start(bf16[2,2,2,128,128]{4,3,2,1,0:T(8,128)(2,1)S(1)} %get-tuple-element.41), channel_id=1, source_target_pairs={{0,64},{32,96},{64,0},{96,32},{1,65},{33,97},{65,1},{97,33},{2,66}... | collective-permute-start | bytes 786440 | tf_op jit(solution)/shard_map/ppermute | solution.py:317
  96.5 0.1 iota_compare_fusion
  96.6 0.8 dynamic-slice_compare_fusion
  97.4 4.3 %collective-permute-done.19 = bf16[2,2,2,128,128]{4,3,2,1,0:T(8,128)(2,1)S(1)} collective-permute-done((bf16[2,2,2,128,128]{4,3,2,1,0:T(8,128)(2,1)S(1)}, bf16[2,2,2,128,128]{4,3,2,1,0:T(8,128)(2,1)S(1)}, u32[]{:S(2)}, u32[]{:S(2)}) %collective-permute-start.19) | collective-permute-done | bytes 262176 | tf_op jit(solution)/shard_map/ppermute | solution.py:317
  101.7 1.4 %collective-permute-done.20 = bf16[2,2,2,128,128]{4,3,2,1,0:T(8,128)(2,1)S(1)} collective-permute-done((bf16[2,2,2,128,128]{4,3,2,1,0:T(8,128)(2,1)S(1)}, bf16[2,2,2,128,128]{4,3,2,1,0:T(8,128)(2,1)S(1)}, u32[]{:S(2)}, u32[]{:S(2)}) %collective-permute-start.20) | collective-permute-done | bytes 262176 | tf_op jit(solution)/shard_map/ppermute | solution.py:317
  103.1 6.6 %collective-permute-done.21 = bf16[2,2,2,128,128]{4,3,2,1,0:T(8,128)(2,1)S(1)} collective-permute-done((bf16[2,2,2,128,128]{4,3,2,1,0:T(8,128)(2,1)S(1)}, bf16[2,2,2,128,128]{4,3,2,1,0:T(8,128)(2,1)S(1)}, u32[]{:S(2)}, u32[]{:S(2)}) %collective-permute-start.21) | collective-permute-done | bytes 262176 | tf_op jit(solution)/shard_map/ppermute | solution.py:317
  109.7 1.1 fusion
  110.9 4.3 %collective-permute-start.22 = (bf16[2,2,128,128]{3,2,1,0:T(8,128)(2,1)S(1)}, bf16[2,2,128,128]{3,2,1,0:T(8,128)(2,1)S(1)}, u32[]{:S(2)}, u32[]{:S(2)}) collective-permute-start(bf16[2,2,128,128]{3,2,1,0:T(8,128)(2,1)S(1)} %get-tuple-element.48), channel_id=1, source_target_pairs={{0,1},{1,0},{2,17},{3,16},{16,3},{17,2},{18,19},{19,18},{4,5},{5,4... | collective-permute-start | bytes 393224 | tf_op jit(solution)/shard_map/ppermute | solution.py:352
  115.2 1.9 %collective-permute-start.23 = (bf16[2,2,128,128]{3,2,1,0:T(8,128)(2,1)S(1)}, bf16[2,2,128,128]{3,2,1,0:T(8,128)(2,1)S(1)}, u32[]{:S(2)}, u32[]{:S(2)}) collective-permute-start(bf16[2,2,128,128]{3,2,1,0:T(8,128)(2,1)S(1)} %get-tuple-element.49), channel_id=1, source_target_pairs={{0,0},{1,1},{2,16},{3,17},{16,2},{17,3},{18,18},{19,19},{4,4},{5,5... | collective-permute-start | bytes 393224 | tf_op jit(solution)/shard_map/ppermute | solution.py:352
  117.1 0.1 broadcast_and_fusion
  117.2 0.6 collective-permute-done.22
  117.8 5.1 %collective-permute-done.23 = bf16[2,2,128,128]{3,2,1,0:T(8,128)(2,1)S(1)} collective-permute-done((bf16[2,2,128,128]{3,2,1,0:T(8,128)(2,1)S(1)}, bf16[2,2,128,128]{3,2,1,0:T(8,128)(2,1)S(1)}, u32[]{:S(2)}, u32[]{:S(2)}) %collective-permute-start.23) | collective-permute-done | bytes 131104 | tf_op jit(solution)/shard_map/ppermute | solution.py:352
  123.0 0.9 and_select_fusion
  (42 shorter events, 0.3 us)
Async XLA Ops:
  1.0 4.5 %collective-permute-start = (bf16[2,128,128]{2,1,0:T(8,128)(2,1)S(1)}, bf16[2,128,128]{2,1,0:T(8,128)(2,1)S(1)}, u32[]{:S(2)}, u32[]{:S(2)}) collective-permute-start(bf16[2,128,128]{2,1,0:T(8,128)(2,1)S(1)} %get-tuple-element.44), channel_id=1, source_target_pairs={{0,4},{4,8},{8,12},{12,0},{1,5},{5,9},{9,13},{13,1},{2,6},{6,10},{... | collective-permute-start | bytes 196616 | tf_op jit(solution)/shard_map/ppermute | solution.py:296
  2.3 3.1 %collective-permute-start.1 = (bf16[2,128,128]{2,1,0:T(8,128)(2,1)S(1)}, bf16[2,128,128]{2,1,0:T(8,128)(2,1)S(1)}, u32[]{:S(2)}, u32[]{:S(2)}) collective-permute-start(bf16[2,128,128]{2,1,0:T(8,128)(2,1)S(1)} %get-tuple-element.43), channel_id=1, source_target_pairs={{0,12},{4,0},{8,4},{12,8},{1,13},{5,1},{9,5},{13,9},{2,14},{6,2},{... | collective-permute-start | bytes 196616 | tf_op jit(solution)/shard_map/ppermute | solution.py:296
  3.8 4.6 %collective-permute-start.2 = (bf16[2,128,128]{2,1,0:T(8,128)(2,1)S(1)}, bf16[2,128,128]{2,1,0:T(8,128)(2,1)S(1)}, u32[]{:S(2)}, u32[]{:S(2)}) collective-permute-start(bf16[2,128,128]{2,1,0:T(8,128)(2,1)S(1)} %get-tuple-element.45), channel_id=1, source_target_pairs={{0,8},{4,12},{8,0},{12,4},{1,9},{5,13},{9,1},{13,5},{2,10},{6,14},... | collective-permute-start | bytes 196616 | tf_op jit(solution)/shard_map/ppermute | solution.py:296
  8.5 35.1 %collective-permute-start.6 = (bf16[24,2,128,128]{3,2,1,0:T(8,128)(2,1)}, bf16[24,2,128,128]{3,2,1,0:T(8,128)(2,1)S(1)}, u32[]{:S(2)}, u32[]{:S(2)}) collective-permute-start(bf16[24,2,128,128]{3,2,1,0:T(8,128)(2,1)} %refs_0_.1), channel_id=1, source_target_pairs={{0,4},{4,8},{8,12},{12,0},{1,5},{5,9},{9,13},{13,1},{2,6},{6,10},{... | collective-permute-start | bytes 4718600 | tf_op jit(solution)/shard_map/ppermute | solution.py:273
  8.7 34.8 %collective-permute-start.7 = (bf16[24,2,128,128]{3,2,1,0:T(8,128)(2,1)}, bf16[24,2,128,128]{3,2,1,0:T(8,128)(2,1)S(1)}, u32[]{:S(2)}, u32[]{:S(2)}) collective-permute-start(bf16[24,2,128,128]{3,2,1,0:T(8,128)(2,1)} %refs_0_.1), channel_id=1, source_target_pairs={{0,12},{4,0},{8,4},{12,8},{1,13},{5,1},{9,5},{13,9},{2,14},{6,2},{... | collective-permute-start | bytes 4718600 | tf_op jit(solution)/shard_map/ppermute | solution.py:273
  11.1 36.1 %collective-permute-start.10 = (bf16[24,2,128,128]{3,2,1,0:T(8,128)(2,1)}, bf16[24,2,128,128]{3,2,1,0:T(8,128)(2,1)S(1)}, u32[]{:S(2)}, u32[]{:S(2)}) collective-permute-start(bf16[24,2,128,128]{3,2,1,0:T(8,128)(2,1)} %refs_5_), channel_id=1, source_target_pairs={{0,1},{1,2},{2,3},{3,0},{4,5},{5,6},{6,7},{7,4},{8,9},{9,10},{10,1... | collective-permute-start | bytes 4718600 | tf_op jit(solution)/shard_map/ppermute | solution.py:273
  12.8 37.9 %collective-permute-start.11 = (bf16[24,2,128,128]{3,2,1,0:T(8,128)(2,1)}, bf16[24,2,128,128]{3,2,1,0:T(8,128)(2,1)S(1)}, u32[]{:S(2)}, u32[]{:S(2)}) collective-permute-start(bf16[24,2,128,128]{3,2,1,0:T(8,128)(2,1)} %refs_5_), channel_id=1, source_target_pairs={{0,3},{1,0},{2,1},{3,2},{4,7},{5,4},{6,5},{7,6},{8,11},{9,8},{10,9... | collective-permute-start | bytes 4718600 | tf_op jit(solution)/shard_map/ppermute | solution.py:273
  14.9 42.7 %copy-start.4 = (bf16[8,128,128]{2,1,0:T(8,128)(2,1)}, bf16[8,128,128]{2,1,0:T(8,128)(2,1)S(1)}, u32[]{:S(2)}) copy-start(bf16[8,128,128]{2,1,0:T(8,128)(2,1)S(1)} %pad_maximum_fusion.refs_6_) | copy-start | bytes 786436
  15.0 5.6 %collective-permute-start.3 = (bf16[8,128,128]{2,1,0:T(8,128)(2,1)S(1)}, bf16[8,128,128]{2,1,0:T(8,128)(2,1)S(1)}, u32[]{:S(2)}, u32[]{:S(2)}) collective-permute-start(bf16[8,128,128]{2,1,0:T(8,128)(2,1)S(1)} %pad_maximum_fusion.refs_6_), channel_id=1, source_target_pairs={{0,32},{32,64},{64,96},{96,0},{1,33},{33,65},{65,97},{97,1},{2,34}... | collective-permute-start | bytes 786440 | tf_op jit(solution)/shard_map/ppermute | solution.py:302
  20.5 33.1 %copy-start.5 = (bf16[8,128,128]{2,1,0:T(8,128)(2,1)}, bf16[8,128,128]{2,1,0:T(8,128)(2,1)S(1)}, u32[]{:S(2)}) copy-start(bf16[8,128,128]{2,1,0:T(8,128)(2,1)S(1)} %collective-permute-done.3.refs_7_) | copy-start | bytes 786436
  20.5 6.7 %collective-permute-start.4 = (bf16[8,128,128]{2,1,0:T(8,128)(2,1)S(1)}, bf16[8,128,128]{2,1,0:T(8,128)(2,1)S(1)}, u32[]{:S(2)}, u32[]{:S(2)}) collective-permute-start(bf16[8,128,128]{2,1,0:T(8,128)(2,1)S(1)} %pad_maximum_fusion.refs_6_), channel_id=1, source_target_pairs={{0,64},{32,96},{64,0},{96,32},{1,65},{33,97},{65,1},{97,33},{2,66}... | collective-permute-start | bytes 786440 | tf_op jit(solution)/shard_map/ppermute | solution.py:302
  27.3 26.3 %copy-start.6 = (bf16[8,128,128]{2,1,0:T(8,128)(2,1)}, bf16[8,128,128]{2,1,0:T(8,128)(2,1)S(1)}, u32[]{:S(2)}) copy-start(bf16[8,128,128]{2,1,0:T(8,128)(2,1)S(1)} %collective-permute-done.4.refs_8_) | copy-start | bytes 786436
  27.3 7.7 %collective-permute-start.5 = (bf16[8,128,128]{2,1,0:T(8,128)(2,1)S(1)}, bf16[8,128,128]{2,1,0:T(8,128)(2,1)}, u32[]{:S(2)}, u32[]{:S(2)}) collective-permute-start(bf16[8,128,128]{2,1,0:T(8,128)(2,1)S(1)} %pad_maximum_fusion.refs_6_), channel_id=1, source_target_pairs={{0,96},{32,0},{64,32},{96,64},{1,97},{33,1},{65,33},{97,65},{2,98}... | collective-permute-start | bytes 786440 | tf_op jit(solution)/shard_map/ppermute | solution.py:302
  43.5 7.1 %copy-start = (bf16[24,2,128,128]{3,2,1,0:T(8,128)(2,1)}, bf16[24,2,128,128]{3,2,1,0:T(8,128)(2,1)S(1)}, u32[]{:S(2)}) copy-start(bf16[24,2,128,128]{3,2,1,0:T(8,128)(2,1)S(1)} %collective-permute-done.6.refs_1_) | copy-start | bytes 4718596
  43.5 7.1 %copy-start.1 = (bf16[24,2,128,128]{3,2,1,0:T(8,128)(2,1)}, bf16[24,2,128,128]{3,2,1,0:T(8,128)(2,1)S(1)}, u32[]{:S(2)}) copy-start(bf16[24,2,128,128]{3,2,1,0:T(8,128)(2,1)S(1)} %collective-permute-done.7.refs_2_) | copy-start | bytes 4718596
  43.5 7.3 %collective-permute-start.14 = (bf16[8,128,128]{2,1,0:T(8,128)(2,1)S(1)}, bf16[8,128,128]{2,1,0:T(8,128)(2,1)S(1)}, u32[]{:S(2)}, u32[]{:S(2)}) collective-permute-start(bf16[8,128,128]{2,1,0:T(8,128)(2,1)S(1)} %pad_maximum_fusion.refs_6_), channel_id=1, source_target_pairs={{0,16},{16,0},{1,17},{17,1},{2,18},{18,2},{3,19},{19,3},{4,20},{20... | collective-permute-start | bytes 786440 | tf_op jit(solution)/shard_map/ppermute | solution.py:307
  46.8 6.8 %collective-permute-start.15 = (bf16[8,128,128]{2,1,0:T(8,128)(2,1)S(1)}, bf16[8,128,128]{2,1,0:T(8,128)(2,1)S(1)}, u32[]{:S(2)}, u32[]{:S(2)}) collective-permute-start(bf16[8,128,128]{2,1,0:T(8,128)(2,1)S(1)} %collective-permute-done.3.refs_7_), channel_id=1, source_target_pairs={{0,16},{16,0},{1,17},{17,1},{2,18},{18,2},{3,19},{19,3},{4,20},{20... | collective-permute-start | bytes 786440 | tf_op jit(solution)/shard_map/ppermute | solution.py:307
  46.9 6.7 %collective-permute-start.16 = (bf16[8,128,128]{2,1,0:T(8,128)(2,1)S(1)}, bf16[8,128,128]{2,1,0:T(8,128)(2,1)S(1)}, u32[]{:S(2)}, u32[]{:S(2)}) collective-permute-start(bf16[8,128,128]{2,1,0:T(8,128)(2,1)S(1)} %collective-permute-done.4.refs_8_), channel_id=1, source_target_pairs={{0,16},{16,0},{1,17},{17,1},{2,18},{18,2},{3,19},{19,3},{4,20},{20... | collective-permute-start | bytes 786440 | tf_op jit(solution)/shard_map/ppermute | solution.py:307
  47.3 6.3 %copy-start.2 = (bf16[24,2,128,128]{3,2,1,0:T(8,128)(2,1)}, bf16[24,2,128,128]{3,2,1,0:T(8,128)(2,1)S(1)}, u32[]{:S(2)}) copy-start(bf16[24,2,128,128]{3,2,1,0:T(8,128)(2,1)S(1)} %collective-permute-done.10.refs_4_.refs_6_) | copy-start | bytes 4718596
  47.3 10.4 %collective-permute-start.17 = (bf16[8,128,128]{2,1,0:T(8,128)(2,1)}, bf16[8,128,128]{2,1,0:T(8,128)(2,1)}, u32[]{:S(2)}, u32[]{:S(2)}) collective-permute-start(bf16[8,128,128]{2,1,0:T(8,128)(2,1)} %collective-permute-done.5.refs_9_), channel_id=1, source_target_pairs={{0,16},{16,0},{1,17},{17,1},{2,18},{18,2},{3,19},{19,3},{4,20},{20... | collective-permute-start | bytes 786440 | tf_op jit(solution)/shard_map/ppermute | solution.py:307
  50.7 3.0 %copy-start.3 = (bf16[24,2,128,128]{3,2,1,0:T(8,128)(2,1)}, bf16[24,2,128,128]{3,2,1,0:T(8,128)(2,1)S(1)}, u32[]{:S(2)}) copy-start(bf16[24,2,128,128]{3,2,1,0:T(8,128)(2,1)S(1)} %collective-permute-done.11.refs_5_.refs_7_) | copy-start | bytes 4718596
  50.7 23.3 %collective-permute-start.8 = (bf16[12,2,128,128]{3,2,1,0:T(8,128)(2,1)S(1)}, bf16[12,2,128,128]{3,2,1,0:T(8,128)(2,1)}, u32[]{:S(2)}, u32[]{:S(2)}) collective-permute-start(bf16[12,2,128,128]{3,2,1,0:T(8,128)(2,1)S(1)} %slice.36), channel_id=1, source_target_pairs={{0,4},{4,8},{8,12},{12,0},{1,5},{5,9},{9,13},{13,1},{2,6},{6,10},{... | collective-permute-start | bytes 2359304 | tf_op jit(solution)/shard_map/ppermute | solution.py:283
  50.8 2.8 %copy-start.7 = (bf16[8,128,128]{2,1,0:T(8,128)(2,1)}, bf16[8,128,128]{2,1,0:T(8,128)(2,1)S(1)}, u32[]{:S(2)}) copy-start(bf16[8,128,128]{2,1,0:T(8,128)(2,1)S(1)} %collective-permute-done.14.refs_10_) | copy-start | bytes 786436
  50.8 23.1 %collective-permute-start.9 = (bf16[12,2,128,128]{3,2,1,0:T(8,128)(2,1)S(1)}, bf16[12,2,128,128]{3,2,1,0:T(8,128)(2,1)}, u32[]{:S(2)}, u32[]{:S(2)}) collective-permute-start(bf16[12,2,128,128]{3,2,1,0:T(8,128)(2,1)S(1)} %slice.37), channel_id=1, source_target_pairs={{0,12},{4,0},{8,4},{12,8},{1,13},{5,1},{9,5},{13,9},{2,14},{6,2},{... | collective-permute-start | bytes 2359304 | tf_op jit(solution)/shard_map/ppermute | solution.py:284
  53.6 0.7 copy-start.8
  53.6 20.4 %collective-permute-start.12 = (bf16[12,2,128,128]{3,2,1,0:T(8,128)(2,1)S(1)}, bf16[12,2,128,128]{3,2,1,0:T(8,128)(2,1)}, u32[]{:S(2)}, u32[]{:S(2)}) collective-permute-start(bf16[12,2,128,128]{3,2,1,0:T(8,128)(2,1)S(1)} %slice.48), channel_id=1, source_target_pairs={{0,1},{1,2},{2,3},{3,0},{4,5},{5,6},{6,7},{7,4},{8,9},{9,10},{10,1... | collective-permute-start | bytes 2359304 | tf_op jit(solution)/shard_map/ppermute | solution.py:283
  54.3 0.7 copy-start.9
  55.0 19.0 %collective-permute-start.13 = (bf16[12,2,128,128]{3,2,1,0:T(8,128)(2,1)S(1)}, bf16[12,2,128,128]{3,2,1,0:T(8,128)(2,1)}, u32[]{:S(2)}, u32[]{:S(2)}) collective-permute-start(bf16[12,2,128,128]{3,2,1,0:T(8,128)(2,1)S(1)} %slice.49), channel_id=1, source_target_pairs={{0,3},{1,0},{2,1},{3,2},{4,7},{5,4},{6,5},{7,6},{8,11},{9,8},{10,9... | collective-permute-start | bytes 2359304 | tf_op jit(solution)/shard_map/ppermute | solution.py:284
  74.0 16.3 %copy-start.10 = (s32[32]{0:T(128)S(1)}, s32[32]{0:T(128)}, u32[]{:S(2)}) copy-start(s32[32]{0:T(128)} %units.3) | copy-start | bytes 388
  89.0 3.8 %collective-permute-start.18 = (bf16[4,2,2,2,128,128]{5,4,3,2,1,0:T(8,128)(2,1)}, bf16[4,2,2,2,128,128]{5,4,3,2,1,0:T(8,128)(2,1)S(1)}, u32[]{:S(2)}, u32[]{:S(2)}) collective-permute-start(bf16[4,2,2,2,128,128]{5,4,3,2,1,0:T(8,128)(2,1)} %get-tuple-element.38), channel_id=1, source_target_pairs={{0,16},{16,0},{1,17},{17,1},{2,18},{18,2},{3,19},{19,3},{4,20},{20... | collective-permute-start | bytes 3145736 | tf_op jit(solution)/shard_map/ppermute | solution.py:311
  94.1 7.6 %collective-permute-start.19 = (bf16[2,2,2,128,128]{4,3,2,1,0:T(8,128)(2,1)S(1)}, bf16[2,2,2,128,128]{4,3,2,1,0:T(8,128)(2,1)S(1)}, u32[]{:S(2)}, u32[]{:S(2)}) collective-permute-start(bf16[2,2,2,128,128]{4,3,2,1,0:T(8,128)(2,1)S(1)} %get-tuple-element.39), channel_id=1, source_target_pairs={{0,32},{32,64},{64,96},{96,0},{1,33},{33,65},{65,97},{97,1},{2,34}... | collective-permute-start | bytes 786440 | tf_op jit(solution)/shard_map/ppermute | solution.py:317
  94.4 8.7 %collective-permute-start.20 = (bf16[2,2,2,128,128]{4,3,2,1,0:T(8,128)(2,1)S(1)}, bf16[2,2,2,128,128]{4,3,2,1,0:T(8,128)(2,1)S(1)}, u32[]{:S(2)}, u32[]{:S(2)}) collective-permute-start(bf16[2,2,2,128,128]{4,3,2,1,0:T(8,128)(2,1)S(1)} %get-tuple-element.41), channel_id=1, source_target_pairs={{0,64},{32,96},{64,0},{96,32},{1,65},{33,97},{65,1},{97,33},{2,66}... | collective-permute-start | bytes 786440 | tf_op jit(solution)/shard_map/ppermute | solution.py:317
  96.5 13.2 %collective-permute-start.21 = (bf16[2,2,2,128,128]{4,3,2,1,0:T(8,128)(2,1)S(1)}, bf16[2,2,2,128,128]{4,3,2,1,0:T(8,128)(2,1)S(1)}, u32[]{:S(2)}, u32[]{:S(2)}) collective-permute-start(bf16[2,2,2,128,128]{4,3,2,1,0:T(8,128)(2,1)S(1)} %get-tuple-element.40), channel_id=1, source_target_pairs={{0,96},{32,0},{64,32},{96,64},{1,97},{33,1},{65,33},{97,65},{2,98}... | collective-permute-start | bytes 786440 | tf_op jit(solution)/shard_map/ppermute | solution.py:317
  110.9 6.9 %collective-permute-start.22 = (bf16[2,2,128,128]{3,2,1,0:T(8,128)(2,1)S(1)}, bf16[2,2,128,128]{3,2,1,0:T(8,128)(2,1)S(1)}, u32[]{:S(2)}, u32[]{:S(2)}) collective-permute-start(bf16[2,2,128,128]{3,2,1,0:T(8,128)(2,1)S(1)} %get-tuple-element.48), channel_id=1, source_target_pairs={{0,1},{1,0},{2,17},{3,16},{16,3},{17,2},{18,19},{19,18},{4,5},{5,4... | collective-permute-start | bytes 393224 | tf_op jit(solution)/shard_map/ppermute | solution.py:352
  115.2 7.8 %collective-permute-start.23 = (bf16[2,2,128,128]{3,2,1,0:T(8,128)(2,1)S(1)}, bf16[2,2,128,128]{3,2,1,0:T(8,128)(2,1)S(1)}, u32[]{:S(2)}, u32[]{:S(2)}) collective-permute-start(bf16[2,2,128,128]{3,2,1,0:T(8,128)(2,1)S(1)} %get-tuple-element.49), channel_id=1, source_target_pairs={{0,0},{1,1},{2,16},{3,17},{16,2},{17,3},{18,18},{19,19},{4,4},{5,5... | collective-permute-start | bytes 393224 | tf_op jit(solution)/shard_map/ppermute | solution.py:352

commit v3 on v2

--- a/solution.py
+++ b/solution.py
@@ -54,17 +54,18 @@
             chip = lax.rem(x + 4 - at % 4, 4)
             whole.append(fetch(wave[at], w.at[2 * chip + (c ^ (at // 4))], sems.at[16 + at]))
     order = (6, 7, 0, 1, 2, 3, 4, 5) if late else range(6)
-    for slot in order:
-        for side, (store, parts) in enumerate(((ls, lefts), (rs, rights))):
-            sem = sems.at[8 * side + slot]
-            i = slot % 2
-            if slot < 6:
-                fetch(parts[slot // 2].at[:, i], store.at[slot], sem)
-            else:
-                for part in range(2):
-                    fetch(
-                        parts[3 + part].at[:, i], store.at[slot, pl.ds(half * part, half)], sem
-                    )
+    turns = [(side, slot) for slot in order for side in range(2)]
+    if late:
+        turns.sort(key=lambda turn: (turn[0] == 0 and turn[1] < 6))
+    for side, slot in turns:
+        store, parts = ((ls, lefts), (rs, rights))[side]
+        sem = sems.at[8 * side + slot]
+        i = slot % 2
+        if slot < 6:
+            fetch(parts[slot // 2].at[:, i], store.at[slot], sem)
+        else:
+            for part in range(2):
+                fetch(parts[3 + part].at[:, i], store.at[slot, pl.ds(half * part, half)], sem)
     for at in range(16):
         seen[at] = 0
 
@@ -123,8 +124,7 @@
                 w[q, l] = w[q, l] * (rows * columns).astype(jnp.bfloat16)
 
         passed = fetch(w, wave_out, sems.at[16])
-    else:
-        counts[8] = 0
+    counts[8] = 0
 
     def out_copy(other, to, e, i, j):
         return [
@@ -163,20 +163,19 @@
                 t[b, : nl * B], wide, (((1,), (1,)), ((), ())), preferred_element_type=jnp.float32
             ).astype(jnp.bfloat16)
             owner = locals_[b] // 2
-            e, j = lax.rem(owner, 2), lax.rem(locals_[b], 2)
+            e, j = lax.rem(owner, 2) ^ lax.rem(z, 2), lax.rem(locals_[b], 2)
             other = (owner // 2) ^ c
             for a, l in enumerate(left_slots):
                 to = lax.rem(y + shift_of(l) + 4 - x, 4)
                 sums[other, to, e, lax.rem(l, 2), j] = total[a * B : (a + 1) * B]
-            if late:
-                for l in left_slots:
-                    to = lax.rem(y + shift_of(l) + 4 - x, 4)
-                    kept, sent = out_copy(other, to, e, lax.rem(l, 2), j)
-                    pl.when(other == 0)(kept.start)
-                    pl.when(other == 1)(sent.start)
-                    n = counts[8]
-                    started[n] = (((other * 4 + to) * 2 + e) * 2 + lax.rem(l, 2)) * 2 + j
-                    counts[8] = n + 1
+            for l in left_slots:
+                to = lax.rem(y + shift_of(l) + 4 - x, 4)
+                kept, sent = out_copy(other, to, e, lax.rem(l, 2), j)
+                pl.when(other == 0)(kept.start)
+                pl.when(other == 1)(sent.start)
+                n = counts[8]
+                started[n] = (((other * 4 + to) * 2 + e) * 2 + lax.rem(l, 2)) * 2 + j
+                counts[8] = n + 1
 
     def rectangle(cls, l0, nl, m0, nm):
         lb, mb = 8 * cls + l0, 16 + 8 * cls + m0
@@ -222,17 +221,15 @@
     for slot in order:
         ready(0, ls, slot)
         ready(1, rs, slot)
-    if late:
-
-        @pl.loop(0, counts[8])
-        def _(n):
-            pltpu.make_async_copy(
-                sums.at[0, 0, 0, 0, 0], keep.at[0, 0, 0, 0], out_sems.at[started[n]]
-            ).wait()
-    else:
-        done = [fetch(sums.at[0], keep, sems.at[24]), fetch(sums.at[1], send, sems.at[25])]
-        for copy in (*done, passed):
-            copy.wait()
+
+    @pl.loop(0, counts[8])
+    def _(n):
+        pltpu.make_async_copy(
+            sums.at[0, 0, 0, 0, 0], keep.at[0, 0, 0, 0], out_sems.at[started[n]]
+        ).wait()
+
+    if not late:
+        passed.wait()
 
 
 def products(pos, allowed, units, lefts, rights, wave, before=()):
@@ -307,9 +304,8 @@
     return (*row, *(lax.ppermute(part, "core", swapped(2, 1)) for part in row))
 
 
-def add_cores(keep, send):
-    other = lax.ppermute(send, "core", shifted(2, 1))
-    both = [keep[d].astype(jnp.float32) + other[d].astype(jnp.float32) for d in range(4)]
+def add_cores(keep, other, s):
+    both = [keep[d, s].astype(jnp.float32) + other[d, s].astype(jnp.float32) for d in range(4)]
     return both[0], [part.astype(jnp.bfloat16) for part in both[1:]]
 
 
@@ -338,8 +334,9 @@
     lefts = (*lefts, *ring_far(far_l, "y"))
     rights = (*rights, *ring_far(far_r, "z"))
     keep, send = products(pos, allowed, block_units, lefts, rights, (masked,), sums)
-    own, chips = add_cores(keep, send)
-    final = add_chips(own, add_send(chips))
+    other = lax.ppermute(send, "core", shifted(2, 1))
+    halves = [add_cores(keep, other, s) for s in range(2)]
+    halves = [(own, add_send(chips)) for own, chips in halves]
 
     got = []
     for s in range(2):
@@ -348,8 +345,8 @@
             for cc in range(2)
             for zz in range(4)
         ]
-        piece = lax.dynamic_index_in_dim(final, s ^ (z & 1), 0, keepdims=False)
-        got.append(lax.ppermute(piece, ("core", "z"), perm))
+        half, got = lax.optimization_barrier((halves[s], got))
+        got.append(lax.ppermute(add_chips(*half), ("core", "z"), perm))
     odd = (z & 1) == 1
     first = jnp.where(odd, got[1], got[0])
     second = jnp.where(odd, got[0], got[1])

time: 124 us -> 120 us (0.968)
  starting transfers between devices: 34.7 us -> 43.7 us
  waiting for transfers between devices: 50 us -> 43.2 us
  Pallas kernels: 31.3 us -> 24.8 us
    ppermute x3 -> x6, waiting for transfers between devices: 12.4 us -> 3.32 us  [add_send(): lax.ppermute(part, 'x', shifted(4, d + 1))]
    pallas_call x2, Pallas kernels: 31.3 us -> 24.8 us  [products(): pl.pallas_call(functools.partial(products_kernel, late, terms), out_shape...]
    ppermute x3, starting transfers between devices: 7.48 us -> 12.8 us  [the longest x2 11.1 us: shards(): got.append(lax.ppermute(add_chips(*half), ('core', 'z'), perm))]
    ppermute x3 -> x6, starting transfers between devices: 2.4 us -> 5.98 us  [add_send(): lax.ppermute(part, 'x', shifted(4, d + 1))]
    ppermute x2, waiting for transfers between devices: 0.01 us -> 3.06 us  [ring_far(): lax.ppermute(halves[0], axis, shifted(4, 1))]
  transfers between devices with their start and end apart: 24 -> 27, of which waited for: 11 -> 12; matrix products, arithmetic and copies ran while one was open for 1% -> 2% of each run, Pallas kernels for 13% -> 11%
where the time goes in v3:
time: 120 us; the launch traced here: 119 us
  starting transfers between devices  43.7 us (36%)
  waiting for transfers between devices  43.2 us (36%)
  Pallas kernels  24.8 us (21%)
  other arithmetic  4.26 us (4%)
  local copies, waits for them, and re-layouts  2.57 us (2%)
    pallas_call x2, Pallas kernels, products(): pl.pallas_call(functools.partial(products_kernel, late, terms), out_shape...  24.8 us
    ppermute x3, waiting for transfers between devices, gather_wave(): row = [mine] + [lax.ppermute(mine, 'x', shifted(4, d)) for d in (1, 2, 3)]  17.8 us
    ppermute x2, starting transfers between devices, shards(): got.append(lax.ppermute(add_chips(*half), ('core', 'z'), perm))  11.1 us
    ppermute x2, waiting for transfers between devices, ring_near(): lax.ppermute(own, axis, shifted(4, 1))  8.51 us
    ppermute x4, starting transfers between devices, share_wave(): return (*row, *(lax.ppermute(part, 'core', swapped(2, 1)) for part in row))  6.92 us
    ppermute x6, starting transfers between devices, add_send(): lax.ppermute(part, 'x', shifted(4, d + 1))  5.98 us
    ppermute x2, waiting for transfers between devices, shards(): got.append(lax.ppermute(add_chips(*half), ('core', 'z'), perm))  4.91 us
    ppermute x2, starting transfers between devices, ring_far(): lax.ppermute(halves[1], axis, shifted(4, -1))  4.76 us
  transfers between devices with their start and end apart: 27, of which 12 were waited for; matrix products, arithmetic and copies ran while one was open for 2% of the time, Pallas kernels for 11%

profile of v3, /device:TPU:7, one launch (start us, length us, event | category | flops | bytes accessed | tf_op | source)
XLA Modules:
  0.0 118.7 jit_solution(3770441731088369911)
XLA Ops:
  0.0 1.0 dynamic-slice_bitcast_fusion
  1.0 1.4 %collective-permute-start = (bf16[2,128,128]{2,1,0:T(8,128)(2,1)S(1)}, bf16[2,128,128]{2,1,0:T(8,128)(2,1)S(1)}, u32[]{:S(2)}, u32[]{:S(2)}) collective-permute-start(bf16[2,128,128]{2,1,0:T(8,128)(2,1)S(1)} %get-tuple-element.67), channel_id=1, source_target_pairs={{0,4},{4,8},{8,12},{12,0},{1,5},{5,9},{9,13},{13,1},{2,6},{6,10},{... | collective-permute-start | bytes 196616 | tf_op jit(solution)/shard_map/ppermute | solution.py:293
  2.3 1.5 %collective-permute-start.1 = (bf16[2,128,128]{2,1,0:T(8,128)(2,1)S(1)}, bf16[2,128,128]{2,1,0:T(8,128)(2,1)S(1)}, u32[]{:S(2)}, u32[]{:S(2)}) collective-permute-start(bf16[2,128,128]{2,1,0:T(8,128)(2,1)S(1)} %get-tuple-element.66), channel_id=1, source_target_pairs={{0,12},{4,0},{8,4},{12,8},{1,13},{5,1},{9,5},{13,9},{2,14},{6,2},{... | collective-permute-start | bytes 196616 | tf_op jit(solution)/shard_map/ppermute | solution.py:293
  3.8 1.6 %collective-permute-start.2 = (bf16[2,128,128]{2,1,0:T(8,128)(2,1)S(1)}, bf16[2,128,128]{2,1,0:T(8,128)(2,1)S(1)}, u32[]{:S(2)}, u32[]{:S(2)}) collective-permute-start(bf16[2,128,128]{2,1,0:T(8,128)(2,1)S(1)} %get-tuple-element.68), channel_id=1, source_target_pairs={{0,8},{4,12},{8,0},{12,4},{1,9},{5,13},{9,1},{13,5},{2,10},{6,14},... | collective-permute-start | bytes 196616 | tf_op jit(solution)/shard_map/ppermute | solution.py:293
  5.4 3.0 %collective-permute-done.2 = bf16[2,128,128]{2,1,0:T(8,128)(2,1)S(1)} collective-permute-done((bf16[2,128,128]{2,1,0:T(8,128)(2,1)S(1)}, bf16[2,128,128]{2,1,0:T(8,128)(2,1)S(1)}, u32[]{:S(2)}, u32[]{:S(2)}) %collective-permute-start.2) | collective-permute-done | bytes 65568 | tf_op jit(solution)/shard_map/ppermute | solution.py:293
  8.5 0.3 collective-permute-start.6
  8.7 2.4 %collective-permute-start.7 = (bf16[24,2,128,128]{3,2,1,0:T(8,128)(2,1)}, bf16[24,2,128,128]{3,2,1,0:T(8,128)(2,1)S(1)}, u32[]{:S(2)}, u32[]{:S(2)}) collective-permute-start(bf16[24,2,128,128]{3,2,1,0:T(8,128)(2,1)} %refs_0_.1), channel_id=1, source_target_pairs={{0,12},{4,0},{8,4},{12,8},{1,13},{5,1},{9,5},{13,9},{2,14},{6,2},{... | collective-permute-start | bytes 4718600 | tf_op jit(solution)/shard_map/ppermute | solution.py:270
  11.1 1.6 %collective-permute-start.10 = (bf16[24,2,128,128]{3,2,1,0:T(8,128)(2,1)}, bf16[24,2,128,128]{3,2,1,0:T(8,128)(2,1)S(1)}, u32[]{:S(2)}, u32[]{:S(2)}) collective-permute-start(bf16[24,2,128,128]{3,2,1,0:T(8,128)(2,1)} %refs_5_), channel_id=1, source_target_pairs={{0,1},{1,2},{2,3},{3,0},{4,5},{5,6},{6,7},{7,4},{8,9},{9,10},{10,1... | collective-permute-start | bytes 4718600 | tf_op jit(solution)/shard_map/ppermute | solution.py:270
  12.8 2.1 %collective-permute-start.11 = (bf16[24,2,128,128]{3,2,1,0:T(8,128)(2,1)}, bf16[24,2,128,128]{3,2,1,0:T(8,128)(2,1)S(1)}, u32[]{:S(2)}, u32[]{:S(2)}) collective-permute-start(bf16[24,2,128,128]{3,2,1,0:T(8,128)(2,1)} %refs_5_), channel_id=1, source_target_pairs={{0,3},{1,0},{2,1},{3,2},{4,7},{5,4},{6,5},{7,6},{8,11},{9,8},{10,9... | collective-permute-start | bytes 4718600 | tf_op jit(solution)/shard_map/ppermute | solution.py:270
  15.0 0.3 collective-permute-start.3
  15.2 5.3 %collective-permute-done.3.refs_7_ = bf16[8,128,128]{2,1,0:T(8,128)(2,1)S(1)} collective-permute-done((bf16[8,128,128]{2,1,0:T(8,128)(2,1)S(1)}, bf16[8,128,128]{2,1,0:T(8,128)(2,1)S(1)}, u32[]{:S(2)}, u32[]{:S(2)}) %collective-permute-start.3) | collective-permute-done | bytes 262176 | tf_op jit(solution)/shard_map/ppermute | solution.py:299
  20.5 1.1 collective-permute-start.4
  21.7 5.6 %collective-permute-done.4.refs_8_ = bf16[8,128,128]{2,1,0:T(8,128)(2,1)S(1)} collective-permute-done((bf16[8,128,128]{2,1,0:T(8,128)(2,1)S(1)}, bf16[8,128,128]{2,1,0:T(8,128)(2,1)S(1)}, u32[]{:S(2)}, u32[]{:S(2)}) %collective-permute-start.4) | collective-permute-done | bytes 262176 | tf_op jit(solution)/shard_map/ppermute | solution.py:299
  27.3 0.8 collective-permute-start.5
  28.1 6.9 %collective-permute-done.5.refs_9_ = bf16[8,128,128]{2,1,0:T(8,128)(2,1)} collective-permute-done((bf16[8,128,128]{2,1,0:T(8,128)(2,1)S(1)}, bf16[8,128,128]{2,1,0:T(8,128)(2,1)}, u32[]{:S(2)}, u32[]{:S(2)}) %collective-permute-start.5) | collective-permute-done | bytes 262176 | tf_op jit(solution)/shard_map/ppermute | solution.py:299
  35.0 8.5 %collective-permute-done.6.refs_1_ = bf16[24,2,128,128]{3,2,1,0:T(8,128)(2,1)S(1)} collective-permute-done((bf16[24,2,128,128]{3,2,1,0:T(8,128)(2,1)}, bf16[24,2,128,128]{3,2,1,0:T(8,128)(2,1)S(1)}, u32[]{:S(2)}, u32[]{:S(2)}) %collective-permute-start.6) | collective-permute-done | bytes 1572896 | tf_op jit(solution)/shard_map/ppermute | solution.py:270
  43.5 3.2 %collective-permute-start.14 = (bf16[8,128,128]{2,1,0:T(8,128)(2,1)S(1)}, bf16[8,128,128]{2,1,0:T(8,128)(2,1)S(1)}, u32[]{:S(2)}, u32[]{:S(2)}) collective-permute-start(bf16[8,128,128]{2,1,0:T(8,128)(2,1)S(1)} %pad_maximum_fusion.refs_6_), channel_id=1, source_target_pairs={{0,16},{16,0},{1,17},{17,1},{2,18},{18,2},{3,19},{19,3},{4,20},{20... | collective-permute-start | bytes 786440 | tf_op jit(solution)/shard_map/ppermute | solution.py:304
  46.8 0.1 collective-permute-start.15
  46.9 0.4 collective-permute-start.16
  47.3 3.2 %collective-permute-start.17 = (bf16[8,128,128]{2,1,0:T(8,128)(2,1)}, bf16[8,128,128]{2,1,0:T(8,128)(2,1)}, u32[]{:S(2)}, u32[]{:S(2)}) collective-permute-start(bf16[8,128,128]{2,1,0:T(8,128)(2,1)} %collective-permute-done.5.refs_9_), channel_id=1, source_target_pairs={{0,16},{16,0},{1,17},{17,1},{2,18},{18,2},{3,19},{19,3},{4,20},{20... | collective-permute-start | bytes 786440 | tf_op jit(solution)/shard_map/ppermute | solution.py:304
  50.7 0.1 collective-permute-start.8
  50.8 2.7 %collective-permute-start.9 = (bf16[12,2,128,128]{3,2,1,0:T(8,128)(2,1)S(1)}, bf16[12,2,128,128]{3,2,1,0:T(8,128)(2,1)}, u32[]{:S(2)}, u32[]{:S(2)}) collective-permute-start(bf16[12,2,128,128]{3,2,1,0:T(8,128)(2,1)S(1)} %slice.61), channel_id=1, source_target_pairs={{0,12},{4,0},{8,4},{12,8},{1,13},{5,1},{9,5},{13,9},{2,14},{6,2},{... | collective-permute-start | bytes 2359304 | tf_op jit(solution)/shard_map/ppermute | solution.py:281
  53.6 0.6 copy-done.8
  54.3 0.7 copy-done.9
  55.0 2.0 %collective-permute-start.13 = (bf16[12,2,128,128]{3,2,1,0:T(8,128)(2,1)S(1)}, bf16[12,2,128,128]{3,2,1,0:T(8,128)(2,1)}, u32[]{:S(2)}, u32[]{:S(2)}) collective-permute-start(bf16[12,2,128,128]{3,2,1,0:T(8,128)(2,1)S(1)} %slice.81), channel_id=1, source_target_pairs={{0,3},{1,0},{2,1},{3,2},{4,7},{5,4},{6,5},{7,6},{8,11},{9,8},{10,9... | collective-permute-start | bytes 2359304 | tf_op jit(solution)/shard_map/ppermute | solution.py:281
  57.0 0.6 pad_add_fusion.pos
  57.6 12.7 %shard_map.55 = (bf16[4,2,2,2,128,128]{5,4,3,2,1,0:T(8,128)(2,1)}, bf16[4,2,2,2,128,128]{5,4,3,2,1,0:T(8,128)(2,1)}, bf16[8,8,128,128]{3,2,1,0:T(8,128)(2,1)}) custom-call(s32[4]{0:T(128)} %pad_add_fusion.pos, s32[32,32]{1,0:T(8,128)} %allowed.3, s32[32]{0:T(128)} %units.3, bf16[24,2,128,128]{3,2,1,0:T(8,128)(2,1)} %refs_0_.1, ...), custom_call_target="tpu_custom_call" | custom-call | flops 6442450944 | bytes 14680064 | tf_op jit(solution)/shard_map/pallas_call | solution.py:243
  70.4 0.9 collective-permute-done.8.refs_3_
  71.2 2.2 %collective-permute-done.12.refs_8_ = bf16[12,2,128,128]{3,2,1,0:T(8,128)(2,1)} collective-permute-done((bf16[12,2,128,128]{3,2,1,0:T(8,128)(2,1)S(1)}, bf16[12,2,128,128]{3,2,1,0:T(8,128)(2,1)}, u32[]{:S(2)}, u32[]{:S(2)}) %collective-permute-start.12) | collective-permute-done | bytes 786464 | tf_op jit(solution)/shard_map/ppermute | solution.py:280
  73.4 12.1 %shard_map.56 = (bf16[4,2,2,2,128,128]{5,4,3,2,1,0:T(8,128)(2,1)}, bf16[4,2,2,2,128,128]{5,4,3,2,1,0:T(8,128)(2,1)}) custom-call(s32[4]{0:T(128)} %pad_add_fusion.pos, s32[32,32]{1,0:T(8,128)} %allowed.3, s32[32]{0:T(128)} %units.3, bf16[24,2,128,128]{3,2,1,0:T(8,128)(2,1)} %refs_0_.1, ...), custom_call_target="tpu_custom_call", output_to_operand_aliasing={{0}: (14, {}), {1}: (15, {})} | custom-call | flops 6442450944 | bytes 14680064 | tf_op jit(solution)/shard_map/pallas_call | solution.py:243
  85.5 1.7 %collective-permute-start.18 = (bf16[4,2,2,2,128,128]{5,4,3,2,1,0:T(8,128)(2,1)}, bf16[4,2,2,2,128,128]{5,4,3,2,1,0:T(8,128)(2,1)S(1)}, u32[]{:S(2)}, u32[]{:S(2)}) collective-permute-start(bf16[4,2,2,2,128,128]{5,4,3,2,1,0:T(8,128)(2,1)} %get-tuple-element.47), channel_id=1, source_target_pairs={{0,16},{16,0},{1,17},{17,1},{2,18},{18,2},{3,19},{19,3},{4,20},{20... | collective-permute-start | bytes 3145736 | tf_op jit(solution)/shard_map/ppermute | solution.py:337
  87.2 2.5 %collective-permute-done.18 = bf16[4,2,2,2,128,128]{5,4,3,2,1,0:T(8,128)(2,1)S(1)} collective-permute-done((bf16[4,2,2,2,128,128]{5,4,3,2,1,0:T(8,128)(2,1)}, bf16[4,2,2,2,128,128]{5,4,3,2,1,0:T(8,128)(2,1)S(1)}, u32[]{:S(2)}, u32[]{:S(2)}) %collective-permute-start.18) | collective-permute-done | bytes 1048608 | tf_op jit(solution)/shard_map/ppermute | solution.py:337
  89.7 1.6 %fusion.5 = (bf16[2,2,128,128]{3,2,1,0:T(8,128)(2,1)S(1)}, bf16[2,2,128,128]{3,2,1,0:T(8,128)(2,1)S(1)}, bf16[2,2,128,128]{3,2,1,0:T(8,128)(2,1)S(1)}, f32[2,2,1...) fusion(bf16[4,2,2,2,128,128]{5,4,3,2,1,0:T(8,128)(2,1)S(1)} %co, ...), kind=kLoop, calls=%fused_computation.17 | loop fusion | flops 1966080 | bytes 3407872 | tf_op jit(solution)/shard_map/convert_element_type | solution.py:309
  91.3 0.3 collective-permute-start.22
  91.6 2.1 %collective-permute-start.23 = (bf16[2,2,128,128]{3,2,1,0:T(8,128)(2,1)S(1)}, bf16[2,2,128,128]{3,2,1,0:T(8,128)(2,1)S(1)}, u32[]{:S(2)}, u32[]{:S(2)}) collective-permute-start(bf16[2,2,128,128]{3,2,1,0:T(8,128)(2,1)S(1)} %get-tuple-element.58), channel_id=1, source_target_pairs={{0,64},{32,96},{64,0},{96,32},{1,65},{33,97},{65,1},{97,33},{2,66}... | collective-permute-start | bytes 393224 | tf_op jit(solution)/shard_map/ppermute | solution.py:313
  93.8 2.7 %collective-permute-start.19 = (bf16[2,2,128,128]{3,2,1,0:T(8,128)(2,1)S(1)}, bf16[2,2,128,128]{3,2,1,0:T(8,128)(2,1)S(1)}, u32[]{:S(2)}, u32[]{:S(2)}) collective-permute-start(bf16[2,2,128,128]{3,2,1,0:T(8,128)(2,1)S(1)} %get-tuple-element.63), channel_id=1, source_target_pairs={{0,32},{32,64},{64,96},{96,0},{1,33},{33,65},{65,97},{97,1},{2,34}... | collective-permute-start | bytes 393224 | tf_op jit(solution)/shard_map/ppermute | solution.py:313
  96.5 0.1 collective-permute-start.20
  96.6 0.8 collective-permute-start.21
  97.4 0.1 collective-permute-done.23
  97.5 3.2 %collective-permute-done.24 = bf16[2,2,128,128]{3,2,1,0:T(8,128)(2,1)S(1)} collective-permute-done((bf16[2,2,128,128]{3,2,1,0:T(8,128)(2,1)S(1)}, bf16[2,2,128,128]{3,2,1,0:T(8,128)(2,1)S(1)}, u32[]{:S(2)}, u32[]{:S(2)}) %collective-permute-start.24) | collective-permute-done | bytes 131104 | tf_op jit(solution)/shard_map/ppermute | solution.py:313
  100.7 0.1 add_convert_fusion.1
  100.8 8.1 %collective-permute-start.25 = (bf16[2,2,128,128]{3,2,1,0:T(8,128)(2,1)S(1)}, bf16[2,2,128,128]{3,2,1,0:T(8,128)(2,1)S(1)}, u32[]{:S(2)}, u32[]{:S(2)}) collective-permute-start(bf16[2,2,128,128]{3,2,1,0:T(8,128)(2,1)S(1)} %add_convert_fusion.1), channel_id=1, source_target_pairs={{0,0},{1,1},{2,16},{3,17},{16,2},{17,3},{18,18},{19,19},{4,4},{5,5... | collective-permute-start | bytes 393224 | tf_op jit(solution)/shard_map/ppermute | solution.py:349
  108.9 0.8 dynamic-slice_compare_fusion
  109.7 2.3 %collective-permute-done.25 = bf16[2,2,128,128]{3,2,1,0:T(8,128)(2,1)S(1)} collective-permute-done((bf16[2,2,128,128]{3,2,1,0:T(8,128)(2,1)S(1)}, bf16[2,2,128,128]{3,2,1,0:T(8,128)(2,1)S(1)}, u32[]{:S(2)}, u32[]{:S(2)}) %collective-permute-start.25) | collective-permute-done | bytes 131104 | tf_op jit(solution)/shard_map/ppermute | solution.py:349
  112.1 3.0 %collective-permute-start.26 = (bf16[2,2,128,128]{3,2,1,0:T(8,128)(2,1)S(1)}, bf16[2,2,128,128]{3,2,1,0:T(8,128)(2,1)S(1)}, u32[]{:S(2)}, u32[]{:S(2)}) collective-permute-start(bf16[2,2,128,128]{3,2,1,0:T(8,128)(2,1)S(1)} %add_convert_fusion), channel_id=1, source_target_pairs={{0,1},{1,0},{2,17},{3,16},{16,3},{17,2},{18,19},{19,18},{4,5},{5,4... | collective-permute-start | bytes 393224 | tf_op jit(solution)/shard_map/ppermute | solution.py:349
  115.1 0.1 broadcast_and_fusion
  115.2 2.6 %collective-permute-done.26 = bf16[2,2,128,128]{3,2,1,0:T(8,128)(2,1)S(1)} collective-permute-done((bf16[2,2,128,128]{3,2,1,0:T(8,128)(2,1)S(1)}, bf16[2,2,128,128]{3,2,1,0:T(8,128)(2,1)S(1)}, u32[]{:S(2)}, u32[]{:S(2)}) %collective-permute-start.26) | collective-permute-done | bytes 131104 | tf_op jit(solution)/shard_map/ppermute | solution.py:349
  117.8 0.9 and_select_fusion
  (48 shorter events, 0.5 us)
Async XLA Ops:
  1.0 4.5 %collective-permute-start = (bf16[2,128,128]{2,1,0:T(8,128)(2,1)S(1)}, bf16[2,128,128]{2,1,0:T(8,128)(2,1)S(1)}, u32[]{:S(2)}, u32[]{:S(2)}) collective-permute-start(bf16[2,128,128]{2,1,0:T(8,128)(2,1)S(1)} %get-tuple-element.67), channel_id=1, source_target_pairs={{0,4},{4,8},{8,12},{12,0},{1,5},{5,9},{9,13},{13,1},{2,6},{6,10},{... | collective-permute-start | bytes 196616 | tf_op jit(solution)/shard_map/ppermute | solution.py:293
  2.3 3.1 %collective-permute-start.1 = (bf16[2,128,128]{2,1,0:T(8,128)(2,1)S(1)}, bf16[2,128,128]{2,1,0:T(8,128)(2,1)S(1)}, u32[]{:S(2)}, u32[]{:S(2)}) collective-permute-start(bf16[2,128,128]{2,1,0:T(8,128)(2,1)S(1)} %get-tuple-element.66), channel_id=1, source_target_pairs={{0,12},{4,0},{8,4},{12,8},{1,13},{5,1},{9,5},{13,9},{2,14},{6,2},{... | collective-permute-start | bytes 196616 | tf_op jit(solution)/shard_map/ppermute | solution.py:293
  3.8 4.6 %collective-permute-start.2 = (bf16[2,128,128]{2,1,0:T(8,128)(2,1)S(1)}, bf16[2,128,128]{2,1,0:T(8,128)(2,1)S(1)}, u32[]{:S(2)}, u32[]{:S(2)}) collective-permute-start(bf16[2,128,128]{2,1,0:T(8,128)(2,1)S(1)} %get-tuple-element.68), channel_id=1, source_target_pairs={{0,8},{4,12},{8,0},{12,4},{1,9},{5,13},{9,1},{13,5},{2,10},{6,14},... | collective-permute-start | bytes 196616 | tf_op jit(solution)/shard_map/ppermute | solution.py:293
  8.5 35.1 %collective-permute-start.6 = (bf16[24,2,128,128]{3,2,1,0:T(8,128)(2,1)}, bf16[24,2,128,128]{3,2,1,0:T(8,128)(2,1)S(1)}, u32[]{:S(2)}, u32[]{:S(2)}) collective-permute-start(bf16[24,2,128,128]{3,2,1,0:T(8,128)(2,1)} %refs_0_.1), channel_id=1, source_target_pairs={{0,4},{4,8},{8,12},{12,0},{1,5},{5,9},{9,13},{13,1},{2,6},{6,10},{... | collective-permute-start | bytes 4718600 | tf_op jit(solution)/shard_map/ppermute | solution.py:270
  8.7 34.8 %collective-permute-start.7 = (bf16[24,2,128,128]{3,2,1,0:T(8,128)(2,1)}, bf16[24,2,128,128]{3,2,1,0:T(8,128)(2,1)S(1)}, u32[]{:S(2)}, u32[]{:S(2)}) collective-permute-start(bf16[24,2,128,128]{3,2,1,0:T(8,128)(2,1)} %refs_0_.1), channel_id=1, source_target_pairs={{0,12},{4,0},{8,4},{12,8},{1,13},{5,1},{9,5},{13,9},{2,14},{6,2},{... | collective-permute-start | bytes 4718600 | tf_op jit(solution)/shard_map/ppermute | solution.py:270
  11.1 36.1 %collective-permute-start.10 = (bf16[24,2,128,128]{3,2,1,0:T(8,128)(2,1)}, bf16[24,2,128,128]{3,2,1,0:T(8,128)(2,1)S(1)}, u32[]{:S(2)}, u32[]{:S(2)}) collective-permute-start(bf16[24,2,128,128]{3,2,1,0:T(8,128)(2,1)} %refs_5_), channel_id=1, source_target_pairs={{0,1},{1,2},{2,3},{3,0},{4,5},{5,6},{6,7},{7,4},{8,9},{9,10},{10,1... | collective-permute-start | bytes 4718600 | tf_op jit(solution)/shard_map/ppermute | solution.py:270
  12.8 37.9 %collective-permute-start.11 = (bf16[24,2,128,128]{3,2,1,0:T(8,128)(2,1)}, bf16[24,2,128,128]{3,2,1,0:T(8,128)(2,1)S(1)}, u32[]{:S(2)}, u32[]{:S(2)}) collective-permute-start(bf16[24,2,128,128]{3,2,1,0:T(8,128)(2,1)} %refs_5_), channel_id=1, source_target_pairs={{0,3},{1,0},{2,1},{3,2},{4,7},{5,4},{6,5},{7,6},{8,11},{9,8},{10,9... | collective-permute-start | bytes 4718600 | tf_op jit(solution)/shard_map/ppermute | solution.py:270
  14.9 42.7 %copy-start.4 = (bf16[8,128,128]{2,1,0:T(8,128)(2,1)}, bf16[8,128,128]{2,1,0:T(8,128)(2,1)S(1)}, u32[]{:S(2)}) copy-start(bf16[8,128,128]{2,1,0:T(8,128)(2,1)S(1)} %pad_maximum_fusion.refs_6_) | copy-start | bytes 786436
  15.0 5.6 %collective-permute-start.3 = (bf16[8,128,128]{2,1,0:T(8,128)(2,1)S(1)}, bf16[8,128,128]{2,1,0:T(8,128)(2,1)S(1)}, u32[]{:S(2)}, u32[]{:S(2)}) collective-permute-start(bf16[8,128,128]{2,1,0:T(8,128)(2,1)S(1)} %pad_maximum_fusion.refs_6_), channel_id=1, source_target_pairs={{0,32},{32,64},{64,96},{96,0},{1,33},{33,65},{65,97},{97,1},{2,34}... | collective-permute-start | bytes 786440 | tf_op jit(solution)/shard_map/ppermute | solution.py:299
  20.5 33.1 %copy-start.5 = (bf16[8,128,128]{2,1,0:T(8,128)(2,1)}, bf16[8,128,128]{2,1,0:T(8,128)(2,1)S(1)}, u32[]{:S(2)}) copy-start(bf16[8,128,128]{2,1,0:T(8,128)(2,1)S(1)} %collective-permute-done.3.refs_7_) | copy-start | bytes 786436
  20.5 6.7 %collective-permute-start.4 = (bf16[8,128,128]{2,1,0:T(8,128)(2,1)S(1)}, bf16[8,128,128]{2,1,0:T(8,128)(2,1)S(1)}, u32[]{:S(2)}, u32[]{:S(2)}) collective-permute-start(bf16[8,128,128]{2,1,0:T(8,128)(2,1)S(1)} %pad_maximum_fusion.refs_6_), channel_id=1, source_target_pairs={{0,64},{32,96},{64,0},{96,32},{1,65},{33,97},{65,1},{97,33},{2,66}... | collective-permute-start | bytes 786440 | tf_op jit(solution)/shard_map/ppermute | solution.py:299
  27.3 26.3 %copy-start.6 = (bf16[8,128,128]{2,1,0:T(8,128)(2,1)}, bf16[8,128,128]{2,1,0:T(8,128)(2,1)S(1)}, u32[]{:S(2)}) copy-start(bf16[8,128,128]{2,1,0:T(8,128)(2,1)S(1)} %collective-permute-done.4.refs_8_) | copy-start | bytes 786436
  27.3 7.7 %collective-permute-start.5 = (bf16[8,128,128]{2,1,0:T(8,128)(2,1)S(1)}, bf16[8,128,128]{2,1,0:T(8,128)(2,1)}, u32[]{:S(2)}, u32[]{:S(2)}) collective-permute-start(bf16[8,128,128]{2,1,0:T(8,128)(2,1)S(1)} %pad_maximum_fusion.refs_6_), channel_id=1, source_target_pairs={{0,96},{32,0},{64,32},{96,64},{1,97},{33,1},{65,33},{97,65},{2,98}... | collective-permute-start | bytes 786440 | tf_op jit(solution)/shard_map/ppermute | solution.py:299
  43.5 7.1 %copy-start = (bf16[24,2,128,128]{3,2,1,0:T(8,128)(2,1)}, bf16[24,2,128,128]{3,2,1,0:T(8,128)(2,1)S(1)}, u32[]{:S(2)}) copy-start(bf16[24,2,128,128]{3,2,1,0:T(8,128)(2,1)S(1)} %collective-permute-done.6.refs_1_) | copy-start | bytes 4718596
  43.5 7.1 %copy-start.1 = (bf16[24,2,128,128]{3,2,1,0:T(8,128)(2,1)}, bf16[24,2,128,128]{3,2,1,0:T(8,128)(2,1)S(1)}, u32[]{:S(2)}) copy-start(bf16[24,2,128,128]{3,2,1,0:T(8,128)(2,1)S(1)} %collective-permute-done.7.refs_2_) | copy-start | bytes 4718596
  43.5 7.3 %collective-permute-start.14 = (bf16[8,128,128]{2,1,0:T(8,128)(2,1)S(1)}, bf16[8,128,128]{2,1,0:T(8,128)(2,1)S(1)}, u32[]{:S(2)}, u32[]{:S(2)}) collective-permute-start(bf16[8,128,128]{2,1,0:T(8,128)(2,1)S(1)} %pad_maximum_fusion.refs_6_), channel_id=1, source_target_pairs={{0,16},{16,0},{1,17},{17,1},{2,18},{18,2},{3,19},{19,3},{4,20},{20... | collective-permute-start | bytes 786440 | tf_op jit(solution)/shard_map/ppermute | solution.py:304
  46.8 6.8 %collective-permute-start.15 = (bf16[8,128,128]{2,1,0:T(8,128)(2,1)S(1)}, bf16[8,128,128]{2,1,0:T(8,128)(2,1)S(1)}, u32[]{:S(2)}, u32[]{:S(2)}) collective-permute-start(bf16[8,128,128]{2,1,0:T(8,128)(2,1)S(1)} %collective-permute-done.3.refs_7_), channel_id=1, source_target_pairs={{0,16},{16,0},{1,17},{17,1},{2,18},{18,2},{3,19},{19,3},{4,20},{20... | collective-permute-start | bytes 786440 | tf_op jit(solution)/shard_map/ppermute | solution.py:304
  46.9 6.7 %collective-permute-start.16 = (bf16[8,128,128]{2,1,0:T(8,128)(2,1)S(1)}, bf16[8,128,128]{2,1,0:T(8,128)(2,1)S(1)}, u32[]{:S(2)}, u32[]{:S(2)}) collective-permute-start(bf16[8,128,128]{2,1,0:T(8,128)(2,1)S(1)} %collective-permute-done.4.refs_8_), channel_id=1, source_target_pairs={{0,16},{16,0},{1,17},{17,1},{2,18},{18,2},{3,19},{19,3},{4,20},{20... | collective-permute-start | bytes 786440 | tf_op jit(solution)/shard_map/ppermute | solution.py:304
  47.3 6.3 %copy-start.2 = (bf16[24,2,128,128]{3,2,1,0:T(8,128)(2,1)}, bf16[24,2,128,128]{3,2,1,0:T(8,128)(2,1)S(1)}, u32[]{:S(2)}) copy-start(bf16[24,2,128,128]{3,2,1,0:T(8,128)(2,1)S(1)} %collective-permute-done.10.refs_4_.refs_6_) | copy-start | bytes 4718596
  47.3 10.3 %collective-permute-start.17 = (bf16[8,128,128]{2,1,0:T(8,128)(2,1)}, bf16[8,128,128]{2,1,0:T(8,128)(2,1)}, u32[]{:S(2)}, u32[]{:S(2)}) collective-permute-start(bf16[8,128,128]{2,1,0:T(8,128)(2,1)} %collective-permute-done.5.refs_9_), channel_id=1, source_target_pairs={{0,16},{16,0},{1,17},{17,1},{2,18},{18,2},{3,19},{19,3},{4,20},{20... | collective-permute-start | bytes 786440 | tf_op jit(solution)/shard_map/ppermute | solution.py:304
  50.7 3.0 %copy-start.3 = (bf16[24,2,128,128]{3,2,1,0:T(8,128)(2,1)}, bf16[24,2,128,128]{3,2,1,0:T(8,128)(2,1)S(1)}, u32[]{:S(2)}) copy-start(bf16[24,2,128,128]{3,2,1,0:T(8,128)(2,1)S(1)} %collective-permute-done.11.refs_5_.refs_7_) | copy-start | bytes 4718596
  50.7 20.6 %collective-permute-start.8 = (bf16[12,2,128,128]{3,2,1,0:T(8,128)(2,1)S(1)}, bf16[12,2,128,128]{3,2,1,0:T(8,128)(2,1)}, u32[]{:S(2)}, u32[]{:S(2)}) collective-permute-start(bf16[12,2,128,128]{3,2,1,0:T(8,128)(2,1)S(1)} %slice.60), channel_id=1, source_target_pairs={{0,4},{4,8},{8,12},{12,0},{1,5},{5,9},{9,13},{13,1},{2,6},{6,10},{... | collective-permute-start | bytes 2359304 | tf_op jit(solution)/shard_map/ppermute | solution.py:280
  50.8 2.8 %copy-start.7 = (bf16[8,128,128]{2,1,0:T(8,128)(2,1)}, bf16[8,128,128]{2,1,0:T(8,128)(2,1)S(1)}, u32[]{:S(2)}) copy-start(bf16[8,128,128]{2,1,0:T(8,128)(2,1)S(1)} %collective-permute-done.14.refs_10_) | copy-start | bytes 786436
  50.8 20.4 %collective-permute-start.9 = (bf16[12,2,128,128]{3,2,1,0:T(8,128)(2,1)S(1)}, bf16[12,2,128,128]{3,2,1,0:T(8,128)(2,1)}, u32[]{:S(2)}, u32[]{:S(2)}) collective-permute-start(bf16[12,2,128,128]{3,2,1,0:T(8,128)(2,1)S(1)} %slice.61), channel_id=1, source_target_pairs={{0,12},{4,0},{8,4},{12,8},{1,13},{5,1},{9,5},{13,9},{2,14},{6,2},{... | collective-permute-start | bytes 2359304 | tf_op jit(solution)/shard_map/ppermute | solution.py:281
  53.6 0.7 copy-start.8
  53.6 19.9 %collective-permute-start.12 = (bf16[12,2,128,128]{3,2,1,0:T(8,128)(2,1)S(1)}, bf16[12,2,128,128]{3,2,1,0:T(8,128)(2,1)}, u32[]{:S(2)}, u32[]{:S(2)}) collective-permute-start(bf16[12,2,128,128]{3,2,1,0:T(8,128)(2,1)S(1)} %slice.80), channel_id=1, source_target_pairs={{0,1},{1,2},{2,3},{3,0},{4,5},{5,6},{6,7},{7,4},{8,9},{9,10},{10,1... | collective-permute-start | bytes 2359304 | tf_op jit(solution)/shard_map/ppermute | solution.py:280
  54.3 0.7 copy-start.9
  55.0 18.4 %collective-permute-start.13 = (bf16[12,2,128,128]{3,2,1,0:T(8,128)(2,1)S(1)}, bf16[12,2,128,128]{3,2,1,0:T(8,128)(2,1)}, u32[]{:S(2)}, u32[]{:S(2)}) collective-permute-start(bf16[12,2,128,128]{3,2,1,0:T(8,128)(2,1)S(1)} %slice.81), channel_id=1, source_target_pairs={{0,3},{1,0},{2,1},{3,2},{4,7},{5,4},{6,5},{7,6},{8,11},{9,8},{10,9... | collective-permute-start | bytes 2359304 | tf_op jit(solution)/shard_map/ppermute | solution.py:281
  73.4 13.8 %copy-start.10 = (s32[32]{0:T(128)S(1)}, s32[32]{0:T(128)}, u32[]{:S(2)}) copy-start(s32[32]{0:T(128)} %units.3) | copy-start | bytes 388
  85.5 4.2 %collective-permute-start.18 = (bf16[4,2,2,2,128,128]{5,4,3,2,1,0:T(8,128)(2,1)}, bf16[4,2,2,2,128,128]{5,4,3,2,1,0:T(8,128)(2,1)S(1)}, u32[]{:S(2)}, u32[]{:S(2)}) collective-permute-start(bf16[4,2,2,2,128,128]{5,4,3,2,1,0:T(8,128)(2,1)} %get-tuple-element.47), channel_id=1, source_target_pairs={{0,16},{16,0},{1,17},{17,1},{2,18},{18,2},{3,19},{19,3},{4,20},{20... | collective-permute-start | bytes 3145736 | tf_op jit(solution)/shard_map/ppermute | solution.py:337
  91.3 5.3 %collective-permute-start.22 = (bf16[2,2,128,128]{3,2,1,0:T(8,128)(2,1)S(1)}, bf16[2,2,128,128]{3,2,1,0:T(8,128)(2,1)S(1)}, u32[]{:S(2)}, u32[]{:S(2)}) collective-permute-start(bf16[2,2,128,128]{3,2,1,0:T(8,128)(2,1)S(1)} %get-tuple-element.59), channel_id=1, source_target_pairs={{0,32},{32,64},{64,96},{96,0},{1,33},{33,65},{65,97},{97,1},{2,34}... | collective-permute-start | bytes 393224 | tf_op jit(solution)/shard_map/ppermute | solution.py:313
  91.6 5.9 %collective-permute-start.23 = (bf16[2,2,128,128]{3,2,1,0:T(8,128)(2,1)S(1)}, bf16[2,2,128,128]{3,2,1,0:T(8,128)(2,1)S(1)}, u32[]{:S(2)}, u32[]{:S(2)}) collective-permute-start(bf16[2,2,128,128]{3,2,1,0:T(8,128)(2,1)S(1)} %get-tuple-element.58), channel_id=1, source_target_pairs={{0,64},{32,96},{64,0},{96,32},{1,65},{33,97},{65,1},{97,33},{2,66}... | collective-permute-start | bytes 393224 | tf_op jit(solution)/shard_map/ppermute | solution.py:313
  93.7 7.0 %collective-permute-start.24 = (bf16[2,2,128,128]{3,2,1,0:T(8,128)(2,1)S(1)}, bf16[2,2,128,128]{3,2,1,0:T(8,128)(2,1)S(1)}, u32[]{:S(2)}, u32[]{:S(2)}) collective-permute-start(bf16[2,2,128,128]{3,2,1,0:T(8,128)(2,1)S(1)} %get-tuple-element.57), channel_id=1, source_target_pairs={{0,96},{32,0},{64,32},{96,64},{1,97},{33,1},{65,33},{97,65},{2,98}... | collective-permute-start | bytes 393224 | tf_op jit(solution)/shard_map/ppermute | solution.py:313
  93.8 15.8 %collective-permute-start.19 = (bf16[2,2,128,128]{3,2,1,0:T(8,128)(2,1)S(1)}, bf16[2,2,128,128]{3,2,1,0:T(8,128)(2,1)S(1)}, u32[]{:S(2)}, u32[]{:S(2)}) collective-permute-start(bf16[2,2,128,128]{3,2,1,0:T(8,128)(2,1)S(1)} %get-tuple-element.63), channel_id=1, source_target_pairs={{0,32},{32,64},{64,96},{96,0},{1,33},{33,65},{65,97},{97,1},{2,34}... | collective-permute-start | bytes 393224 | tf_op jit(solution)/shard_map/ppermute | solution.py:313
  96.5 13.2 %collective-permute-start.20 = (bf16[2,2,128,128]{3,2,1,0:T(8,128)(2,1)S(1)}, bf16[2,2,128,128]{3,2,1,0:T(8,128)(2,1)S(1)}, u32[]{:S(2)}, u32[]{:S(2)}) collective-permute-start(bf16[2,2,128,128]{3,2,1,0:T(8,128)(2,1)S(1)} %get-tuple-element.62), channel_id=1, source_target_pairs={{0,64},{32,96},{64,0},{96,32},{1,65},{33,97},{65,1},{97,33},{2,66}... | collective-permute-start | bytes 393224 | tf_op jit(solution)/shard_map/ppermute | solution.py:313
  96.6 13.1 %collective-permute-start.21 = (bf16[2,2,128,128]{3,2,1,0:T(8,128)(2,1)S(1)}, bf16[2,2,128,128]{3,2,1,0:T(8,128)(2,1)S(1)}, u32[]{:S(2)}, u32[]{:S(2)}) collective-permute-start(bf16[2,2,128,128]{3,2,1,0:T(8,128)(2,1)S(1)} %get-tuple-element.61), channel_id=1, source_target_pairs={{0,96},{32,0},{64,32},{96,64},{1,97},{33,1},{65,33},{97,65},{2,98}... | collective-permute-start | bytes 393224 | tf_op jit(solution)/shard_map/ppermute | solution.py:313
  100.8 11.3 %collective-permute-start.25 = (bf16[2,2,128,128]{3,2,1,0:T(8,128)(2,1)S(1)}, bf16[2,2,128,128]{3,2,1,0:T(8,128)(2,1)S(1)}, u32[]{:S(2)}, u32[]{:S(2)}) collective-permute-start(bf16[2,2,128,128]{3,2,1,0:T(8,128)(2,1)S(1)} %add_convert_fusion.1), channel_id=1, source_target_pairs={{0,0},{1,1},{2,16},{3,17},{16,2},{17,3},{18,18},{19,19},{4,4},{5,5... | collective-permute-start | bytes 393224 | tf_op jit(solution)/shard_map/ppermute | solution.py:349
  112.1 5.7 %collective-permute-start.26 = (bf16[2,2,128,128]{3,2,1,0:T(8,128)(2,1)S(1)}, bf16[2,2,128,128]{3,2,1,0:T(8,128)(2,1)S(1)}, u32[]{:S(2)}, u32[]{:S(2)}) collective-permute-start(bf16[2,2,128,128]{3,2,1,0:T(8,128)(2,1)S(1)} %add_convert_fusion), channel_id=1, source_target_pairs={{0,1},{1,0},{2,17},{3,16},{16,3},{17,2},{18,19},{19,18},{4,5},{5,4... | collective-permute-start | bytes 393224 | tf_op jit(solution)/shard_map/ppermute | solution.py:349

commit v4 on v3

--- a/solution.py
+++ b/solution.py
@@ -24,8 +24,8 @@
     rights, refs = refs[:pieces], refs[pieces:]
     wave, refs = (refs[:1], refs[1:]) if late else (refs[:8], refs[8:])
     if late:
-        refs = refs[2:]
-    keep, send, *refs = refs
+        refs = refs[4:]
+    outs, refs = refs[:4], refs[4:]
     if not late:
         wave_out, *refs = refs
     ls, rs, w, t, sums, lists, counts, seen, started, sems, out_sems = refs
@@ -130,10 +130,10 @@
         return [
             pltpu.make_async_copy(
                 sums.at[other, to, e, i, j],
-                out.at[to, e, i, j],
+                out.at[to, i, j],
                 out_sems.at[(((other * 4 + to) * 2 + e) * 2 + i) * 2 + j],
             )
-            for out in (keep, send)
+            for out in outs
         ]
 
     def item(left_slots, right_slots):
@@ -170,9 +170,8 @@
                 sums[other, to, e, lax.rem(l, 2), j] = total[a * B : (a + 1) * B]
             for l in left_slots:
                 to = lax.rem(y + shift_of(l) + 4 - x, 4)
-                kept, sent = out_copy(other, to, e, lax.rem(l, 2), j)
-                pl.when(other == 0)(kept.start)
-                pl.when(other == 1)(sent.start)
+                for at, copy in enumerate(out_copy(other, to, e, lax.rem(l, 2), j)):
+                    pl.when(2 * other + e == at)(copy.start)
                 n = counts[8]
                 started[n] = (((other * 4 + to) * 2 + e) * 2 + lax.rem(l, 2)) * 2 + j
                 counts[8] = n + 1
@@ -225,7 +224,7 @@
     @pl.loop(0, counts[8])
     def _(n):
         pltpu.make_async_copy(
-            sums.at[0, 0, 0, 0, 0], keep.at[0, 0, 0, 0], out_sems.at[started[n]]
+            sums.at[0, 0, 0, 0, 0], outs[0].at[0, 0, 0], out_sems.at[started[n]]
         ).wait()
 
     if not late:
@@ -236,16 +235,16 @@
     terms = lefts[0].shape[0]
     smem = pl.BlockSpec(memory_space=pltpu.SMEM)
     hbm = pl.BlockSpec(memory_space=pl.ANY)
-    out = jax.ShapeDtypeStruct((4, 2, 2, 2, B, B), jnp.bfloat16)
+    out = jax.ShapeDtypeStruct((4, 2, 2, B, B), jnp.bfloat16)
     masked = jax.ShapeDtypeStruct((8, 8, B, B), jnp.bfloat16)
     late = bool(before)
     n_in = 3 + 2 * len(lefts) + len(wave)
     return pl.pallas_call(
         functools.partial(products_kernel, late, terms),
-        out_shape=(out, out) if late else (out, out, masked),
+        out_shape=(out,) * 4 if late else (out,) * 4 + (masked,),
         in_specs=[smem] * 3 + [hbm] * (n_in - 3 + len(before)),
-        out_specs=(hbm,) * (2 if late else 3),
-        input_output_aliases={n_in: 0, n_in + 1: 1} if late else {},
+        out_specs=(hbm,) * (4 if late else 5),
+        input_output_aliases={n_in + at: at for at in range(len(before))},
         scratch_shapes=[
             pltpu.VMEM((8, terms, B, B), jnp.bfloat16),
             pltpu.VMEM((8, terms, B, B), jnp.bfloat16),
@@ -304,8 +303,9 @@
     return (*row, *(lax.ppermute(part, "core", swapped(2, 1)) for part in row))
 
 
-def add_cores(keep, other, s):
-    both = [keep[d, s].astype(jnp.float32) + other[d, s].astype(jnp.float32) for d in range(4)]
+def add_cores(keep, send):
+    other = lax.ppermute(send, "core", shifted(2, 1))
+    both = [keep[d].astype(jnp.float32) + other[d].astype(jnp.float32) for d in range(4)]
     return both[0], [part.astype(jnp.bfloat16) for part in both[1:]]
 
 
@@ -333,9 +333,8 @@
     *sums, masked = products(pos, allowed, block_units, lefts, rights, wave)
     lefts = (*lefts, *ring_far(far_l, "y"))
     rights = (*rights, *ring_far(far_r, "z"))
-    keep, send = products(pos, allowed, block_units, lefts, rights, (masked,), sums)
-    other = lax.ppermute(send, "core", shifted(2, 1))
-    halves = [add_cores(keep, other, s) for s in range(2)]
+    sums = products(pos, allowed, block_units, lefts, rights, (masked,), sums)
+    halves = [add_cores(sums[s], sums[2 + s]) for s in range(2)]
     halves = [(own, add_send(chips)) for own, chips in halves]
 
     got = []

time: 120 us -> 121 us (level)
  waiting for transfers between devices: 43.2 us -> 38.9 us
  Pallas kernels: 24.8 us -> 29.1 us
  starting transfers between devices: 43.7 us -> 46 us
    pallas_call x2, Pallas kernels: 24.8 us -> 29.1 us  [products(): pl.pallas_call(functools.partial(products_kernel, late, terms), out_shape...]
    ppermute x2, waiting for transfers between devices: 3.06 us -> 0.01 us  [ring_far(): lax.ppermute(halves[0], axis, shifted(4, 1))]
    ppermute x2, starting transfers between devices: 11.1 us -> 13.8 us  [shards(): got.append(lax.ppermute(add_chips(*half), ('core', 'z'), perm))]
    ppermute x1 -> x2, waiting for transfers between devices: 2.49 us -> 1.57 us  [add_cores(): other = lax.ppermute(send, 'core', shifted(2, 1))]
  transfers between devices with their start and end apart: 27 -> 28, of which waited for: 12 -> 9; matrix products, arithmetic and copies ran while one was open for 2% -> 3% of each run, Pallas kernels for 11% -> 14%
where the time goes in v4:
time: 121 us
  starting transfers between devices  46 us (38%)
  waiting for transfers between devices  38.9 us (32%)
  Pallas kernels  29.1 us (24%)
  other arithmetic  3.97 us (3%)
  local copies, waits for them, and re-layouts  2.56 us (2%)
    pallas_call x2, Pallas kernels, products(): pl.pallas_call(functools.partial(products_kernel, late, terms), out_shape...  29.1 us
    ppermute x3, waiting for transfers between devices, gather_wave(): row = [mine] + [lax.ppermute(mine, 'x', shifted(4, d)) for d in (1, 2, 3)]  17.8 us
    ppermute x2, starting transfers between devices, shards(): got.append(lax.ppermute(add_chips(*half), ('core', 'z'), perm))  13.8 us
    ppermute x2, waiting for transfers between devices, ring_near(): lax.ppermute(own, axis, shifted(4, 1))  8.51 us
    ppermute x4, starting transfers between devices, share_wave(): return (*row, *(lax.ppermute(part, 'core', swapped(2, 1)) for part in row))  6.92 us
    ppermute x6, starting transfers between devices, add_send(): lax.ppermute(part, 'x', shifted(4, d + 1))  6.04 us
    ppermute x2, waiting for transfers between devices, shards(): got.append(lax.ppermute(add_chips(*half), ('core', 'z'), perm))  4.79 us
    ppermute x2, starting transfers between devices, ring_far(): lax.ppermute(halves[1], axis, shifted(4, -1))  4.76 us
  transfers between devices with their start and end apart: 28, of which 9 were waited for; matrix products, arithmetic and copies ran while one was open for 3% of the time, Pallas kernels for 14%

profile of v4, /device:TPU:7, one launch (start us, length us, event | category | flops | bytes accessed | tf_op | source)
XLA Modules:
  0.0 120.9 jit_solution(4896023689595623989)
XLA Ops:
  0.0 1.0 dynamic-slice_bitcast_fusion
  1.0 1.4 %collective-permute-start = (bf16[2,128,128]{2,1,0:T(8,128)(2,1)S(1)}, bf16[2,128,128]{2,1,0:T(8,128)(2,1)S(1)}, u32[]{:S(2)}, u32[]{:S(2)}) collective-permute-start(bf16[2,128,128]{2,1,0:T(8,128)(2,1)S(1)} %get-tuple-element.67), channel_id=1, source_target_pairs={{0,4},{4,8},{8,12},{12,0},{1,5},{5,9},{9,13},{13,1},{2,6},{6,10},{... | collective-permute-start | bytes 196616 | tf_op jit(solution)/shard_map/ppermute | solution.py:292
  2.3 1.5 %collective-permute-start.1 = (bf16[2,128,128]{2,1,0:T(8,128)(2,1)S(1)}, bf16[2,128,128]{2,1,0:T(8,128)(2,1)S(1)}, u32[]{:S(2)}, u32[]{:S(2)}) collective-permute-start(bf16[2,128,128]{2,1,0:T(8,128)(2,1)S(1)} %get-tuple-element.66), channel_id=1, source_target_pairs={{0,12},{4,0},{8,4},{12,8},{1,13},{5,1},{9,5},{13,9},{2,14},{6,2},{... | collective-permute-start | bytes 196616 | tf_op jit(solution)/shard_map/ppermute | solution.py:292
  3.8 1.6 %collective-permute-start.2 = (bf16[2,128,128]{2,1,0:T(8,128)(2,1)S(1)}, bf16[2,128,128]{2,1,0:T(8,128)(2,1)S(1)}, u32[]{:S(2)}, u32[]{:S(2)}) collective-permute-start(bf16[2,128,128]{2,1,0:T(8,128)(2,1)S(1)} %get-tuple-element.68), channel_id=1, source_target_pairs={{0,8},{4,12},{8,0},{12,4},{1,9},{5,13},{9,1},{13,5},{2,10},{6,14},... | collective-permute-start | bytes 196616 | tf_op jit(solution)/shard_map/ppermute | solution.py:292
  5.4 3.0 %collective-permute-done.2 = bf16[2,128,128]{2,1,0:T(8,128)(2,1)S(1)} collective-permute-done((bf16[2,128,128]{2,1,0:T(8,128)(2,1)S(1)}, bf16[2,128,128]{2,1,0:T(8,128)(2,1)S(1)}, u32[]{:S(2)}, u32[]{:S(2)}) %collective-permute-start.2) | collective-permute-done | bytes 65568 | tf_op jit(solution)/shard_map/ppermute | solution.py:292
  8.5 0.3 collective-permute-start.6
  8.7 2.4 %collective-permute-start.7 = (bf16[24,2,128,128]{3,2,1,0:T(8,128)(2,1)}, bf16[24,2,128,128]{3,2,1,0:T(8,128)(2,1)S(1)}, u32[]{:S(2)}, u32[]{:S(2)}) collective-permute-start(bf16[24,2,128,128]{3,2,1,0:T(8,128)(2,1)} %refs_0_.1), channel_id=1, source_target_pairs={{0,12},{4,0},{8,4},{12,8},{1,13},{5,1},{9,5},{13,9},{2,14},{6,2},{... | collective-permute-start | bytes 4718600 | tf_op jit(solution)/shard_map/ppermute | solution.py:269
  11.1 1.6 %collective-permute-start.10 = (bf16[24,2,128,128]{3,2,1,0:T(8,128)(2,1)}, bf16[24,2,128,128]{3,2,1,0:T(8,128)(2,1)S(1)}, u32[]{:S(2)}, u32[]{:S(2)}) collective-permute-start(bf16[24,2,128,128]{3,2,1,0:T(8,128)(2,1)} %refs_5_), channel_id=1, source_target_pairs={{0,1},{1,2},{2,3},{3,0},{4,5},{5,6},{6,7},{7,4},{8,9},{9,10},{10,1... | collective-permute-start | bytes 4718600 | tf_op jit(solution)/shard_map/ppermute | solution.py:269
  12.8 2.1 %collective-permute-start.11 = (bf16[24,2,128,128]{3,2,1,0:T(8,128)(2,1)}, bf16[24,2,128,128]{3,2,1,0:T(8,128)(2,1)S(1)}, u32[]{:S(2)}, u32[]{:S(2)}) collective-permute-start(bf16[24,2,128,128]{3,2,1,0:T(8,128)(2,1)} %refs_5_), channel_id=1, source_target_pairs={{0,3},{1,0},{2,1},{3,2},{4,7},{5,4},{6,5},{7,6},{8,11},{9,8},{10,9... | collective-permute-start | bytes 4718600 | tf_op jit(solution)/shard_map/ppermute | solution.py:269
  15.0 0.3 collective-permute-start.3
  15.2 5.3 %collective-permute-done.3.refs_7_ = bf16[8,128,128]{2,1,0:T(8,128)(2,1)S(1)} collective-permute-done((bf16[8,128,128]{2,1,0:T(8,128)(2,1)S(1)}, bf16[8,128,128]{2,1,0:T(8,128)(2,1)S(1)}, u32[]{:S(2)}, u32[]{:S(2)}) %collective-permute-start.3) | collective-permute-done | bytes 262176 | tf_op jit(solution)/shard_map/ppermute | solution.py:298
  20.5 1.1 collective-permute-start.4
  21.7 5.6 %collective-permute-done.4.refs_8_ = bf16[8,128,128]{2,1,0:T(8,128)(2,1)S(1)} collective-permute-done((bf16[8,128,128]{2,1,0:T(8,128)(2,1)S(1)}, bf16[8,128,128]{2,1,0:T(8,128)(2,1)S(1)}, u32[]{:S(2)}, u32[]{:S(2)}) %collective-permute-start.4) | collective-permute-done | bytes 262176 | tf_op jit(solution)/shard_map/ppermute | solution.py:298
  27.3 0.8 collective-permute-start.5
  28.1 6.9 %collective-permute-done.5.refs_9_ = bf16[8,128,128]{2,1,0:T(8,128)(2,1)} collective-permute-done((bf16[8,128,128]{2,1,0:T(8,128)(2,1)S(1)}, bf16[8,128,128]{2,1,0:T(8,128)(2,1)}, u32[]{:S(2)}, u32[]{:S(2)}) %collective-permute-start.5) | collective-permute-done | bytes 262176 | tf_op jit(solution)/shard_map/ppermute | solution.py:298
  35.0 8.5 %collective-permute-done.6.refs_1_ = bf16[24,2,128,128]{3,2,1,0:T(8,128)(2,1)S(1)} collective-permute-done((bf16[24,2,128,128]{3,2,1,0:T(8,128)(2,1)}, bf16[24,2,128,128]{3,2,1,0:T(8,128)(2,1)S(1)}, u32[]{:S(2)}, u32[]{:S(2)}) %collective-permute-start.6) | collective-permute-done | bytes 1572896 | tf_op jit(solution)/shard_map/ppermute | solution.py:269
  43.5 3.2 %collective-permute-start.14 = (bf16[8,128,128]{2,1,0:T(8,128)(2,1)S(1)}, bf16[8,128,128]{2,1,0:T(8,128)(2,1)S(1)}, u32[]{:S(2)}, u32[]{:S(2)}) collective-permute-start(bf16[8,128,128]{2,1,0:T(8,128)(2,1)S(1)} %pad_maximum_fusion.refs_6_), channel_id=1, source_target_pairs={{0,16},{16,0},{1,17},{17,1},{2,18},{18,2},{3,19},{19,3},{4,20},{20... | collective-permute-start | bytes 786440 | tf_op jit(solution)/shard_map/ppermute | solution.py:303
  46.8 0.1 collective-permute-start.15
  46.9 0.4 collective-permute-start.16
  47.3 3.2 %collective-permute-start.17 = (bf16[8,128,128]{2,1,0:T(8,128)(2,1)}, bf16[8,128,128]{2,1,0:T(8,128)(2,1)}, u32[]{:S(2)}, u32[]{:S(2)}) collective-permute-start(bf16[8,128,128]{2,1,0:T(8,128)(2,1)} %collective-permute-done.5.refs_9_), channel_id=1, source_target_pairs={{0,16},{16,0},{1,17},{17,1},{2,18},{18,2},{3,19},{19,3},{4,20},{20... | collective-permute-start | bytes 786440 | tf_op jit(solution)/shard_map/ppermute | solution.py:303
  50.7 0.1 collective-permute-start.8
  50.8 2.7 %collective-permute-start.9 = (bf16[12,2,128,128]{3,2,1,0:T(8,128)(2,1)S(1)}, bf16[12,2,128,128]{3,2,1,0:T(8,128)(2,1)}, u32[]{:S(2)}, u32[]{:S(2)}) collective-permute-start(bf16[12,2,128,128]{3,2,1,0:T(8,128)(2,1)S(1)} %slice.61), channel_id=1, source_target_pairs={{0,12},{4,0},{8,4},{12,8},{1,13},{5,1},{9,5},{13,9},{2,14},{6,2},{... | collective-permute-start | bytes 2359304 | tf_op jit(solution)/shard_map/ppermute | solution.py:280
  53.6 0.6 copy-done.9
  54.3 0.7 copy-done.10
  55.0 2.0 %collective-permute-start.13 = (bf16[12,2,128,128]{3,2,1,0:T(8,128)(2,1)S(1)}, bf16[12,2,128,128]{3,2,1,0:T(8,128)(2,1)}, u32[]{:S(2)}, u32[]{:S(2)}) collective-permute-start(bf16[12,2,128,128]{3,2,1,0:T(8,128)(2,1)S(1)} %slice.81), channel_id=1, source_target_pairs={{0,3},{1,0},{2,1},{3,2},{4,7},{5,4},{6,5},{7,6},{8,11},{9,8},{10,9... | collective-permute-start | bytes 2359304 | tf_op jit(solution)/shard_map/ppermute | solution.py:280
  57.0 0.6 pad_add_fusion.pos
  57.6 16.7 %shard_map.55 = (bf16[4,2,2,128,128]{4,3,2,1,0:T(8,128)(2,1)}, bf16[4,2,2,128,128]{4,3,2,1,0:T(8,128)(2,1)}, bf16[4,2,2,128,128]{4,3,2,1,0:T(8,128)(2,1)}, bf16[...) custom-call(s32[4]{0:T(128)} %pad_add_fusion.pos, s32[32,32]{1,0:T(8,128)} %allowed.3, s32[32]{0:T(128)} %units.3, ...), custom_call_target="tpu_custom_call" | custom-call | flops 6442450944 | bytes 14680064 | tf_op jit(solution)/shard_map/pallas_call | solution.py:242
  74.4 12.4 %shard_map.56 = (bf16[4,2,2,128,128]{4,3,2,1,0:T(8,128)(2,1)}, bf16[4,2,2,128,128]{4,3,2,1,0:T(8,128)(2,1)}, bf16[4,2,2,128,128]{4,3,2,1,0:T(8,128)(2,1)}, bf16[4,2,2,128,128]{4,3,2,1,0:T(8,128)(2,1)}) custom-call(s32[4]{0:T(128)} %pad_add_fusion.pos, s32[32,32]{1,0:T(8,128)} %allowed.3, ...), custom_call_target="tpu_custom_call", output_to_operand_aliasing={{0}: (14, {}), {1}: (15, {}), {2}: (16, {}), {3}: (17, {})} | custom-call | flops 6442450944 | bytes 14680064 | tf_op jit(solution)/shard_map/pallas_call | solution.py:242
  86.8 1.3 %collective-permute-start.22 = (bf16[4,2,2,128,128]{4,3,2,1,0:T(8,128)(2,1)}, bf16[4,2,2,128,128]{4,3,2,1,0:T(8,128)(2,1)S(1)}, u32[]{:S(2)}, u32[]{:S(2)}) collective-permute-start(bf16[4,2,2,128,128]{4,3,2,1,0:T(8,128)(2,1)} %get-tuple-element.55), channel_id=1, source_target_pairs={{0,16},{16,0},{1,17},{17,1},{2,18},{18,2},{3,19},{19,3},{4,20},{20... | collective-permute-start | bytes 1572872 | tf_op jit(solution)/shard_map/ppermute | solution.py:307
  88.0 0.1 collective-permute-start.18
  88.1 0.1 iota_compare_fusion
  88.2 1.6 %collective-permute-done.22 = bf16[4,2,2,128,128]{4,3,2,1,0:T(8,128)(2,1)S(1)} collective-permute-done((bf16[4,2,2,128,128]{4,3,2,1,0:T(8,128)(2,1)}, bf16[4,2,2,128,128]{4,3,2,1,0:T(8,128)(2,1)S(1)}, u32[]{:S(2)}, u32[]{:S(2)}) %collective-permute-start.22) | collective-permute-done | bytes 524320 | tf_op jit(solution)/shard_map/ppermute | solution.py:307
  89.8 1.2 %fusion.5 = (bf16[2,2,128,128]{3,2,1,0:T(8,128)(2,1)S(1)}, bf16[2,2,128,128]{3,2,1,0:T(8,128)(2,1)S(1)}, bf16[2,2,128,128]{3,2,1,0:T(8,128)(2,1)S(1)}, f32[2,2,128,128]{3,2,1,0:T(8,128)S(1)}) fusion(bf16[4,2,2,128,128]{4,3,2,1,0:T(8,128)(2,1)S(1)} %collective-permute-done.22, bf16[4,2,2,128,128]{4,3,2,1,0:T(8,128)(2,1)} %get-tuple-element.54), kind=kLoop, calls=%fused_computation.17 | loop fusion | flops 983040 | bytes 1703936 | tf_op jit(solution)/shard_map/convert_element_type | solution.py:309
  91.0 0.3 collective-permute-start.23
  91.3 2.2 %collective-permute-start.24 = (bf16[2,2,128,128]{3,2,1,0:T(8,128)(2,1)S(1)}, bf16[2,2,128,128]{3,2,1,0:T(8,128)(2,1)S(1)}, u32[]{:S(2)}, u32[]{:S(2)}) collective-permute-start(bf16[2,2,128,128]{3,2,1,0:T(8,128)(2,1)S(1)} %get-tuple-element.70), channel_id=1, source_target_pairs={{0,64},{32,96},{64,0},{96,32},{1,65},{33,97},{65,1},{97,33},{2,66}... | collective-permute-start | bytes 393224 | tf_op jit(solution)/shard_map/ppermute | solution.py:313
  93.4 0.1 fusion.2
  93.6 2.7 %collective-permute-start.19 = (bf16[2,2,128,128]{3,2,1,0:T(8,128)(2,1)S(1)}, bf16[2,2,128,128]{3,2,1,0:T(8,128)(2,1)S(1)}, u32[]{:S(2)}, u32[]{:S(2)}) collective-permute-start(bf16[2,2,128,128]{3,2,1,0:T(8,128)(2,1)S(1)} %get-tuple-element.75), channel_id=1, source_target_pairs={{0,32},{32,64},{64,96},{96,0},{1,33},{33,65},{65,97},{97,1},{2,34}... | collective-permute-start | bytes 393224 | tf_op jit(solution)/shard_map/ppermute | solution.py:313
  96.3 0.1 collective-permute-start.20
  96.4 0.8 collective-permute-start.21
  97.2 3.1 %collective-permute-done.25 = bf16[2,2,128,128]{3,2,1,0:T(8,128)(2,1)S(1)} collective-permute-done((bf16[2,2,128,128]{3,2,1,0:T(8,128)(2,1)S(1)}, bf16[2,2,128,128]{3,2,1,0:T(8,128)(2,1)S(1)}, u32[]{:S(2)}, u32[]{:S(2)}) %collective-permute-start.25) | collective-permute-done | bytes 131104 | tf_op jit(solution)/shard_map/ppermute | solution.py:313
  100.4 9.4 %collective-permute-start.26 = (bf16[2,2,128,128]{3,2,1,0:T(8,128)(2,1)S(1)}, bf16[2,2,128,128]{3,2,1,0:T(8,128)(2,1)S(1)}, u32[]{:S(2)}, u32[]{:S(2)}) collective-permute-start(bf16[2,2,128,128]{3,2,1,0:T(8,128)(2,1)S(1)} %add_convert_fusion.1), channel_id=1, source_target_pairs={{0,0},{1,1},{2,16},{3,17},{16,2},{17,3},{18,18},{19,19},{4,4},{5,5... | collective-permute-start | bytes 393224 | tf_op jit(solution)/shard_map/ppermute | solution.py:348
  109.7 0.8 dynamic-slice_compare_fusion
  110.6 2.2 %collective-permute-done.26 = bf16[2,2,128,128]{3,2,1,0:T(8,128)(2,1)S(1)} collective-permute-done((bf16[2,2,128,128]{3,2,1,0:T(8,128)(2,1)S(1)}, bf16[2,2,128,128]{3,2,1,0:T(8,128)(2,1)S(1)}, u32[]{:S(2)}, u32[]{:S(2)}) %collective-permute-start.26) | collective-permute-done | bytes 131104 | tf_op jit(solution)/shard_map/ppermute | solution.py:348
  112.8 0.1 add_convert_fusion
  112.9 4.4 %collective-permute-start.27 = (bf16[2,2,128,128]{3,2,1,0:T(8,128)(2,1)S(1)}, bf16[2,2,128,128]{3,2,1,0:T(8,128)(2,1)S(1)}, u32[]{:S(2)}, u32[]{:S(2)}) collective-permute-start(bf16[2,2,128,128]{3,2,1,0:T(8,128)(2,1)S(1)} %add_convert_fusion), channel_id=1, source_target_pairs={{0,1},{1,0},{2,17},{3,16},{16,3},{17,2},{18,19},{19,18},{4,5},{5,4... | collective-permute-start | bytes 393224 | tf_op jit(solution)/shard_map/ppermute | solution.py:348
  117.3 0.1 broadcast_and_fusion
  117.4 2.6 %collective-permute-done.27 = bf16[2,2,128,128]{3,2,1,0:T(8,128)(2,1)S(1)} collective-permute-done((bf16[2,2,128,128]{3,2,1,0:T(8,128)(2,1)S(1)}, bf16[2,2,128,128]{3,2,1,0:T(8,128)(2,1)S(1)}, u32[]{:S(2)}, u32[]{:S(2)}) %collective-permute-start.27) | collective-permute-done | bytes 131104 | tf_op jit(solution)/shard_map/ppermute | solution.py:348
  120.0 0.9 and_select_fusion
  (53 shorter events, 0.5 us)
Async XLA Ops:
  1.0 4.5 %collective-permute-start = (bf16[2,128,128]{2,1,0:T(8,128)(2,1)S(1)}, bf16[2,128,128]{2,1,0:T(8,128)(2,1)S(1)}, u32[]{:S(2)}, u32[]{:S(2)}) collective-permute-start(bf16[2,128,128]{2,1,0:T(8,128)(2,1)S(1)} %get-tuple-element.67), channel_id=1, source_target_pairs={{0,4},{4,8},{8,12},{12,0},{1,5},{5,9},{9,13},{13,1},{2,6},{6,10},{... | collective-permute-start | bytes 196616 | tf_op jit(solution)/shard_map/ppermute | solution.py:292
  2.3 3.1 %collective-permute-start.1 = (bf16[2,128,128]{2,1,0:T(8,128)(2,1)S(1)}, bf16[2,128,128]{2,1,0:T(8,128)(2,1)S(1)}, u32[]{:S(2)}, u32[]{:S(2)}) collective-permute-start(bf16[2,128,128]{2,1,0:T(8,128)(2,1)S(1)} %get-tuple-element.66), channel_id=1, source_target_pairs={{0,12},{4,0},{8,4},{12,8},{1,13},{5,1},{9,5},{13,9},{2,14},{6,2},{... | collective-permute-start | bytes 196616 | tf_op jit(solution)/shard_map/ppermute | solution.py:292
  3.8 4.6 %collective-permute-start.2 = (bf16[2,128,128]{2,1,0:T(8,128)(2,1)S(1)}, bf16[2,128,128]{2,1,0:T(8,128)(2,1)S(1)}, u32[]{:S(2)}, u32[]{:S(2)}) collective-permute-start(bf16[2,128,128]{2,1,0:T(8,128)(2,1)S(1)} %get-tuple-element.68), channel_id=1, source_target_pairs={{0,8},{4,12},{8,0},{12,4},{1,9},{5,13},{9,1},{13,5},{2,10},{6,14},... | collective-permute-start | bytes 196616 | tf_op jit(solution)/shard_map/ppermute | solution.py:292
  8.5 35.1 %collective-permute-start.6 = (bf16[24,2,128,128]{3,2,1,0:T(8,128)(2,1)}, bf16[24,2,128,128]{3,2,1,0:T(8,128)(2,1)S(1)}, u32[]{:S(2)}, u32[]{:S(2)}) collective-permute-start(bf16[24,2,128,128]{3,2,1,0:T(8,128)(2,1)} %refs_0_.1), channel_id=1, source_target_pairs={{0,4},{4,8},{8,12},{12,0},{1,5},{5,9},{9,13},{13,1},{2,6},{6,10},{... | collective-permute-start | bytes 4718600 | tf_op jit(solution)/shard_map/ppermute | solution.py:269
  8.7 34.8 %collective-permute-start.7 = (bf16[24,2,128,128]{3,2,1,0:T(8,128)(2,1)}, bf16[24,2,128,128]{3,2,1,0:T(8,128)(2,1)S(1)}, u32[]{:S(2)}, u32[]{:S(2)}) collective-permute-start(bf16[24,2,128,128]{3,2,1,0:T(8,128)(2,1)} %refs_0_.1), channel_id=1, source_target_pairs={{0,12},{4,0},{8,4},{12,8},{1,13},{5,1},{9,5},{13,9},{2,14},{6,2},{... | collective-permute-start | bytes 4718600 | tf_op jit(solution)/shard_map/ppermute | solution.py:269
  11.1 36.1 %collective-permute-start.10 = (bf16[24,2,128,128]{3,2,1,0:T(8,128)(2,1)}, bf16[24,2,128,128]{3,2,1,0:T(8,128)(2,1)S(1)}, u32[]{:S(2)}, u32[]{:S(2)}) collective-permute-start(bf16[24,2,128,128]{3,2,1,0:T(8,128)(2,1)} %refs_5_), channel_id=1, source_target_pairs={{0,1},{1,2},{2,3},{3,0},{4,5},{5,6},{6,7},{7,4},{8,9},{9,10},{10,1... | collective-permute-start | bytes 4718600 | tf_op jit(solution)/shard_map/ppermute | solution.py:269
  12.8 37.9 %collective-permute-start.11 = (bf16[24,2,128,128]{3,2,1,0:T(8,128)(2,1)}, bf16[24,2,128,128]{3,2,1,0:T(8,128)(2,1)S(1)}, u32[]{:S(2)}, u32[]{:S(2)}) collective-permute-start(bf16[24,2,128,128]{3,2,1,0:T(8,128)(2,1)} %refs_5_), channel_id=1, source_target_pairs={{0,3},{1,0},{2,1},{3,2},{4,7},{5,4},{6,5},{7,6},{8,11},{9,8},{10,9... | collective-permute-start | bytes 4718600 | tf_op jit(solution)/shard_map/ppermute | solution.py:269
  14.9 42.6 %copy-start.5 = (bf16[8,128,128]{2,1,0:T(8,128)(2,1)}, bf16[8,128,128]{2,1,0:T(8,128)(2,1)S(1)}, u32[]{:S(2)}) copy-start(bf16[8,128,128]{2,1,0:T(8,128)(2,1)S(1)} %pad_maximum_fusion.refs_6_) | copy-start | bytes 786436
  15.0 5.6 %collective-permute-start.3 = (bf16[8,128,128]{2,1,0:T(8,128)(2,1)S(1)}, bf16[8,128,128]{2,1,0:T(8,128)(2,1)S(1)}, u32[]{:S(2)}, u32[]{:S(2)}) collective-permute-start(bf16[8,128,128]{2,1,0:T(8,128)(2,1)S(1)} %pad_maximum_fusion.refs_6_), channel_id=1, source_target_pairs={{0,32},{32,64},{64,96},{96,0},{1,33},{33,65},{65,97},{97,1},{2,34}... | collective-permute-start | bytes 786440 | tf_op jit(solution)/shard_map/ppermute | solution.py:298
  20.5 33.1 %copy-start.6 = (bf16[8,128,128]{2,1,0:T(8,128)(2,1)}, bf16[8,128,128]{2,1,0:T(8,128)(2,1)S(1)}, u32[]{:S(2)}) copy-start(bf16[8,128,128]{2,1,0:T(8,128)(2,1)S(1)} %collective-permute-done.3.refs_7_) | copy-start | bytes 786436
  20.5 6.7 %collective-permute-start.4 = (bf16[8,128,128]{2,1,0:T(8,128)(2,1)S(1)}, bf16[8,128,128]{2,1,0:T(8,128)(2,1)S(1)}, u32[]{:S(2)}, u32[]{:S(2)}) collective-permute-start(bf16[8,128,128]{2,1,0:T(8,128)(2,1)S(1)} %pad_maximum_fusion.refs_6_), channel_id=1, source_target_pairs={{0,64},{32,96},{64,0},{96,32},{1,65},{33,97},{65,1},{97,33},{2,66}... | collective-permute-start | bytes 786440 | tf_op jit(solution)/shard_map/ppermute | solution.py:298
  27.3 26.3 %copy-start.7 = (bf16[8,128,128]{2,1,0:T(8,128)(2,1)}, bf16[8,128,128]{2,1,0:T(8,128)(2,1)S(1)}, u32[]{:S(2)}) copy-start(bf16[8,128,128]{2,1,0:T(8,128)(2,1)S(1)} %collective-permute-done.4.refs_8_) | copy-start | bytes 786436
  27.3 7.7 %collective-permute-start.5 = (bf16[8,128,128]{2,1,0:T(8,128)(2,1)S(1)}, bf16[8,128,128]{2,1,0:T(8,128)(2,1)}, u32[]{:S(2)}, u32[]{:S(2)}) collective-permute-start(bf16[8,128,128]{2,1,0:T(8,128)(2,1)S(1)} %pad_maximum_fusion.refs_6_), channel_id=1, source_target_pairs={{0,96},{32,0},{64,32},{96,64},{1,97},{33,1},{65,33},{97,65},{2,98}... | collective-permute-start | bytes 786440 | tf_op jit(solution)/shard_map/ppermute | solution.py:298
  43.5 7.1 %copy-start.1 = (bf16[24,2,128,128]{3,2,1,0:T(8,128)(2,1)}, bf16[24,2,128,128]{3,2,1,0:T(8,128)(2,1)S(1)}, u32[]{:S(2)}) copy-start(bf16[24,2,128,128]{3,2,1,0:T(8,128)(2,1)S(1)} %collective-permute-done.6.refs_1_) | copy-start | bytes 4718596
  43.5 7.1 %copy-start.2 = (bf16[24,2,128,128]{3,2,1,0:T(8,128)(2,1)}, bf16[24,2,128,128]{3,2,1,0:T(8,128)(2,1)S(1)}, u32[]{:S(2)}) copy-start(bf16[24,2,128,128]{3,2,1,0:T(8,128)(2,1)S(1)} %collective-permute-done.7.refs_2_) | copy-start | bytes 4718596
  43.5 7.3 %collective-permute-start.14 = (bf16[8,128,128]{2,1,0:T(8,128)(2,1)S(1)}, bf16[8,128,128]{2,1,0:T(8,128)(2,1)S(1)}, u32[]{:S(2)}, u32[]{:S(2)}) collective-permute-start(bf16[8,128,128]{2,1,0:T(8,128)(2,1)S(1)} %pad_maximum_fusion.refs_6_), channel_id=1, source_target_pairs={{0,16},{16,0},{1,17},{17,1},{2,18},{18,2},{3,19},{19,3},{4,20},{20... | collective-permute-start | bytes 786440 | tf_op jit(solution)/shard_map/ppermute | solution.py:303
  46.8 6.8 %collective-permute-start.15 = (bf16[8,128,128]{2,1,0:T(8,128)(2,1)S(1)}, bf16[8,128,128]{2,1,0:T(8,128)(2,1)S(1)}, u32[]{:S(2)}, u32[]{:S(2)}) collective-permute-start(bf16[8,128,128]{2,1,0:T(8,128)(2,1)S(1)} %collective-permute-done.3.refs_7_), channel_id=1, source_target_pairs={{0,16},{16,0},{1,17},{17,1},{2,18},{18,2},{3,19},{19,3},{4,20},{20... | collective-permute-start | bytes 786440 | tf_op jit(solution)/shard_map/ppermute | solution.py:303
  46.9 6.7 %collective-permute-start.16 = (bf16[8,128,128]{2,1,0:T(8,128)(2,1)S(1)}, bf16[8,128,128]{2,1,0:T(8,128)(2,1)S(1)}, u32[]{:S(2)}, u32[]{:S(2)}) collective-permute-start(bf16[8,128,128]{2,1,0:T(8,128)(2,1)S(1)} %collective-permute-done.4.refs_8_), channel_id=1, source_target_pairs={{0,16},{16,0},{1,17},{17,1},{2,18},{18,2},{3,19},{19,3},{4,20},{20... | collective-permute-start | bytes 786440 | tf_op jit(solution)/shard_map/ppermute | solution.py:303
  47.3 6.3 %copy-start.3 = (bf16[24,2,128,128]{3,2,1,0:T(8,128)(2,1)}, bf16[24,2,128,128]{3,2,1,0:T(8,128)(2,1)S(1)}, u32[]{:S(2)}) copy-start(bf16[24,2,128,128]{3,2,1,0:T(8,128)(2,1)S(1)} %collective-permute-done.10.refs_4_.refs_6_) | copy-start | bytes 4718596
  47.3 10.3 %collective-permute-start.17 = (bf16[8,128,128]{2,1,0:T(8,128)(2,1)}, bf16[8,128,128]{2,1,0:T(8,128)(2,1)}, u32[]{:S(2)}, u32[]{:S(2)}) collective-permute-start(bf16[8,128,128]{2,1,0:T(8,128)(2,1)} %collective-permute-done.5.refs_9_), channel_id=1, source_target_pairs={{0,16},{16,0},{1,17},{17,1},{2,18},{18,2},{3,19},{19,3},{4,20},{20... | collective-permute-start | bytes 786440 | tf_op jit(solution)/shard_map/ppermute | solution.py:303
  50.7 3.0 %copy-start.4 = (bf16[24,2,128,128]{3,2,1,0:T(8,128)(2,1)}, bf16[24,2,128,128]{3,2,1,0:T(8,128)(2,1)S(1)}, u32[]{:S(2)}) copy-start(bf16[24,2,128,128]{3,2,1,0:T(8,128)(2,1)S(1)} %collective-permute-done.11.refs_5_.refs_7_) | copy-start | bytes 4718596
  50.7 23.7 %collective-permute-start.8 = (bf16[12,2,128,128]{3,2,1,0:T(8,128)(2,1)S(1)}, bf16[12,2,128,128]{3,2,1,0:T(8,128)(2,1)}, u32[]{:S(2)}, u32[]{:S(2)}) collective-permute-start(bf16[12,2,128,128]{3,2,1,0:T(8,128)(2,1)S(1)} %slice.60), channel_id=1, source_target_pairs={{0,4},{4,8},{8,12},{12,0},{1,5},{5,9},{9,13},{13,1},{2,6},{6,10},{... | collective-permute-start | bytes 2359304 | tf_op jit(solution)/shard_map/ppermute | solution.py:279
  50.8 2.8 %copy-start.8 = (bf16[8,128,128]{2,1,0:T(8,128)(2,1)}, bf16[8,128,128]{2,1,0:T(8,128)(2,1)S(1)}, u32[]{:S(2)}) copy-start(bf16[8,128,128]{2,1,0:T(8,128)(2,1)S(1)} %collective-permute-done.14.refs_10_) | copy-start | bytes 786436
  50.8 23.5 %collective-permute-start.9 = (bf16[12,2,128,128]{3,2,1,0:T(8,128)(2,1)S(1)}, bf16[12,2,128,128]{3,2,1,0:T(8,128)(2,1)}, u32[]{:S(2)}, u32[]{:S(2)}) collective-permute-start(bf16[12,2,128,128]{3,2,1,0:T(8,128)(2,1)S(1)} %slice.61), channel_id=1, source_target_pairs={{0,12},{4,0},{8,4},{12,8},{1,13},{5,1},{9,5},{13,9},{2,14},{6,2},{... | collective-permute-start | bytes 2359304 | tf_op jit(solution)/shard_map/ppermute | solution.py:280
  53.6 0.7 copy-start.9
  53.6 20.8 %collective-permute-start.12 = (bf16[12,2,128,128]{3,2,1,0:T(8,128)(2,1)S(1)}, bf16[12,2,128,128]{3,2,1,0:T(8,128)(2,1)}, u32[]{:S(2)}, u32[]{:S(2)}) collective-permute-start(bf16[12,2,128,128]{3,2,1,0:T(8,128)(2,1)S(1)} %slice.80), channel_id=1, source_target_pairs={{0,1},{1,2},{2,3},{3,0},{4,5},{5,6},{6,7},{7,4},{8,9},{9,10},{10,1... | collective-permute-start | bytes 2359304 | tf_op jit(solution)/shard_map/ppermute | solution.py:279
  54.3 0.7 copy-start.10
  55.0 19.4 %collective-permute-start.13 = (bf16[12,2,128,128]{3,2,1,0:T(8,128)(2,1)S(1)}, bf16[12,2,128,128]{3,2,1,0:T(8,128)(2,1)}, u32[]{:S(2)}, u32[]{:S(2)}) collective-permute-start(bf16[12,2,128,128]{3,2,1,0:T(8,128)(2,1)S(1)} %slice.81), channel_id=1, source_target_pairs={{0,3},{1,0},{2,1},{3,2},{4,7},{5,4},{6,5},{7,6},{8,11},{9,8},{10,9... | collective-permute-start | bytes 2359304 | tf_op jit(solution)/shard_map/ppermute | solution.py:280
  74.4 13.7 %copy-start.11 = (s32[32]{0:T(128)S(1)}, s32[32]{0:T(128)}, u32[]{:S(2)}) copy-start(s32[32]{0:T(128)} %units.3) | copy-start | bytes 388
  86.7 6.7 %copy-start = (bf16[4,2,2,128,128]{4,3,2,1,0:T(8,128)(2,1)S(1)}, bf16[4,2,2,128,128]{4,3,2,1,0:T(8,128)(2,1)}, u32[]{:S(2)}) copy-start(bf16[4,2,2,128,128]{4,3,2,1,0:T(8,128)(2,1)} %get-tuple-element.52) | copy-start | bytes 1572868
  86.8 3.0 %collective-permute-start.22 = (bf16[4,2,2,128,128]{4,3,2,1,0:T(8,128)(2,1)}, bf16[4,2,2,128,128]{4,3,2,1,0:T(8,128)(2,1)S(1)}, u32[]{:S(2)}, u32[]{:S(2)}) collective-permute-start(bf16[4,2,2,128,128]{4,3,2,1,0:T(8,128)(2,1)} %get-tuple-element.55), channel_id=1, source_target_pairs={{0,16},{16,0},{1,17},{17,1},{2,18},{18,2},{3,19},{19,3},{4,20},{20... | collective-permute-start | bytes 1572872 | tf_op jit(solution)/shard_map/ppermute | solution.py:307
  88.0 5.4 %collective-permute-start.18 = (bf16[4,2,2,128,128]{4,3,2,1,0:T(8,128)(2,1)}, bf16[4,2,2,128,128]{4,3,2,1,0:T(8,128)(2,1)S(1)}, u32[]{:S(2)}, u32[]{:S(2)}) collective-permute-start(bf16[4,2,2,128,128]{4,3,2,1,0:T(8,128)(2,1)} %get-tuple-element.53), channel_id=1, source_target_pairs={{0,16},{16,0},{1,17},{17,1},{2,18},{18,2},{3,19},{19,3},{4,20},{20... | collective-permute-start | bytes 1572872 | tf_op jit(solution)/shard_map/ppermute | solution.py:307
  91.0 5.4 %collective-permute-start.23 = (bf16[2,2,128,128]{3,2,1,0:T(8,128)(2,1)S(1)}, bf16[2,2,128,128]{3,2,1,0:T(8,128)(2,1)S(1)}, u32[]{:S(2)}, u32[]{:S(2)}) collective-permute-start(bf16[2,2,128,128]{3,2,1,0:T(8,128)(2,1)S(1)} %get-tuple-element.71), channel_id=1, source_target_pairs={{0,32},{32,64},{64,96},{96,0},{1,33},{33,65},{65,97},{97,1},{2,34}... | collective-permute-start | bytes 393224 | tf_op jit(solution)/shard_map/ppermute | solution.py:313
  91.3 5.9 %collective-permute-start.24 = (bf16[2,2,128,128]{3,2,1,0:T(8,128)(2,1)S(1)}, bf16[2,2,128,128]{3,2,1,0:T(8,128)(2,1)S(1)}, u32[]{:S(2)}, u32[]{:S(2)}) collective-permute-start(bf16[2,2,128,128]{3,2,1,0:T(8,128)(2,1)S(1)} %get-tuple-element.70), channel_id=1, source_target_pairs={{0,64},{32,96},{64,0},{96,32},{1,65},{33,97},{65,1},{97,33},{2,66}... | collective-permute-start | bytes 393224 | tf_op jit(solution)/shard_map/ppermute | solution.py:313
  93.4 6.9 %collective-permute-start.25 = (bf16[2,2,128,128]{3,2,1,0:T(8,128)(2,1)S(1)}, bf16[2,2,128,128]{3,2,1,0:T(8,128)(2,1)S(1)}, u32[]{:S(2)}, u32[]{:S(2)}) collective-permute-start(bf16[2,2,128,128]{3,2,1,0:T(8,128)(2,1)S(1)} %get-tuple-element.69), channel_id=1, source_target_pairs={{0,96},{32,0},{64,32},{96,64},{1,97},{33,1},{65,33},{97,65},{2,98}... | collective-permute-start | bytes 393224 | tf_op jit(solution)/shard_map/ppermute | solution.py:313
  93.6 16.9 %collective-permute-start.19 = (bf16[2,2,128,128]{3,2,1,0:T(8,128)(2,1)S(1)}, bf16[2,2,128,128]{3,2,1,0:T(8,128)(2,1)S(1)}, u32[]{:S(2)}, u32[]{:S(2)}) collective-permute-start(bf16[2,2,128,128]{3,2,1,0:T(8,128)(2,1)S(1)} %get-tuple-element.75), channel_id=1, source_target_pairs={{0,32},{32,64},{64,96},{96,0},{1,33},{33,65},{65,97},{97,1},{2,34}... | collective-permute-start | bytes 393224 | tf_op jit(solution)/shard_map/ppermute | solution.py:313
  96.3 14.2 %collective-permute-start.20 = (bf16[2,2,128,128]{3,2,1,0:T(8,128)(2,1)S(1)}, bf16[2,2,128,128]{3,2,1,0:T(8,128)(2,1)S(1)}, u32[]{:S(2)}, u32[]{:S(2)}) collective-permute-start(bf16[2,2,128,128]{3,2,1,0:T(8,128)(2,1)S(1)} %get-tuple-element.74), channel_id=1, source_target_pairs={{0,64},{32,96},{64,0},{96,32},{1,65},{33,97},{65,1},{97,33},{2,66}... | collective-permute-start | bytes 393224 | tf_op jit(solution)/shard_map/ppermute | solution.py:313
  96.4 14.1 %collective-permute-start.21 = (bf16[2,2,128,128]{3,2,1,0:T(8,128)(2,1)S(1)}, bf16[2,2,128,128]{3,2,1,0:T(8,128)(2,1)S(1)}, u32[]{:S(2)}, u32[]{:S(2)}) collective-permute-start(bf16[2,2,128,128]{3,2,1,0:T(8,128)(2,1)S(1)} %get-tuple-element.73), channel_id=1, source_target_pairs={{0,96},{32,0},{64,32},{96,64},{1,97},{33,1},{65,33},{97,65},{2,98}... | collective-permute-start | bytes 393224 | tf_op jit(solution)/shard_map/ppermute | solution.py:313
  100.4 12.4 %collective-permute-start.26 = (bf16[2,2,128,128]{3,2,1,0:T(8,128)(2,1)S(1)}, bf16[2,2,128,128]{3,2,1,0:T(8,128)(2,1)S(1)}, u32[]{:S(2)}, u32[]{:S(2)}) collective-permute-start(bf16[2,2,128,128]{3,2,1,0:T(8,128)(2,1)S(1)} %add_convert_fusion.1), channel_id=1, source_target_pairs={{0,0},{1,1},{2,16},{3,17},{16,2},{17,3},{18,18},{19,19},{4,4},{5,5... | collective-permute-start | bytes 393224 | tf_op jit(solution)/shard_map/ppermute | solution.py:348
  112.9 7.1 %collective-permute-start.27 = (bf16[2,2,128,128]{3,2,1,0:T(8,128)(2,1)S(1)}, bf16[2,2,128,128]{3,2,1,0:T(8,128)(2,1)S(1)}, u32[]{:S(2)}, u32[]{:S(2)}) collective-permute-start(bf16[2,2,128,128]{3,2,1,0:T(8,128)(2,1)S(1)} %add_convert_fusion), channel_id=1, source_target_pairs={{0,1},{1,0},{2,17},{3,16},{16,3},{17,2},{18,19},{19,18},{4,5},{5,4... | collective-permute-start | bytes 393224 | tf_op jit(solution)/shard_map/ppermute | solution.py:348

commit v5 on v4

--- a/solution.py
+++ b/solution.py
@@ -17,7 +17,7 @@
     return [(i, (i + step) % size) for i in range(size)]
 
 
-def products_kernel(late, terms, pos, allowed, units, *refs):
+def products_kernel(late, terms, allowed, units, *refs):
     half = terms // 2
     pieces = 5 if late else 3
     lefts, refs = refs[:pieces], refs[pieces:]
@@ -29,7 +29,7 @@
     if not late:
         wave_out, *refs = refs
     ls, rs, w, t, sums, lists, counts, seen, started, sems, out_sems = refs
-    y, z, x, c = pos[0], pos[1], pos[2], pos[3]
+    y, z, x, c = (lax.axis_index(name) for name in ("y", "z", "x", "core"))
     whole = []
 
     def fetch(src, dst, sem):
@@ -231,18 +231,18 @@
         passed.wait()
 
 
-def products(pos, allowed, units, lefts, rights, wave, before=()):
+def products(allowed, units, lefts, rights, wave, before=()):
     terms = lefts[0].shape[0]
     smem = pl.BlockSpec(memory_space=pltpu.SMEM)
     hbm = pl.BlockSpec(memory_space=pl.ANY)
     out = jax.ShapeDtypeStruct((4, 2, 2, B, B), jnp.bfloat16)
     masked = jax.ShapeDtypeStruct((8, 8, B, B), jnp.bfloat16)
     late = bool(before)
-    n_in = 3 + 2 * len(lefts) + len(wave)
+    n_in = 2 + 2 * len(lefts) + len(wave)
     return pl.pallas_call(
         functools.partial(products_kernel, late, terms),
         out_shape=(out,) * 4 if late else (out,) * 4 + (masked,),
-        in_specs=[smem] * 3 + [hbm] * (n_in - 3 + len(before)),
+        in_specs=[smem] * 2 + [hbm] * (n_in - 2 + len(before)),
         out_specs=(hbm,) * (4 if late else 5),
         input_output_aliases={n_in + at: at for at in range(len(before))},
         scratch_shapes=[
@@ -262,7 +262,7 @@
         cost_estimate=pl.CostEstimate(
             flops=32 * terms * 4 * B**3, bytes_accessed=14 * 2**20, transcendentals=0
         ),
-    )(pos, allowed, units, *lefts, *rights, *wave, *before)
+    )(allowed, units, *lefts, *rights, *wave, *before)
 
 
 def ring_near(own, axis):
@@ -328,12 +328,11 @@
     row, *near_l = lax.optimization_barrier((row, *near_l))
     wave = share_wave(row)
     lefts, rights = (left_operator, *near_l), (right_operator, *near_r)
-    pos = jnp.stack([y, z, x, c]).astype(jnp.int32)
     far_l, far_r = far_half(near_l), far_half(near_r)
-    *sums, masked = products(pos, allowed, block_units, lefts, rights, wave)
+    *sums, masked = products(allowed, block_units, lefts, rights, wave)
     lefts = (*lefts, *ring_far(far_l, "y"))
     rights = (*rights, *ring_far(far_r, "z"))
-    sums = products(pos, allowed, block_units, lefts, rights, (masked,), sums)
+    sums = products(allowed, block_units, lefts, rights, (masked,), sums)
     halves = [add_cores(sums[s], sums[2 + s]) for s in range(2)]
     halves = [(own, add_send(chips)) for own, chips in halves]
 

time: 121 us -> 120 us (level)
  starting transfers between devices: 46 us -> 44.6 us
    ppermute x2, starting transfers between devices: 13.8 us -> 11.5 us  [shards(): got.append(lax.ppermute(add_chips(*half), ('core', 'z'), perm))]
  transfers between devices with their start and end apart: 28 -> 28, of which waited for: 9 -> 10; matrix products, arithmetic and copies ran while one was open for 3% -> 2% of each run, Pallas kernels for 14% -> 14%
where the time goes in v5:
time: 120 us
  starting transfers between devices  44.6 us (37%)
  waiting for transfers between devices  39.3 us (33%)
  Pallas kernels  30 us (25%)
  other arithmetic  3.4 us (3%)
  local copies, waits for them, and re-layouts  2.17 us (2%)
    pallas_call x2, Pallas kernels, products(): pl.pallas_call(functools.partial(products_kernel, late, terms), out_shape...  30 us
    ppermute x3, waiting for transfers between devices, gather_wave(): row = [mine] + [lax.ppermute(mine, 'x', shifted(4, d)) for d in (1, 2, 3)]  17.8 us
    ppermute x2, starting transfers between devices, shards(): got.append(lax.ppermute(add_chips(*half), ('core', 'z'), perm))  11.5 us
    ppermute x2, waiting for transfers between devices, ring_near(): lax.ppermute(own, axis, shifted(4, 1))  8.51 us
    ppermute x4, starting transfers between devices, share_wave(): return (*row, *(lax.ppermute(part, 'core', swapped(2, 1)) for part in row))  6.92 us
    ppermute x6, starting transfers between devices, add_send(): lax.ppermute(part, 'x', shifted(4, d + 1))  6.04 us
    ppermute x2, starting transfers between devices, ring_far(): lax.ppermute(halves[1], axis, shifted(4, -1))  5.39 us
    ppermute x2, starting transfers between devices, ring_near(): lax.ppermute(own, axis, shifted(4, -1))  4.53 us
  transfers between devices with their start and end apart: 28, of which 10 were waited for; matrix products, arithmetic and copies ran while one was open for 2% of the time, Pallas kernels for 14%

profile of v5, /device:TPU:7, one launch (start us, length us, event | category | flops | bytes accessed | tf_op | source)
XLA Modules:
  0.0 119.7 jit_solution(6148958085363303428)
XLA Ops:
  0.0 1.0 dynamic-slice_bitcast_fusion
  1.0 1.4 %collective-permute-start = (bf16[2,128,128]{2,1,0:T(8,128)(2,1)S(1)}, bf16[2,128,128]{2,1,0:T(8,128)(2,1)S(1)}, u32[]{:S(2)}, u32[]{:S(2)}) collective-permute-start(bf16[2,128,128]{2,1,0:T(8,128)(2,1)S(1)} %get-tuple-element.67), channel_id=1, source_target_pairs={{0,4},{4,8},{8,12},{12,0},{1,5},{5,9},{9,13},{13,1},{2,6},{6,10},{... | collective-permute-start | bytes 196616 | tf_op jit(solution)/shard_map/ppermute | solution.py:292
  2.3 1.5 %collective-permute-start.1 = (bf16[2,128,128]{2,1,0:T(8,128)(2,1)S(1)}, bf16[2,128,128]{2,1,0:T(8,128)(2,1)S(1)}, u32[]{:S(2)}, u32[]{:S(2)}) collective-permute-start(bf16[2,128,128]{2,1,0:T(8,128)(2,1)S(1)} %get-tuple-element.66), channel_id=1, source_target_pairs={{0,12},{4,0},{8,4},{12,8},{1,13},{5,1},{9,5},{13,9},{2,14},{6,2},{... | collective-permute-start | bytes 196616 | tf_op jit(solution)/shard_map/ppermute | solution.py:292
  3.8 1.6 %collective-permute-start.2 = (bf16[2,128,128]{2,1,0:T(8,128)(2,1)S(1)}, bf16[2,128,128]{2,1,0:T(8,128)(2,1)S(1)}, u32[]{:S(2)}, u32[]{:S(2)}) collective-permute-start(bf16[2,128,128]{2,1,0:T(8,128)(2,1)S(1)} %get-tuple-element.68), channel_id=1, source_target_pairs={{0,8},{4,12},{8,0},{12,4},{1,9},{5,13},{9,1},{13,5},{2,10},{6,14},... | collective-permute-start | bytes 196616 | tf_op jit(solution)/shard_map/ppermute | solution.py:292
  5.4 3.0 %collective-permute-done.2 = bf16[2,128,128]{2,1,0:T(8,128)(2,1)S(1)} collective-permute-done((bf16[2,128,128]{2,1,0:T(8,128)(2,1)S(1)}, bf16[2,128,128]{2,1,0:T(8,128)(2,1)S(1)}, u32[]{:S(2)}, u32[]{:S(2)}) %collective-permute-start.2) | collective-permute-done | bytes 65568 | tf_op jit(solution)/shard_map/ppermute | solution.py:292
  8.5 0.3 collective-permute-start.6
  8.7 2.4 %collective-permute-start.7 = (bf16[24,2,128,128]{3,2,1,0:T(8,128)(2,1)}, bf16[24,2,128,128]{3,2,1,0:T(8,128)(2,1)S(1)}, u32[]{:S(2)}, u32[]{:S(2)}) collective-permute-start(bf16[24,2,128,128]{3,2,1,0:T(8,128)(2,1)} %refs_0_.1), channel_id=1, source_target_pairs={{0,12},{4,0},{8,4},{12,8},{1,13},{5,1},{9,5},{13,9},{2,14},{6,2},{... | collective-permute-start | bytes 4718600 | tf_op jit(solution)/shard_map/ppermute | solution.py:269
  11.1 1.6 %collective-permute-start.10 = (bf16[24,2,128,128]{3,2,1,0:T(8,128)(2,1)}, bf16[24,2,128,128]{3,2,1,0:T(8,128)(2,1)S(1)}, u32[]{:S(2)}, u32[]{:S(2)}) collective-permute-start(bf16[24,2,128,128]{3,2,1,0:T(8,128)(2,1)} %refs_5_), channel_id=1, source_target_pairs={{0,1},{1,2},{2,3},{3,0},{4,5},{5,6},{6,7},{7,4},{8,9},{9,10},{10,1... | collective-permute-start | bytes 4718600 | tf_op jit(solution)/shard_map/ppermute | solution.py:269
  12.8 2.1 %collective-permute-start.11 = (bf16[24,2,128,128]{3,2,1,0:T(8,128)(2,1)}, bf16[24,2,128,128]{3,2,1,0:T(8,128)(2,1)S(1)}, u32[]{:S(2)}, u32[]{:S(2)}) collective-permute-start(bf16[24,2,128,128]{3,2,1,0:T(8,128)(2,1)} %refs_5_), channel_id=1, source_target_pairs={{0,3},{1,0},{2,1},{3,2},{4,7},{5,4},{6,5},{7,6},{8,11},{9,8},{10,9... | collective-permute-start | bytes 4718600 | tf_op jit(solution)/shard_map/ppermute | solution.py:269
  15.0 0.3 collective-permute-start.3
  15.2 5.3 %collective-permute-done.3.refs_7_ = bf16[8,128,128]{2,1,0:T(8,128)(2,1)S(1)} collective-permute-done((bf16[8,128,128]{2,1,0:T(8,128)(2,1)S(1)}, bf16[8,128,128]{2,1,0:T(8,128)(2,1)S(1)}, u32[]{:S(2)}, u32[]{:S(2)}) %collective-permute-start.3) | collective-permute-done | bytes 262176 | tf_op jit(solution)/shard_map/ppermute | solution.py:298
  20.5 1.1 collective-permute-start.4
  21.7 5.6 %collective-permute-done.4.refs_8_ = bf16[8,128,128]{2,1,0:T(8,128)(2,1)S(1)} collective-permute-done((bf16[8,128,128]{2,1,0:T(8,128)(2,1)S(1)}, bf16[8,128,128]{2,1,0:T(8,128)(2,1)S(1)}, u32[]{:S(2)}, u32[]{:S(2)}) %collective-permute-start.4) | collective-permute-done | bytes 262176 | tf_op jit(solution)/shard_map/ppermute | solution.py:298
  27.3 0.8 collective-permute-start.5
  28.1 6.9 %collective-permute-done.5.refs_9_ = bf16[8,128,128]{2,1,0:T(8,128)(2,1)S(1)} collective-permute-done((bf16[8,128,128]{2,1,0:T(8,128)(2,1)S(1)}, bf16[8,128,128]{2,1,0:T(8,128)(2,1)S(1)}, u32[]{:S(2)}, u32[]{:S(2)}) %collective-permute-start.5) | collective-permute-done | bytes 262176 | tf_op jit(solution)/shard_map/ppermute | solution.py:298
  35.0 8.5 %collective-permute-done.6.refs_1_ = bf16[24,2,128,128]{3,2,1,0:T(8,128)(2,1)S(1)} collective-permute-done((bf16[24,2,128,128]{3,2,1,0:T(8,128)(2,1)}, bf16[24,2,128,128]{3,2,1,0:T(8,128)(2,1)S(1)}, u32[]{:S(2)}, u32[]{:S(2)}) %collective-permute-start.6) | collective-permute-done | bytes 1572896 | tf_op jit(solution)/shard_map/ppermute | solution.py:269
  43.5 3.2 %collective-permute-start.14 = (bf16[8,128,128]{2,1,0:T(8,128)(2,1)S(1)}, bf16[8,128,128]{2,1,0:T(8,128)(2,1)}, u32[]{:S(2)}, u32[]{:S(2)}) collective-permute-start(bf16[8,128,128]{2,1,0:T(8,128)(2,1)S(1)} %pad_maximum_fusion.refs_6_), channel_id=1, source_target_pairs={{0,16},{16,0},{1,17},{17,1},{2,18},{18,2},{3,19},{19,3},{4,20},{20... | collective-permute-start | bytes 786440 | tf_op jit(solution)/shard_map/ppermute | solution.py:303
  46.8 0.1 collective-permute-start.15
  46.9 0.4 collective-permute-start.16
  47.3 3.2 %collective-permute-start.17 = (bf16[8,128,128]{2,1,0:T(8,128)(2,1)S(1)}, bf16[8,128,128]{2,1,0:T(8,128)(2,1)}, u32[]{:S(2)}, u32[]{:S(2)}) collective-permute-start(bf16[8,128,128]{2,1,0:T(8,128)(2,1)S(1)} %collective-permute-done.5.refs_9_), channel_id=1, source_target_pairs={{0,16},{16,0},{1,17},{17,1},{2,18},{18,2},{3,19},{19,3},{4,20},{20... | collective-permute-start | bytes 786440 | tf_op jit(solution)/shard_map/ppermute | solution.py:303
  50.7 0.1 collective-permute-start.8
  50.9 2.7 %collective-permute-start.9 = (bf16[12,2,128,128]{3,2,1,0:T(8,128)(2,1)S(1)}, bf16[12,2,128,128]{3,2,1,0:T(8,128)(2,1)S(1)}, u32[]{:S(2)}, u32[]{:S(2)}) collective-permute-start(bf16[12,2,128,128]{3,2,1,0:T(8,128)(2,1)S(1)} %slice.61), channel_id=1, source_target_pairs={{0,12},{4,0},{8,4},{12,8},{1,13},{5,1},{9,5},{13,9},{2,14},{6,2},{... | collective-permute-start | bytes 2359304 | tf_op jit(solution)/shard_map/ppermute | solution.py:280
  53.7 2.7 %collective-permute-start.13 = (bf16[12,2,128,128]{3,2,1,0:T(8,128)(2,1)S(1)}, bf16[12,2,128,128]{3,2,1,0:T(8,128)(2,1)}, u32[]{:S(2)}, u32[]{:S(2)}) collective-permute-start(bf16[12,2,128,128]{3,2,1,0:T(8,128)(2,1)S(1)} %slice.81), channel_id=1, source_target_pairs={{0,3},{1,0},{2,1},{3,2},{4,7},{5,4},{6,5},{7,6},{8,11},{9,8},{10,9... | collective-permute-start | bytes 2359304 | tf_op jit(solution)/shard_map/ppermute | solution.py:280
  56.4 16.2 %shard_map.55 = (bf16[4,2,2,128,128]{4,3,2,1,0:T(8,128)(2,1)}, bf16[4,2,2,128,128]{4,3,2,1,0:T(8,128)(2,1)}, bf16[4,2,2,128,128]{4,3,2,1,0:T(8,128)(2,1)}, bf16[...) custom-call(s32[32,32]{1,0:T(8,128)} %allowed.3, s32[32]{0:T(128)} %units.3, bf16[24,2,128,128]{3,2,1,0:T(8,128)(2,1)} %refs_0_.1, ...), custom_call_target="tpu_custom_call" | custom-call | flops 6442450944 | bytes 14680064 | tf_op jit(solution)/shard_map/pallas_call | solution.py:242
  72.6 0.7 collective-permute-done.12.refs_8_
  73.4 0.1 copy-done.6
  73.5 0.3 copy-done.7
  73.8 0.5 copy-done.8
  74.3 13.8 %shard_map.56 = (bf16[4,2,2,128,128]{4,3,2,1,0:T(8,128)(2,1)}, bf16[4,2,2,128,128]{4,3,2,1,0:T(8,128)(2,1)}, bf16[4,2,2,128,128]{4,3,2,1,0:T(8,128)(2,1)}, bf16[4,2,2,128,128]{4,3,2,1,0:T(8,128)(2,1)}) custom-call(s32[32,32]{1,0:T(8,128)} %allowed.3, s32[32]{0:T(128)} %units.3, ...), custom_call_target="tpu_custom_call", output_to_operand_aliasing={{0}: (13, {}), {1}: (14, {}), {2}: (15, {}), {3}: (16, {})} | custom-call | flops 6442450944 | bytes 14680064 | tf_op jit(solution)/shard_map/pallas_call | solution.py:242
  88.0 1.5 %collective-permute-start.22 = (bf16[4,2,2,128,128]{4,3,2,1,0:T(8,128)(2,1)}, bf16[4,2,2,128,128]{4,3,2,1,0:T(8,128)(2,1)S(1)}, u32[]{:S(2)}, u32[]{:S(2)}) collective-permute-start(bf16[4,2,2,128,128]{4,3,2,1,0:T(8,128)(2,1)} %get-tuple-element.55), channel_id=1, source_target_pairs={{0,16},{16,0},{1,17},{17,1},{2,18},{18,2},{3,19},{19,3},{4,20},{20... | collective-permute-start | bytes 1572872 | tf_op jit(solution)/shard_map/ppermute | solution.py:307
  89.5 0.1 collective-permute-start.18
  89.6 0.1 iota_compare_fusion
  89.7 1.6 %collective-permute-done.22 = bf16[4,2,2,128,128]{4,3,2,1,0:T(8,128)(2,1)S(1)} collective-permute-done((bf16[4,2,2,128,128]{4,3,2,1,0:T(8,128)(2,1)}, bf16[4,2,2,128,128]{4,3,2,1,0:T(8,128)(2,1)S(1)}, u32[]{:S(2)}, u32[]{:S(2)}) %collective-permute-start.22) | collective-permute-done | bytes 524320 | tf_op jit(solution)/shard_map/ppermute | solution.py:307
  91.3 1.2 %fusion.5 = (bf16[2,2,128,128]{3,2,1,0:T(8,128)(2,1)S(1)}, bf16[2,2,128,128]{3,2,1,0:T(8,128)(2,1)S(1)}, bf16[2,2,128,128]{3,2,1,0:T(8,128)(2,1)S(1)}, f32[2,2,128,128]{3,2,1,0:T(8,128)S(1)}) fusion(bf16[4,2,2,128,128]{4,3,2,1,0:T(8,128)(2,1)S(1)} %collective-permute-done.22, bf16[4,2,2,128,128]{4,3,2,1,0:T(8,128)(2,1)} %get-tuple-element.54), kind=kLoop, calls=%fused_computation.17 | loop fusion | flops 983040 | bytes 1703936 | tf_op jit(solution)/shard_map/convert_element_type | solution.py:309
  92.5 0.3 collective-permute-start.23
  92.8 2.1 %collective-permute-start.24 = (bf16[2,2,128,128]{3,2,1,0:T(8,128)(2,1)S(1)}, bf16[2,2,128,128]{3,2,1,0:T(8,128)(2,1)S(1)}, u32[]{:S(2)}, u32[]{:S(2)}) collective-permute-start(bf16[2,2,128,128]{3,2,1,0:T(8,128)(2,1)S(1)} %get-tuple-element.70), channel_id=1, source_target_pairs={{0,64},{32,96},{64,0},{96,32},{1,65},{33,97},{65,1},{97,33},{2,66}... | collective-permute-start | bytes 393224 | tf_op jit(solution)/shard_map/ppermute | solution.py:313
  95.0 0.1 fusion.2
  95.1 2.7 %collective-permute-start.19 = (bf16[2,2,128,128]{3,2,1,0:T(8,128)(2,1)S(1)}, bf16[2,2,128,128]{3,2,1,0:T(8,128)(2,1)S(1)}, u32[]{:S(2)}, u32[]{:S(2)}) collective-permute-start(bf16[2,2,128,128]{3,2,1,0:T(8,128)(2,1)S(1)} %get-tuple-element.75), channel_id=1, source_target_pairs={{0,32},{32,64},{64,96},{96,0},{1,33},{33,65},{65,97},{97,1},{2,34}... | collective-permute-start | bytes 393224 | tf_op jit(solution)/shard_map/ppermute | solution.py:313
  97.8 0.1 collective-permute-start.20
  98.0 0.8 collective-permute-start.21
  98.7 3.1 %collective-permute-done.25 = bf16[2,2,128,128]{3,2,1,0:T(8,128)(2,1)S(1)} collective-permute-done((bf16[2,2,128,128]{3,2,1,0:T(8,128)(2,1)S(1)}, bf16[2,2,128,128]{3,2,1,0:T(8,128)(2,1)S(1)}, u32[]{:S(2)}, u32[]{:S(2)}) %collective-permute-start.25) | collective-permute-done | bytes 131104 | tf_op jit(solution)/shard_map/ppermute | solution.py:313
  101.9 6.2 %collective-permute-start.26 = (bf16[2,2,128,128]{3,2,1,0:T(8,128)(2,1)S(1)}, bf16[2,2,128,128]{3,2,1,0:T(8,128)(2,1)S(1)}, u32[]{:S(2)}, u32[]{:S(2)}) collective-permute-start(bf16[2,2,128,128]{3,2,1,0:T(8,128)(2,1)S(1)} %add_convert_fusion.1), channel_id=1, source_target_pairs={{0,0},{1,1},{2,16},{3,17},{16,2},{17,3},{18,18},{19,19},{4,4},{5,5... | collective-permute-start | bytes 393224 | tf_op jit(solution)/shard_map/ppermute | solution.py:347
  108.1 0.8 dynamic-slice_compare_fusion
  109.0 1.8 %collective-permute-done.26 = bf16[2,2,128,128]{3,2,1,0:T(8,128)(2,1)S(1)} collective-permute-done((bf16[2,2,128,128]{3,2,1,0:T(8,128)(2,1)S(1)}, bf16[2,2,128,128]{3,2,1,0:T(8,128)(2,1)S(1)}, u32[]{:S(2)}, u32[]{:S(2)}) %collective-permute-start.26) | collective-permute-done | bytes 131104 | tf_op jit(solution)/shard_map/ppermute | solution.py:347
  110.9 5.3 %collective-permute-start.27 = (bf16[2,2,128,128]{3,2,1,0:T(8,128)(2,1)S(1)}, bf16[2,2,128,128]{3,2,1,0:T(8,128)(2,1)S(1)}, u32[]{:S(2)}, u32[]{:S(2)}) collective-permute-start(bf16[2,2,128,128]{3,2,1,0:T(8,128)(2,1)S(1)} %add_convert_fusion), channel_id=1, source_target_pairs={{0,1},{1,0},{2,17},{3,16},{16,3},{17,2},{18,19},{19,18},{4,5},{5,4... | collective-permute-start | bytes 393224 | tf_op jit(solution)/shard_map/ppermute | solution.py:347
  116.1 0.1 broadcast_and_fusion
  116.2 2.6 %collective-permute-done.27 = bf16[2,2,128,128]{3,2,1,0:T(8,128)(2,1)S(1)} collective-permute-done((bf16[2,2,128,128]{3,2,1,0:T(8,128)(2,1)S(1)}, bf16[2,2,128,128]{3,2,1,0:T(8,128)(2,1)S(1)}, u32[]{:S(2)}, u32[]{:S(2)}) %collective-permute-start.27) | collective-permute-done | bytes 131104 | tf_op jit(solution)/shard_map/ppermute | solution.py:347
  118.8 0.9 and_select_fusion
  (56 shorter events, 0.6 us)
Async XLA Ops:
  1.0 4.5 %collective-permute-start = (bf16[2,128,128]{2,1,0:T(8,128)(2,1)S(1)}, bf16[2,128,128]{2,1,0:T(8,128)(2,1)S(1)}, u32[]{:S(2)}, u32[]{:S(2)}) collective-permute-start(bf16[2,128,128]{2,1,0:T(8,128)(2,1)S(1)} %get-tuple-element.67), channel_id=1, source_target_pairs={{0,4},{4,8},{8,12},{12,0},{1,5},{5,9},{9,13},{13,1},{2,6},{6,10},{... | collective-permute-start | bytes 196616 | tf_op jit(solution)/shard_map/ppermute | solution.py:292
  2.3 3.1 %collective-permute-start.1 = (bf16[2,128,128]{2,1,0:T(8,128)(2,1)S(1)}, bf16[2,128,128]{2,1,0:T(8,128)(2,1)S(1)}, u32[]{:S(2)}, u32[]{:S(2)}) collective-permute-start(bf16[2,128,128]{2,1,0:T(8,128)(2,1)S(1)} %get-tuple-element.66), channel_id=1, source_target_pairs={{0,12},{4,0},{8,4},{12,8},{1,13},{5,1},{9,5},{13,9},{2,14},{6,2},{... | collective-permute-start | bytes 196616 | tf_op jit(solution)/shard_map/ppermute | solution.py:292
  3.8 4.6 %collective-permute-start.2 = (bf16[2,128,128]{2,1,0:T(8,128)(2,1)S(1)}, bf16[2,128,128]{2,1,0:T(8,128)(2,1)S(1)}, u32[]{:S(2)}, u32[]{:S(2)}) collective-permute-start(bf16[2,128,128]{2,1,0:T(8,128)(2,1)S(1)} %get-tuple-element.68), channel_id=1, source_target_pairs={{0,8},{4,12},{8,0},{12,4},{1,9},{5,13},{9,1},{13,5},{2,10},{6,14},... | collective-permute-start | bytes 196616 | tf_op jit(solution)/shard_map/ppermute | solution.py:292
  8.5 35.1 %collective-permute-start.6 = (bf16[24,2,128,128]{3,2,1,0:T(8,128)(2,1)}, bf16[24,2,128,128]{3,2,1,0:T(8,128)(2,1)S(1)}, u32[]{:S(2)}, u32[]{:S(2)}) collective-permute-start(bf16[24,2,128,128]{3,2,1,0:T(8,128)(2,1)} %refs_0_.1), channel_id=1, source_target_pairs={{0,4},{4,8},{8,12},{12,0},{1,5},{5,9},{9,13},{13,1},{2,6},{6,10},{... | collective-permute-start | bytes 4718600 | tf_op jit(solution)/shard_map/ppermute | solution.py:269
  8.7 34.8 %collective-permute-start.7 = (bf16[24,2,128,128]{3,2,1,0:T(8,128)(2,1)}, bf16[24,2,128,128]{3,2,1,0:T(8,128)(2,1)S(1)}, u32[]{:S(2)}, u32[]{:S(2)}) collective-permute-start(bf16[24,2,128,128]{3,2,1,0:T(8,128)(2,1)} %refs_0_.1), channel_id=1, source_target_pairs={{0,12},{4,0},{8,4},{12,8},{1,13},{5,1},{9,5},{13,9},{2,14},{6,2},{... | collective-permute-start | bytes 4718600 | tf_op jit(solution)/shard_map/ppermute | solution.py:269
  11.1 36.1 %collective-permute-start.10 = (bf16[24,2,128,128]{3,2,1,0:T(8,128)(2,1)}, bf16[24,2,128,128]{3,2,1,0:T(8,128)(2,1)S(1)}, u32[]{:S(2)}, u32[]{:S(2)}) collective-permute-start(bf16[24,2,128,128]{3,2,1,0:T(8,128)(2,1)} %refs_5_), channel_id=1, source_target_pairs={{0,1},{1,2},{2,3},{3,0},{4,5},{5,6},{6,7},{7,4},{8,9},{9,10},{10,1... | collective-permute-start | bytes 4718600 | tf_op jit(solution)/shard_map/ppermute | solution.py:269
  12.8 37.9 %collective-permute-start.11 = (bf16[24,2,128,128]{3,2,1,0:T(8,128)(2,1)}, bf16[24,2,128,128]{3,2,1,0:T(8,128)(2,1)S(1)}, u32[]{:S(2)}, u32[]{:S(2)}) collective-permute-start(bf16[24,2,128,128]{3,2,1,0:T(8,128)(2,1)} %refs_5_), channel_id=1, source_target_pairs={{0,3},{1,0},{2,1},{3,2},{4,7},{5,4},{6,5},{7,6},{8,11},{9,8},{10,9... | collective-permute-start | bytes 4718600 | tf_op jit(solution)/shard_map/ppermute | solution.py:269
  14.9 41.4 %copy-start.5 = (bf16[8,128,128]{2,1,0:T(8,128)(2,1)}, bf16[8,128,128]{2,1,0:T(8,128)(2,1)S(1)}, u32[]{:S(2)}) copy-start(bf16[8,128,128]{2,1,0:T(8,128)(2,1)S(1)} %pad_maximum_fusion.refs_6_) | copy-start | bytes 786436
  15.0 5.6 %collective-permute-start.3 = (bf16[8,128,128]{2,1,0:T(8,128)(2,1)S(1)}, bf16[8,128,128]{2,1,0:T(8,128)(2,1)S(1)}, u32[]{:S(2)}, u32[]{:S(2)}) collective-permute-start(bf16[8,128,128]{2,1,0:T(8,128)(2,1)S(1)} %pad_maximum_fusion.refs_6_), channel_id=1, source_target_pairs={{0,32},{32,64},{64,96},{96,0},{1,33},{33,65},{65,97},{97,1},{2,34}... | collective-permute-start | bytes 786440 | tf_op jit(solution)/shard_map/ppermute | solution.py:298
  20.5 35.8 %copy-start.9 = (bf16[8,128,128]{2,1,0:T(8,128)(2,1)}, bf16[8,128,128]{2,1,0:T(8,128)(2,1)S(1)}, u32[]{:S(2)}) copy-start(bf16[8,128,128]{2,1,0:T(8,128)(2,1)S(1)} %collective-permute-done.3.refs_7_) | copy-start | bytes 786436
  20.5 6.7 %collective-permute-start.4 = (bf16[8,128,128]{2,1,0:T(8,128)(2,1)S(1)}, bf16[8,128,128]{2,1,0:T(8,128)(2,1)S(1)}, u32[]{:S(2)}, u32[]{:S(2)}) collective-permute-start(bf16[8,128,128]{2,1,0:T(8,128)(2,1)S(1)} %pad_maximum_fusion.refs_6_), channel_id=1, source_target_pairs={{0,64},{32,96},{64,0},{96,32},{1,65},{33,97},{65,1},{97,33},{2,66}... | collective-permute-start | bytes 786440 | tf_op jit(solution)/shard_map/ppermute | solution.py:298
  27.3 29.0 %copy-start.10 = (bf16[8,128,128]{2,1,0:T(8,128)(2,1)}, bf16[8,128,128]{2,1,0:T(8,128)(2,1)S(1)}, u32[]{:S(2)}) copy-start(bf16[8,128,128]{2,1,0:T(8,128)(2,1)S(1)} %collective-permute-done.4.refs_8_) | copy-start | bytes 786436
  27.3 7.7 %collective-permute-start.5 = (bf16[8,128,128]{2,1,0:T(8,128)(2,1)S(1)}, bf16[8,128,128]{2,1,0:T(8,128)(2,1)S(1)}, u32[]{:S(2)}, u32[]{:S(2)}) collective-permute-start(bf16[8,128,128]{2,1,0:T(8,128)(2,1)S(1)} %pad_maximum_fusion.refs_6_), channel_id=1, source_target_pairs={{0,96},{32,0},{64,32},{96,64},{1,97},{33,1},{65,33},{97,65},{2,98}... | collective-permute-start | bytes 786440 | tf_op jit(solution)/shard_map/ppermute | solution.py:298
  35.0 21.3 %copy-start.11 = (bf16[8,128,128]{2,1,0:T(8,128)(2,1)}, bf16[8,128,128]{2,1,0:T(8,128)(2,1)S(1)}, u32[]{:S(2)}) copy-start(bf16[8,128,128]{2,1,0:T(8,128)(2,1)S(1)} %collective-permute-done.5.refs_9_) | copy-start | bytes 786436
  43.5 7.1 %copy-start.1 = (bf16[24,2,128,128]{3,2,1,0:T(8,128)(2,1)}, bf16[24,2,128,128]{3,2,1,0:T(8,128)(2,1)S(1)}, u32[]{:S(2)}) copy-start(bf16[24,2,128,128]{3,2,1,0:T(8,128)(2,1)S(1)} %collective-permute-done.6.refs_1_) | copy-start | bytes 4718596
  43.5 7.1 %copy-start.2 = (bf16[24,2,128,128]{3,2,1,0:T(8,128)(2,1)}, bf16[24,2,128,128]{3,2,1,0:T(8,128)(2,1)S(1)}, u32[]{:S(2)}) copy-start(bf16[24,2,128,128]{3,2,1,0:T(8,128)(2,1)S(1)} %collective-permute-done.7.refs_2_) | copy-start | bytes 4718596
  43.5 7.4 %collective-permute-start.14 = (bf16[8,128,128]{2,1,0:T(8,128)(2,1)S(1)}, bf16[8,128,128]{2,1,0:T(8,128)(2,1)}, u32[]{:S(2)}, u32[]{:S(2)}) collective-permute-start(bf16[8,128,128]{2,1,0:T(8,128)(2,1)S(1)} %pad_maximum_fusion.refs_6_), channel_id=1, source_target_pairs={{0,16},{16,0},{1,17},{17,1},{2,18},{18,2},{3,19},{19,3},{4,20},{20... | collective-permute-start | bytes 786440 | tf_op jit(solution)/shard_map/ppermute | solution.py:303
  46.8 6.9 %collective-permute-start.15 = (bf16[8,128,128]{2,1,0:T(8,128)(2,1)S(1)}, bf16[8,128,128]{2,1,0:T(8,128)(2,1)}, u32[]{:S(2)}, u32[]{:S(2)}) collective-permute-start(bf16[8,128,128]{2,1,0:T(8,128)(2,1)S(1)} %collective-permute-done.3.refs_7_), channel_id=1, source_target_pairs={{0,16},{16,0},{1,17},{17,1},{2,18},{18,2},{3,19},{19,3},{4,20},{20... | collective-permute-start | bytes 786440 | tf_op jit(solution)/shard_map/ppermute | solution.py:303
  46.9 6.8 %collective-permute-start.16 = (bf16[8,128,128]{2,1,0:T(8,128)(2,1)S(1)}, bf16[8,128,128]{2,1,0:T(8,128)(2,1)S(1)}, u32[]{:S(2)}, u32[]{:S(2)}) collective-permute-start(bf16[8,128,128]{2,1,0:T(8,128)(2,1)S(1)} %collective-permute-done.4.refs_8_), channel_id=1, source_target_pairs={{0,16},{16,0},{1,17},{17,1},{2,18},{18,2},{3,19},{19,3},{4,20},{20... | collective-permute-start | bytes 786440 | tf_op jit(solution)/shard_map/ppermute | solution.py:303
  47.3 9.0 %copy-start.3 = (bf16[24,2,128,128]{3,2,1,0:T(8,128)(2,1)}, bf16[24,2,128,128]{3,2,1,0:T(8,128)(2,1)S(1)}, u32[]{:S(2)}) copy-start(bf16[24,2,128,128]{3,2,1,0:T(8,128)(2,1)S(1)} %collective-permute-done.10.refs_4_.refs_6_) | copy-start | bytes 4718596
  47.3 9.0 %collective-permute-start.17 = (bf16[8,128,128]{2,1,0:T(8,128)(2,1)S(1)}, bf16[8,128,128]{2,1,0:T(8,128)(2,1)}, u32[]{:S(2)}, u32[]{:S(2)}) collective-permute-start(bf16[8,128,128]{2,1,0:T(8,128)(2,1)S(1)} %collective-permute-done.5.refs_9_), channel_id=1, source_target_pairs={{0,16},{16,0},{1,17},{17,1},{2,18},{18,2},{3,19},{19,3},{4,20},{20... | collective-permute-start | bytes 786440 | tf_op jit(solution)/shard_map/ppermute | solution.py:303
  50.7 5.6 %copy-start.4 = (bf16[24,2,128,128]{3,2,1,0:T(8,128)(2,1)}, bf16[24,2,128,128]{3,2,1,0:T(8,128)(2,1)S(1)}, u32[]{:S(2)}) copy-start(bf16[24,2,128,128]{3,2,1,0:T(8,128)(2,1)S(1)} %collective-permute-done.11.refs_5_.refs_7_) | copy-start | bytes 4718596
  50.7 21.9 %collective-permute-start.8 = (bf16[12,2,128,128]{3,2,1,0:T(8,128)(2,1)S(1)}, bf16[12,2,128,128]{3,2,1,0:T(8,128)(2,1)S(1)}, u32[]{:S(2)}, u32[]{:S(2)}) collective-permute-start(bf16[12,2,128,128]{3,2,1,0:T(8,128)(2,1)S(1)} %slice.60), channel_id=1, source_target_pairs={{0,4},{4,8},{8,12},{12,0},{1,5},{5,9},{9,13},{13,1},{2,6},{6,10},{... | collective-permute-start | bytes 2359304 | tf_op jit(solution)/shard_map/ppermute | solution.py:279
  50.9 21.7 %collective-permute-start.9 = (bf16[12,2,128,128]{3,2,1,0:T(8,128)(2,1)S(1)}, bf16[12,2,128,128]{3,2,1,0:T(8,128)(2,1)S(1)}, u32[]{:S(2)}, u32[]{:S(2)}) collective-permute-start(bf16[12,2,128,128]{3,2,1,0:T(8,128)(2,1)S(1)} %slice.61), channel_id=1, source_target_pairs={{0,12},{4,0},{8,4},{12,8},{1,13},{5,1},{9,5},{13,9},{2,14},{6,2},{... | collective-permute-start | bytes 2359304 | tf_op jit(solution)/shard_map/ppermute | solution.py:280
  53.6 19.7 %collective-permute-start.12 = (bf16[12,2,128,128]{3,2,1,0:T(8,128)(2,1)S(1)}, bf16[12,2,128,128]{3,2,1,0:T(8,128)(2,1)S(1)}, u32[]{:S(2)}, u32[]{:S(2)}) collective-permute-start(bf16[12,2,128,128]{3,2,1,0:T(8,128)(2,1)S(1)} %slice.80), channel_id=1, source_target_pairs={{0,1},{1,2},{2,3},{3,0},{4,5},{5,6},{6,7},{7,4},{8,9},{9,10},{10,1... | collective-permute-start | bytes 2359304 | tf_op jit(solution)/shard_map/ppermute | solution.py:279
  53.6 2.7 %copy-start.12 = (bf16[8,128,128]{2,1,0:T(8,128)(2,1)}, bf16[8,128,128]{2,1,0:T(8,128)(2,1)S(1)}, u32[]{:S(2)}) copy-start(bf16[8,128,128]{2,1,0:T(8,128)(2,1)S(1)} %collective-permute-done.16.refs_12_) | copy-start | bytes 786436
  53.7 19.7 %collective-permute-start.13 = (bf16[12,2,128,128]{3,2,1,0:T(8,128)(2,1)S(1)}, bf16[12,2,128,128]{3,2,1,0:T(8,128)(2,1)}, u32[]{:S(2)}, u32[]{:S(2)}) collective-permute-start(bf16[12,2,128,128]{3,2,1,0:T(8,128)(2,1)S(1)} %slice.81), channel_id=1, source_target_pairs={{0,3},{1,0},{2,1},{3,2},{4,7},{5,4},{6,5},{7,6},{8,11},{9,8},{10,9... | collective-permute-start | bytes 2359304 | tf_op jit(solution)/shard_map/ppermute | solution.py:280
  72.6 0.9 copy-start.6
  72.6 1.1 copy-start.7
  73.4 0.9 copy-start.8
  74.3 15.4 %copy-start.13 = (s32[32]{0:T(128)S(1)}, s32[32]{0:T(128)}, u32[]{:S(2)}) copy-start(s32[32]{0:T(128)} %units.3) | copy-start | bytes 388
  88.0 6.9 %copy-start = (bf16[4,2,2,128,128]{4,3,2,1,0:T(8,128)(2,1)S(1)}, bf16[4,2,2,128,128]{4,3,2,1,0:T(8,128)(2,1)}, u32[]{:S(2)}) copy-start(bf16[4,2,2,128,128]{4,3,2,1,0:T(8,128)(2,1)} %get-tuple-element.52) | copy-start | bytes 1572868
  88.0 3.3 %collective-permute-start.22 = (bf16[4,2,2,128,128]{4,3,2,1,0:T(8,128)(2,1)}, bf16[4,2,2,128,128]{4,3,2,1,0:T(8,128)(2,1)S(1)}, u32[]{:S(2)}, u32[]{:S(2)}) collective-permute-start(bf16[4,2,2,128,128]{4,3,2,1,0:T(8,128)(2,1)} %get-tuple-element.55), channel_id=1, source_target_pairs={{0,16},{16,0},{1,17},{17,1},{2,18},{18,2},{3,19},{19,3},{4,20},{20... | collective-permute-start | bytes 1572872 | tf_op jit(solution)/shard_map/ppermute | solution.py:307
  89.5 5.4 %collective-permute-start.18 = (bf16[4,2,2,128,128]{4,3,2,1,0:T(8,128)(2,1)}, bf16[4,2,2,128,128]{4,3,2,1,0:T(8,128)(2,1)S(1)}, u32[]{:S(2)}, u32[]{:S(2)}) collective-permute-start(bf16[4,2,2,128,128]{4,3,2,1,0:T(8,128)(2,1)} %get-tuple-element.53), channel_id=1, source_target_pairs={{0,16},{16,0},{1,17},{17,1},{2,18},{18,2},{3,19},{19,3},{4,20},{20... | collective-permute-start | bytes 1572872 | tf_op jit(solution)/shard_map/ppermute | solution.py:307
  92.5 5.4 %collective-permute-start.23 = (bf16[2,2,128,128]{3,2,1,0:T(8,128)(2,1)S(1)}, bf16[2,2,128,128]{3,2,1,0:T(8,128)(2,1)S(1)}, u32[]{:S(2)}, u32[]{:S(2)}) collective-permute-start(bf16[2,2,128,128]{3,2,1,0:T(8,128)(2,1)S(1)} %get-tuple-element.71), channel_id=1, source_target_pairs={{0,32},{32,64},{64,96},{96,0},{1,33},{33,65},{65,97},{97,1},{2,34}... | collective-permute-start | bytes 393224 | tf_op jit(solution)/shard_map/ppermute | solution.py:313
  92.8 5.9 %collective-permute-start.24 = (bf16[2,2,128,128]{3,2,1,0:T(8,128)(2,1)S(1)}, bf16[2,2,128,128]{3,2,1,0:T(8,128)(2,1)S(1)}, u32[]{:S(2)}, u32[]{:S(2)}) collective-permute-start(bf16[2,2,128,128]{3,2,1,0:T(8,128)(2,1)S(1)} %get-tuple-element.70), channel_id=1, source_target_pairs={{0,64},{32,96},{64,0},{96,32},{1,65},{33,97},{65,1},{97,33},{2,66}... | collective-permute-start | bytes 393224 | tf_op jit(solution)/shard_map/ppermute | solution.py:313
  94.9 6.9 %collective-permute-start.25 = (bf16[2,2,128,128]{3,2,1,0:T(8,128)(2,1)S(1)}, bf16[2,2,128,128]{3,2,1,0:T(8,128)(2,1)S(1)}, u32[]{:S(2)}, u32[]{:S(2)}) collective-permute-start(bf16[2,2,128,128]{3,2,1,0:T(8,128)(2,1)S(1)} %get-tuple-element.69), channel_id=1, source_target_pairs={{0,96},{32,0},{64,32},{96,64},{1,97},{33,1},{65,33},{97,65},{2,98}... | collective-permute-start | bytes 393224 | tf_op jit(solution)/shard_map/ppermute | solution.py:313
  95.1 13.8 %collective-permute-start.19 = (bf16[2,2,128,128]{3,2,1,0:T(8,128)(2,1)S(1)}, bf16[2,2,128,128]{3,2,1,0:T(8,128)(2,1)S(1)}, u32[]{:S(2)}, u32[]{:S(2)}) collective-permute-start(bf16[2,2,128,128]{3,2,1,0:T(8,128)(2,1)S(1)} %get-tuple-element.75), channel_id=1, source_target_pairs={{0,32},{32,64},{64,96},{96,0},{1,33},{33,65},{65,97},{97,1},{2,34}... | collective-permute-start | bytes 393224 | tf_op jit(solution)/shard_map/ppermute | solution.py:313
  97.8 11.1 %collective-permute-start.20 = (bf16[2,2,128,128]{3,2,1,0:T(8,128)(2,1)S(1)}, bf16[2,2,128,128]{3,2,1,0:T(8,128)(2,1)S(1)}, u32[]{:S(2)}, u32[]{:S(2)}) collective-permute-start(bf16[2,2,128,128]{3,2,1,0:T(8,128)(2,1)S(1)} %get-tuple-element.74), channel_id=1, source_target_pairs={{0,64},{32,96},{64,0},{96,32},{1,65},{33,97},{65,1},{97,33},{2,66}... | collective-permute-start | bytes 393224 | tf_op jit(solution)/shard_map/ppermute | solution.py:313
  98.0 11.0 %collective-permute-start.21 = (bf16[2,2,128,128]{3,2,1,0:T(8,128)(2,1)S(1)}, bf16[2,2,128,128]{3,2,1,0:T(8,128)(2,1)S(1)}, u32[]{:S(2)}, u32[]{:S(2)}) collective-permute-start(bf16[2,2,128,128]{3,2,1,0:T(8,128)(2,1)S(1)} %get-tuple-element.73), channel_id=1, source_target_pairs={{0,96},{32,0},{64,32},{96,64},{1,97},{33,1},{65,33},{97,65},{2,98}... | collective-permute-start | bytes 393224 | tf_op jit(solution)/shard_map/ppermute | solution.py:313
  101.9 8.8 %collective-permute-start.26 = (bf16[2,2,128,128]{3,2,1,0:T(8,128)(2,1)S(1)}, bf16[2,2,128,128]{3,2,1,0:T(8,128)(2,1)S(1)}, u32[]{:S(2)}, u32[]{:S(2)}) collective-permute-start(bf16[2,2,128,128]{3,2,1,0:T(8,128)(2,1)S(1)} %add_convert_fusion.1), channel_id=1, source_target_pairs={{0,0},{1,1},{2,16},{3,17},{16,2},{17,3},{18,18},{19,19},{4,4},{5,5... | collective-permute-start | bytes 393224 | tf_op jit(solution)/shard_map/ppermute | solution.py:347
  110.9 7.9 %collective-permute-start.27 = (bf16[2,2,128,128]{3,2,1,0:T(8,128)(2,1)S(1)}, bf16[2,2,128,128]{3,2,1,0:T(8,128)(2,1)S(1)}, u32[]{:S(2)}, u32[]{:S(2)}) collective-permute-start(bf16[2,2,128,128]{3,2,1,0:T(8,128)(2,1)S(1)} %add_convert_fusion), channel_id=1, source_target_pairs={{0,1},{1,0},{2,17},{3,16},{16,3},{17,2},{18,19},{19,18},{4,5},{5,4... | collective-permute-start | bytes 393224 | tf_op jit(solution)/shard_map/ppermute | solution.py:347

commit v6 on v5

--- a/solution.py
+++ b/solution.py
@@ -258,7 +258,7 @@
             pltpu.SemaphoreType.DMA((26,)),
             pltpu.SemaphoreType.DMA((64,)),
         ],
-        compiler_params=pltpu.CompilerParams(vmem_limit_bytes=58 * 2**20),
+        compiler_params=pltpu.CompilerParams(vmem_limit_bytes=59 * 2**20),
         cost_estimate=pl.CostEstimate(
             flops=32 * terms * 4 * B**3, bytes_accessed=14 * 2**20, transcendentals=0
         ),

time: 120 us -> 120 us (level)
  waiting for transfers between devices: 39.3 us -> 44.1 us
  starting transfers between devices: 44.6 us -> 41.7 us
  Pallas kernels: 30 us -> 28.6 us
    ppermute x2, waiting for transfers between devices: 4.39 us -> 8.28 us  [shards(): got.append(lax.ppermute(add_chips(*half), ('core', 'z'), perm))]
    ppermute x2, starting transfers between devices: 11.5 us -> 8.56 us  [shards(): got.append(lax.ppermute(add_chips(*half), ('core', 'z'), perm))]
    pallas_call x2, Pallas kernels: 30 us -> 28.6 us  [products(): pl.pallas_call(functools.partial(products_kernel, late, terms), out_shape...]
  transfers between devices with their start and end apart: 28 -> 28, of which waited for: 10 -> 10; matrix products, arithmetic and copies ran while one was open for 2% -> 2% of each run, Pallas kernels for 14% -> 13%
where the time goes in v6:
time: 120 us; the launch traced here: 119 us
  waiting for transfers between devices  44.1 us (37%)
  starting transfers between devices  41.7 us (35%)
  Pallas kernels  28.6 us (24%)
  other arithmetic  3.4 us (3%)
  local copies, waits for them, and re-layouts  1.31 us (1%)
    pallas_call x2, Pallas kernels, products(): pl.pallas_call(functools.partial(products_kernel, late, terms), out_shape...  28.6 us
    ppermute x3, waiting for transfers between devices, gather_wave(): row = [mine] + [lax.ppermute(mine, 'x', shifted(4, d)) for d in (1, 2, 3)]  17.8 us
    ppermute x2, starting transfers between devices, shards(): got.append(lax.ppermute(add_chips(*half), ('core', 'z'), perm))  8.56 us
    ppermute x2, waiting for transfers between devices, ring_near(): lax.ppermute(own, axis, shifted(4, 1))  8.51 us
    ppermute x2, waiting for transfers between devices, shards(): got.append(lax.ppermute(add_chips(*half), ('core', 'z'), perm))  8.28 us
    ppermute x4, starting transfers between devices, share_wave(): return (*row, *(lax.ppermute(part, 'core', swapped(2, 1)) for part in row))  6.92 us
    ppermute x6, starting transfers between devices, add_send(): lax.ppermute(part, 'x', shifted(4, d + 1))  6.04 us
    ppermute x2, starting transfers between devices, ring_far(): lax.ppermute(halves[1], axis, shifted(4, -1))  5.39 us
  transfers between devices with their start and end apart: 28, of which 10 were waited for; matrix products, arithmetic and copies ran while one was open for 2% of the time, Pallas kernels for 13%

profile of v6, /device:TPU:7, one launch (start us, length us, event | category | flops | bytes accessed | tf_op | source)
XLA Modules:
  0.0 119.4 jit_solution(11785348819349739430)
XLA Ops:
  0.0 1.0 dynamic-slice_bitcast_fusion
  1.0 1.4 %collective-permute-start = (bf16[2,128,128]{2,1,0:T(8,128)(2,1)S(1)}, bf16[2,128,128]{2,1,0:T(8,128)(2,1)S(1)}, u32[]{:S(2)}, u32[]{:S(2)}) collective-permute-start(bf16[2,128,128]{2,1,0:T(8,128)(2,1)S(1)} %get-tuple-element.67), channel_id=1, source_target_pairs={{0,4},{4,8},{8,12},{12,0},{1,5},{5,9},{9,13},{13,1},{2,6},{6,10},{... | collective-permute-start | bytes 196616 | tf_op jit(solution)/shard_map/ppermute | solution.py:292
  2.3 1.5 %collective-permute-start.1 = (bf16[2,128,128]{2,1,0:T(8,128)(2,1)S(1)}, bf16[2,128,128]{2,1,0:T(8,128)(2,1)S(1)}, u32[]{:S(2)}, u32[]{:S(2)}) collective-permute-start(bf16[2,128,128]{2,1,0:T(8,128)(2,1)S(1)} %get-tuple-element.66), channel_id=1, source_target_pairs={{0,12},{4,0},{8,4},{12,8},{1,13},{5,1},{9,5},{13,9},{2,14},{6,2},{... | collective-permute-start | bytes 196616 | tf_op jit(solution)/shard_map/ppermute | solution.py:292
  3.8 1.6 %collective-permute-start.2 = (bf16[2,128,128]{2,1,0:T(8,128)(2,1)S(1)}, bf16[2,128,128]{2,1,0:T(8,128)(2,1)S(1)}, u32[]{:S(2)}, u32[]{:S(2)}) collective-permute-start(bf16[2,128,128]{2,1,0:T(8,128)(2,1)S(1)} %get-tuple-element.68), channel_id=1, source_target_pairs={{0,8},{4,12},{8,0},{12,4},{1,9},{5,13},{9,1},{13,5},{2,10},{6,14},... | collective-permute-start | bytes 196616 | tf_op jit(solution)/shard_map/ppermute | solution.py:292
  5.4 3.0 %collective-permute-done.2 = bf16[2,128,128]{2,1,0:T(8,128)(2,1)S(1)} collective-permute-done((bf16[2,128,128]{2,1,0:T(8,128)(2,1)S(1)}, bf16[2,128,128]{2,1,0:T(8,128)(2,1)S(1)}, u32[]{:S(2)}, u32[]{:S(2)}) %collective-permute-start.2) | collective-permute-done | bytes 65568 | tf_op jit(solution)/shard_map/ppermute | solution.py:292
  8.5 0.3 collective-permute-start.6
  8.7 2.4 %collective-permute-start.7 = (bf16[24,2,128,128]{3,2,1,0:T(8,128)(2,1)}, bf16[24,2,128,128]{3,2,1,0:T(8,128)(2,1)S(1)}, u32[]{:S(2)}, u32[]{:S(2)}) collective-permute-start(bf16[24,2,128,128]{3,2,1,0:T(8,128)(2,1)} %refs_0_.1), channel_id=1, source_target_pairs={{0,12},{4,0},{8,4},{12,8},{1,13},{5,1},{9,5},{13,9},{2,14},{6,2},{... | collective-permute-start | bytes 4718600 | tf_op jit(solution)/shard_map/ppermute | solution.py:269
  11.1 1.6 %collective-permute-start.10 = (bf16[24,2,128,128]{3,2,1,0:T(8,128)(2,1)}, bf16[24,2,128,128]{3,2,1,0:T(8,128)(2,1)S(1)}, u32[]{:S(2)}, u32[]{:S(2)}) collective-permute-start(bf16[24,2,128,128]{3,2,1,0:T(8,128)(2,1)} %refs_5_), channel_id=1, source_target_pairs={{0,1},{1,2},{2,3},{3,0},{4,5},{5,6},{6,7},{7,4},{8,9},{9,10},{10,1... | collective-permute-start | bytes 4718600 | tf_op jit(solution)/shard_map/ppermute | solution.py:269
  12.8 2.1 %collective-permute-start.11 = (bf16[24,2,128,128]{3,2,1,0:T(8,128)(2,1)}, bf16[24,2,128,128]{3,2,1,0:T(8,128)(2,1)S(1)}, u32[]{:S(2)}, u32[]{:S(2)}) collective-permute-start(bf16[24,2,128,128]{3,2,1,0:T(8,128)(2,1)} %refs_5_), channel_id=1, source_target_pairs={{0,3},{1,0},{2,1},{3,2},{4,7},{5,4},{6,5},{7,6},{8,11},{9,8},{10,9... | collective-permute-start | bytes 4718600 | tf_op jit(solution)/shard_map/ppermute | solution.py:269
  15.0 0.3 collective-permute-start.3
  15.2 5.3 %collective-permute-done.3.refs_7_ = bf16[8,128,128]{2,1,0:T(8,128)(2,1)S(1)} collective-permute-done((bf16[8,128,128]{2,1,0:T(8,128)(2,1)S(1)}, bf16[8,128,128]{2,1,0:T(8,128)(2,1)S(1)}, u32[]{:S(2)}, u32[]{:S(2)}) %collective-permute-start.3) | collective-permute-done | bytes 262176 | tf_op jit(solution)/shard_map/ppermute | solution.py:298
  20.5 1.1 collective-permute-start.4
  21.7 5.6 %collective-permute-done.4.refs_8_ = bf16[8,128,128]{2,1,0:T(8,128)(2,1)S(1)} collective-permute-done((bf16[8,128,128]{2,1,0:T(8,128)(2,1)S(1)}, bf16[8,128,128]{2,1,0:T(8,128)(2,1)S(1)}, u32[]{:S(2)}, u32[]{:S(2)}) %collective-permute-start.4) | collective-permute-done | bytes 262176 | tf_op jit(solution)/shard_map/ppermute | solution.py:298
  27.3 0.8 collective-permute-start.5
  28.1 6.9 %collective-permute-done.5.refs_9_ = bf16[8,128,128]{2,1,0:T(8,128)(2,1)S(1)} collective-permute-done((bf16[8,128,128]{2,1,0:T(8,128)(2,1)S(1)}, bf16[8,128,128]{2,1,0:T(8,128)(2,1)S(1)}, u32[]{:S(2)}, u32[]{:S(2)}) %collective-permute-start.5) | collective-permute-done | bytes 262176 | tf_op jit(solution)/shard_map/ppermute | solution.py:298
  35.0 8.5 %collective-permute-done.6.refs_1_ = bf16[24,2,128,128]{3,2,1,0:T(8,128)(2,1)S(1)} collective-permute-done((bf16[24,2,128,128]{3,2,1,0:T(8,128)(2,1)}, bf16[24,2,128,128]{3,2,1,0:T(8,128)(2,1)S(1)}, u32[]{:S(2)}, u32[]{:S(2)}) %collective-permute-start.6) | collective-permute-done | bytes 1572896 | tf_op jit(solution)/shard_map/ppermute | solution.py:269
  43.5 3.2 %collective-permute-start.14 = (bf16[8,128,128]{2,1,0:T(8,128)(2,1)S(1)}, bf16[8,128,128]{2,1,0:T(8,128)(2,1)S(1)}, u32[]{:S(2)}, u32[]{:S(2)}) collective-permute-start(bf16[8,128,128]{2,1,0:T(8,128)(2,1)S(1)} %pad_maximum_fusion.refs_6_), channel_id=1, source_target_pairs={{0,16},{16,0},{1,17},{17,1},{2,18},{18,2},{3,19},{19,3},{4,20},{20... | collective-permute-start | bytes 786440 | tf_op jit(solution)/shard_map/ppermute | solution.py:303
  46.8 0.1 collective-permute-start.15
  46.9 0.4 collective-permute-start.16
  47.3 3.2 %collective-permute-start.17 = (bf16[8,128,128]{2,1,0:T(8,128)(2,1)S(1)}, bf16[8,128,128]{2,1,0:T(8,128)(2,1)}, u32[]{:S(2)}, u32[]{:S(2)}) collective-permute-start(bf16[8,128,128]{2,1,0:T(8,128)(2,1)S(1)} %collective-permute-done.5.refs_9_), channel_id=1, source_target_pairs={{0,16},{16,0},{1,17},{17,1},{2,18},{18,2},{3,19},{19,3},{4,20},{20... | collective-permute-start | bytes 786440 | tf_op jit(solution)/shard_map/ppermute | solution.py:303
  50.5 0.1 slice.61
  50.6 0.1 slice.80
  50.7 0.1 collective-permute-start.8
  50.9 2.7 %collective-permute-start.9 = (bf16[12,2,128,128]{3,2,1,0:T(8,128)(2,1)S(1)}, bf16[12,2,128,128]{3,2,1,0:T(8,128)(2,1)S(1)}, u32[]{:S(2)}, u32[]{:S(2)}) collective-permute-start(bf16[12,2,128,128]{3,2,1,0:T(8,128)(2,1)S(1)} %slice.61), channel_id=1, source_target_pairs={{0,12},{4,0},{8,4},{12,8},{1,13},{5,1},{9,5},{13,9},{2,14},{6,2},{... | collective-permute-start | bytes 2359304 | tf_op jit(solution)/shard_map/ppermute | solution.py:280
  53.7 2.7 %collective-permute-start.13 = (bf16[12,2,128,128]{3,2,1,0:T(8,128)(2,1)S(1)}, bf16[12,2,128,128]{3,2,1,0:T(8,128)(2,1)}, u32[]{:S(2)}, u32[]{:S(2)}) collective-permute-start(bf16[12,2,128,128]{3,2,1,0:T(8,128)(2,1)S(1)} %slice.81), channel_id=1, source_target_pairs={{0,3},{1,0},{2,1},{3,2},{4,7},{5,4},{6,5},{7,6},{8,11},{9,8},{10,9... | collective-permute-start | bytes 2359304 | tf_op jit(solution)/shard_map/ppermute | solution.py:280
  56.4 15.3 %shard_map.55 = (bf16[4,2,2,128,128]{4,3,2,1,0:T(8,128)(2,1)}, bf16[4,2,2,128,128]{4,3,2,1,0:T(8,128)(2,1)}, bf16[4,2,2,128,128]{4,3,2,1,0:T(8,128)(2,1)}, bf16[...) custom-call(s32[32,32]{1,0:T(8,128)} %allowed.3, s32[32]{0:T(128)} %units.3, bf16[24,2,128,128]{3,2,1,0:T(8,128)(2,1)} %refs_0_.1, ...), custom_call_target="tpu_custom_call" | custom-call | flops 6442450944 | bytes 14680064 | tf_op jit(solution)/shard_map/pallas_call | solution.py:242
  71.8 1.7 %collective-permute-done.12.refs_8_ = bf16[12,2,128,128]{3,2,1,0:T(8,128)(2,1)} collective-permute-done((bf16[12,2,128,128]{3,2,1,0:T(8,128)(2,1)S(1)}, bf16[12,2,128,128]{3,2,1,0:T(8,128)(2,1)}, u32[]{:S(2)}, u32[]{:S(2)}) %collective-permute-start.12) | collective-permute-done | bytes 786464 | tf_op jit(solution)/shard_map/ppermute | solution.py:279
  73.5 13.2 %shard_map.56 = (bf16[4,2,2,128,128]{4,3,2,1,0:T(8,128)(2,1)}, bf16[4,2,2,128,128]{4,3,2,1,0:T(8,128)(2,1)}, bf16[4,2,2,128,128]{4,3,2,1,0:T(8,128)(2,1)}, bf16[4,2,2,128,128]{4,3,2,1,0:T(8,128)(2,1)}) custom-call(s32[32,32]{1,0:T(8,128)} %allowed.3, s32[32]{0:T(128)} %units.3, ...), custom_call_target="tpu_custom_call", output_to_operand_aliasing={{0}: (13, {}), {1}: (14, {}), {2}: (15, {}), {3}: (16, {})} | custom-call | flops 6442450944 | bytes 14680064 | tf_op jit(solution)/shard_map/pallas_call | solution.py:242
  86.8 1.5 %collective-permute-start.22 = (bf16[4,2,2,128,128]{4,3,2,1,0:T(8,128)(2,1)}, bf16[4,2,2,128,128]{4,3,2,1,0:T(8,128)(2,1)S(1)}, u32[]{:S(2)}, u32[]{:S(2)}) collective-permute-start(bf16[4,2,2,128,128]{4,3,2,1,0:T(8,128)(2,1)} %get-tuple-element.55), channel_id=1, source_target_pairs={{0,16},{16,0},{1,17},{17,1},{2,18},{18,2},{3,19},{19,3},{4,20},{20... | collective-permute-start | bytes 1572872 | tf_op jit(solution)/shard_map/ppermute | solution.py:307
  88.3 0.1 collective-permute-start.18
  88.4 0.1 iota_compare_fusion
  88.5 1.6 %collective-permute-done.22 = bf16[4,2,2,128,128]{4,3,2,1,0:T(8,128)(2,1)S(1)} collective-permute-done((bf16[4,2,2,128,128]{4,3,2,1,0:T(8,128)(2,1)}, bf16[4,2,2,128,128]{4,3,2,1,0:T(8,128)(2,1)S(1)}, u32[]{:S(2)}, u32[]{:S(2)}) %collective-permute-start.22) | collective-permute-done | bytes 524320 | tf_op jit(solution)/shard_map/ppermute | solution.py:307
  90.0 1.2 %fusion.5 = (bf16[2,2,128,128]{3,2,1,0:T(8,128)(2,1)S(1)}, bf16[2,2,128,128]{3,2,1,0:T(8,128)(2,1)S(1)}, bf16[2,2,128,128]{3,2,1,0:T(8,128)(2,1)S(1)}, f32[2,2,128,128]{3,2,1,0:T(8,128)S(1)}) fusion(bf16[4,2,2,128,128]{4,3,2,1,0:T(8,128)(2,1)S(1)} %collective-permute-done.22, bf16[4,2,2,128,128]{4,3,2,1,0:T(8,128)(2,1)} %get-tuple-element.54), kind=kLoop, calls=%fused_computation.17 | loop fusion | flops 983040 | bytes 1703936 | tf_op jit(solution)/shard_map/convert_element_type | solution.py:309
  91.3 0.3 collective-permute-start.23
  91.5 2.1 %collective-permute-start.24 = (bf16[2,2,128,128]{3,2,1,0:T(8,128)(2,1)S(1)}, bf16[2,2,128,128]{3,2,1,0:T(8,128)(2,1)S(1)}, u32[]{:S(2)}, u32[]{:S(2)}) collective-permute-start(bf16[2,2,128,128]{3,2,1,0:T(8,128)(2,1)S(1)} %get-tuple-element.70), channel_id=1, source_target_pairs={{0,64},{32,96},{64,0},{96,32},{1,65},{33,97},{65,1},{97,33},{2,66}... | collective-permute-start | bytes 393224 | tf_op jit(solution)/shard_map/ppermute | solution.py:313
  93.7 0.1 fusion.2
  93.8 2.7 %collective-permute-start.19 = (bf16[2,2,128,128]{3,2,1,0:T(8,128)(2,1)S(1)}, bf16[2,2,128,128]{3,2,1,0:T(8,128)(2,1)S(1)}, u32[]{:S(2)}, u32[]{:S(2)}) collective-permute-start(bf16[2,2,128,128]{3,2,1,0:T(8,128)(2,1)S(1)} %get-tuple-element.75), channel_id=1, source_target_pairs={{0,32},{32,64},{64,96},{96,0},{1,33},{33,65},{65,97},{97,1},{2,34}... | collective-permute-start | bytes 393224 | tf_op jit(solution)/shard_map/ppermute | solution.py:313
  96.6 0.1 collective-permute-start.20
  96.7 0.8 collective-permute-start.21
  97.5 3.1 %collective-permute-done.25 = bf16[2,2,128,128]{3,2,1,0:T(8,128)(2,1)S(1)} collective-permute-done((bf16[2,2,128,128]{3,2,1,0:T(8,128)(2,1)S(1)}, bf16[2,2,128,128]{3,2,1,0:T(8,128)(2,1)S(1)}, u32[]{:S(2)}, u32[]{:S(2)}) %collective-permute-start.25) | collective-permute-done | bytes 131104 | tf_op jit(solution)/shard_map/ppermute | solution.py:313
  100.7 8.4 %collective-permute-start.26 = (bf16[2,2,128,128]{3,2,1,0:T(8,128)(2,1)S(1)}, bf16[2,2,128,128]{3,2,1,0:T(8,128)(2,1)S(1)}, u32[]{:S(2)}, u32[]{:S(2)}) collective-permute-start(bf16[2,2,128,128]{3,2,1,0:T(8,128)(2,1)S(1)} %add_convert_fusion.1), channel_id=1, source_target_pairs={{0,0},{1,1},{2,16},{3,17},{16,2},{17,3},{18,18},{19,19},{4,4},{5,5... | collective-permute-start | bytes 393224 | tf_op jit(solution)/shard_map/ppermute | solution.py:347
  109.1 0.8 dynamic-slice_compare_fusion
  109.9 2.8 %collective-permute-done.26 = bf16[2,2,128,128]{3,2,1,0:T(8,128)(2,1)S(1)} collective-permute-done((bf16[2,2,128,128]{3,2,1,0:T(8,128)(2,1)S(1)}, bf16[2,2,128,128]{3,2,1,0:T(8,128)(2,1)S(1)}, u32[]{:S(2)}, u32[]{:S(2)}) %collective-permute-start.26) | collective-permute-done | bytes 131104 | tf_op jit(solution)/shard_map/ppermute | solution.py:347
  112.7 0.1 add_convert_fusion
  112.8 0.1 collective-permute-start.27
  113.0 0.1 broadcast_and_fusion
  113.0 5.5 %collective-permute-done.27 = bf16[2,2,128,128]{3,2,1,0:T(8,128)(2,1)S(1)} collective-permute-done((bf16[2,2,128,128]{3,2,1,0:T(8,128)(2,1)S(1)}, bf16[2,2,128,128]{3,2,1,0:T(8,128)(2,1)S(1)}, u32[]{:S(2)}, u32[]{:S(2)}) %collective-permute-start.27) | collective-permute-done | bytes 131104 | tf_op jit(solution)/shard_map/ppermute | solution.py:347
  118.5 0.9 and_select_fusion
  (58 shorter events, 0.4 us)
Async XLA Ops:
  1.0 4.5 %collective-permute-start = (bf16[2,128,128]{2,1,0:T(8,128)(2,1)S(1)}, bf16[2,128,128]{2,1,0:T(8,128)(2,1)S(1)}, u32[]{:S(2)}, u32[]{:S(2)}) collective-permute-start(bf16[2,128,128]{2,1,0:T(8,128)(2,1)S(1)} %get-tuple-element.67), channel_id=1, source_target_pairs={{0,4},{4,8},{8,12},{12,0},{1,5},{5,9},{9,13},{13,1},{2,6},{6,10},{... | collective-permute-start | bytes 196616 | tf_op jit(solution)/shard_map/ppermute | solution.py:292
  2.3 3.1 %collective-permute-start.1 = (bf16[2,128,128]{2,1,0:T(8,128)(2,1)S(1)}, bf16[2,128,128]{2,1,0:T(8,128)(2,1)S(1)}, u32[]{:S(2)}, u32[]{:S(2)}) collective-permute-start(bf16[2,128,128]{2,1,0:T(8,128)(2,1)S(1)} %get-tuple-element.66), channel_id=1, source_target_pairs={{0,12},{4,0},{8,4},{12,8},{1,13},{5,1},{9,5},{13,9},{2,14},{6,2},{... | collective-permute-start | bytes 196616 | tf_op jit(solution)/shard_map/ppermute | solution.py:292
  3.8 4.6 %collective-permute-start.2 = (bf16[2,128,128]{2,1,0:T(8,128)(2,1)S(1)}, bf16[2,128,128]{2,1,0:T(8,128)(2,1)S(1)}, u32[]{:S(2)}, u32[]{:S(2)}) collective-permute-start(bf16[2,128,128]{2,1,0:T(8,128)(2,1)S(1)} %get-tuple-element.68), channel_id=1, source_target_pairs={{0,8},{4,12},{8,0},{12,4},{1,9},{5,13},{9,1},{13,5},{2,10},{6,14},... | collective-permute-start | bytes 196616 | tf_op jit(solution)/shard_map/ppermute | solution.py:292
  8.5 35.1 %collective-permute-start.6 = (bf16[24,2,128,128]{3,2,1,0:T(8,128)(2,1)}, bf16[24,2,128,128]{3,2,1,0:T(8,128)(2,1)S(1)}, u32[]{:S(2)}, u32[]{:S(2)}) collective-permute-start(bf16[24,2,128,128]{3,2,1,0:T(8,128)(2,1)} %refs_0_.1), channel_id=1, source_target_pairs={{0,4},{4,8},{8,12},{12,0},{1,5},{5,9},{9,13},{13,1},{2,6},{6,10},{... | collective-permute-start | bytes 4718600 | tf_op jit(solution)/shard_map/ppermute | solution.py:269
  8.7 34.8 %collective-permute-start.7 = (bf16[24,2,128,128]{3,2,1,0:T(8,128)(2,1)}, bf16[24,2,128,128]{3,2,1,0:T(8,128)(2,1)S(1)}, u32[]{:S(2)}, u32[]{:S(2)}) collective-permute-start(bf16[24,2,128,128]{3,2,1,0:T(8,128)(2,1)} %refs_0_.1), channel_id=1, source_target_pairs={{0,12},{4,0},{8,4},{12,8},{1,13},{5,1},{9,5},{13,9},{2,14},{6,2},{... | collective-permute-start | bytes 4718600 | tf_op jit(solution)/shard_map/ppermute | solution.py:269
  11.1 36.1 %collective-permute-start.10 = (bf16[24,2,128,128]{3,2,1,0:T(8,128)(2,1)}, bf16[24,2,128,128]{3,2,1,0:T(8,128)(2,1)S(1)}, u32[]{:S(2)}, u32[]{:S(2)}) collective-permute-start(bf16[24,2,128,128]{3,2,1,0:T(8,128)(2,1)} %refs_5_), channel_id=1, source_target_pairs={{0,1},{1,2},{2,3},{3,0},{4,5},{5,6},{6,7},{7,4},{8,9},{9,10},{10,1... | collective-permute-start | bytes 4718600 | tf_op jit(solution)/shard_map/ppermute | solution.py:269
  12.8 37.9 %collective-permute-start.11 = (bf16[24,2,128,128]{3,2,1,0:T(8,128)(2,1)}, bf16[24,2,128,128]{3,2,1,0:T(8,128)(2,1)S(1)}, u32[]{:S(2)}, u32[]{:S(2)}) collective-permute-start(bf16[24,2,128,128]{3,2,1,0:T(8,128)(2,1)} %refs_5_), channel_id=1, source_target_pairs={{0,3},{1,0},{2,1},{3,2},{4,7},{5,4},{6,5},{7,6},{8,11},{9,8},{10,9... | collective-permute-start | bytes 4718600 | tf_op jit(solution)/shard_map/ppermute | solution.py:269
  14.9 41.5 %copy-start.5 = (bf16[8,128,128]{2,1,0:T(8,128)(2,1)}, bf16[8,128,128]{2,1,0:T(8,128)(2,1)S(1)}, u32[]{:S(2)}) copy-start(bf16[8,128,128]{2,1,0:T(8,128)(2,1)S(1)} %pad_maximum_fusion.refs_6_) | copy-start | bytes 786436
  15.0 5.6 %collective-permute-start.3 = (bf16[8,128,128]{2,1,0:T(8,128)(2,1)S(1)}, bf16[8,128,128]{2,1,0:T(8,128)(2,1)S(1)}, u32[]{:S(2)}, u32[]{:S(2)}) collective-permute-start(bf16[8,128,128]{2,1,0:T(8,128)(2,1)S(1)} %pad_maximum_fusion.refs_6_), channel_id=1, source_target_pairs={{0,32},{32,64},{64,96},{96,0},{1,33},{33,65},{65,97},{97,1},{2,34}... | collective-permute-start | bytes 786440 | tf_op jit(solution)/shard_map/ppermute | solution.py:298
  20.5 35.8 %copy-start.8 = (bf16[8,128,128]{2,1,0:T(8,128)(2,1)}, bf16[8,128,128]{2,1,0:T(8,128)(2,1)S(1)}, u32[]{:S(2)}) copy-start(bf16[8,128,128]{2,1,0:T(8,128)(2,1)S(1)} %collective-permute-done.3.refs_7_) | copy-start | bytes 786436
  20.5 6.7 %collective-permute-start.4 = (bf16[8,128,128]{2,1,0:T(8,128)(2,1)S(1)}, bf16[8,128,128]{2,1,0:T(8,128)(2,1)S(1)}, u32[]{:S(2)}, u32[]{:S(2)}) collective-permute-start(bf16[8,128,128]{2,1,0:T(8,128)(2,1)S(1)} %pad_maximum_fusion.refs_6_), channel_id=1, source_target_pairs={{0,64},{32,96},{64,0},{96,32},{1,65},{33,97},{65,1},{97,33},{2,66}... | collective-permute-start | bytes 786440 | tf_op jit(solution)/shard_map/ppermute | solution.py:298
  27.3 29.1 %copy-start.9 = (bf16[8,128,128]{2,1,0:T(8,128)(2,1)}, bf16[8,128,128]{2,1,0:T(8,128)(2,1)S(1)}, u32[]{:S(2)}) copy-start(bf16[8,128,128]{2,1,0:T(8,128)(2,1)S(1)} %collective-permute-done.4.refs_8_) | copy-start | bytes 786436
  27.3 7.7 %collective-permute-start.5 = (bf16[8,128,128]{2,1,0:T(8,128)(2,1)S(1)}, bf16[8,128,128]{2,1,0:T(8,128)(2,1)S(1)}, u32[]{:S(2)}, u32[]{:S(2)}) collective-permute-start(bf16[8,128,128]{2,1,0:T(8,128)(2,1)S(1)} %pad_maximum_fusion.refs_6_), channel_id=1, source_target_pairs={{0,96},{32,0},{64,32},{96,64},{1,97},{33,1},{65,33},{97,65},{2,98}... | collective-permute-start | bytes 786440 | tf_op jit(solution)/shard_map/ppermute | solution.py:298
  35.0 21.3 %copy-start.10 = (bf16[8,128,128]{2,1,0:T(8,128)(2,1)}, bf16[8,128,128]{2,1,0:T(8,128)(2,1)S(1)}, u32[]{:S(2)}) copy-start(bf16[8,128,128]{2,1,0:T(8,128)(2,1)S(1)} %collective-permute-done.5.refs_9_) | copy-start | bytes 786436
  43.5 7.1 %copy-start.1 = (bf16[24,2,128,128]{3,2,1,0:T(8,128)(2,1)}, bf16[24,2,128,128]{3,2,1,0:T(8,128)(2,1)S(1)}, u32[]{:S(2)}) copy-start(bf16[24,2,128,128]{3,2,1,0:T(8,128)(2,1)S(1)} %collective-permute-done.6.refs_1_) | copy-start | bytes 4718596
  43.5 7.1 %copy-start.2 = (bf16[24,2,128,128]{3,2,1,0:T(8,128)(2,1)}, bf16[24,2,128,128]{3,2,1,0:T(8,128)(2,1)S(1)}, u32[]{:S(2)}) copy-start(bf16[24,2,128,128]{3,2,1,0:T(8,128)(2,1)S(1)} %collective-permute-done.7.refs_2_) | copy-start | bytes 4718596
  43.5 7.4 %collective-permute-start.14 = (bf16[8,128,128]{2,1,0:T(8,128)(2,1)S(1)}, bf16[8,128,128]{2,1,0:T(8,128)(2,1)S(1)}, u32[]{:S(2)}, u32[]{:S(2)}) collective-permute-start(bf16[8,128,128]{2,1,0:T(8,128)(2,1)S(1)} %pad_maximum_fusion.refs_6_), channel_id=1, source_target_pairs={{0,16},{16,0},{1,17},{17,1},{2,18},{18,2},{3,19},{19,3},{4,20},{20... | collective-permute-start | bytes 786440 | tf_op jit(solution)/shard_map/ppermute | solution.py:303
  46.8 6.9 %collective-permute-start.15 = (bf16[8,128,128]{2,1,0:T(8,128)(2,1)S(1)}, bf16[8,128,128]{2,1,0:T(8,128)(2,1)S(1)}, u32[]{:S(2)}, u32[]{:S(2)}) collective-permute-start(bf16[8,128,128]{2,1,0:T(8,128)(2,1)S(1)} %collective-permute-done.3.refs_7_), channel_id=1, source_target_pairs={{0,16},{16,0},{1,17},{17,1},{2,18},{18,2},{3,19},{19,3},{4,20},{20... | collective-permute-start | bytes 786440 | tf_op jit(solution)/shard_map/ppermute | solution.py:303
  46.9 6.8 %collective-permute-start.16 = (bf16[8,128,128]{2,1,0:T(8,128)(2,1)S(1)}, bf16[8,128,128]{2,1,0:T(8,128)(2,1)S(1)}, u32[]{:S(2)}, u32[]{:S(2)}) collective-permute-start(bf16[8,128,128]{2,1,0:T(8,128)(2,1)S(1)} %collective-permute-done.4.refs_8_), channel_id=1, source_target_pairs={{0,16},{16,0},{1,17},{17,1},{2,18},{18,2},{3,19},{19,3},{4,20},{20... | collective-permute-start | bytes 786440 | tf_op jit(solution)/shard_map/ppermute | solution.py:303
  47.3 9.0 %copy-start.3 = (bf16[24,2,128,128]{3,2,1,0:T(8,128)(2,1)}, bf16[24,2,128,128]{3,2,1,0:T(8,128)(2,1)S(1)}, u32[]{:S(2)}) copy-start(bf16[24,2,128,128]{3,2,1,0:T(8,128)(2,1)S(1)} %collective-permute-done.10.refs_4_.refs_6_) | copy-start | bytes 4718596
  47.3 9.1 %collective-permute-start.17 = (bf16[8,128,128]{2,1,0:T(8,128)(2,1)S(1)}, bf16[8,128,128]{2,1,0:T(8,128)(2,1)}, u32[]{:S(2)}, u32[]{:S(2)}) collective-permute-start(bf16[8,128,128]{2,1,0:T(8,128)(2,1)S(1)} %collective-permute-done.5.refs_9_), channel_id=1, source_target_pairs={{0,16},{16,0},{1,17},{17,1},{2,18},{18,2},{3,19},{19,3},{4,20},{20... | collective-permute-start | bytes 786440 | tf_op jit(solution)/shard_map/ppermute | solution.py:303
  50.7 5.6 %copy-start.4 = (bf16[24,2,128,128]{3,2,1,0:T(8,128)(2,1)}, bf16[24,2,128,128]{3,2,1,0:T(8,128)(2,1)S(1)}, u32[]{:S(2)}) copy-start(bf16[24,2,128,128]{3,2,1,0:T(8,128)(2,1)S(1)} %collective-permute-done.11.refs_5_.refs_7_) | copy-start | bytes 4718596
  50.7 21.0 %collective-permute-start.8 = (bf16[12,2,128,128]{3,2,1,0:T(8,128)(2,1)S(1)}, bf16[12,2,128,128]{3,2,1,0:T(8,128)(2,1)S(1)}, u32[]{:S(2)}, u32[]{:S(2)}) collective-permute-start(bf16[12,2,128,128]{3,2,1,0:T(8,128)(2,1)S(1)} %slice.60), channel_id=1, source_target_pairs={{0,4},{4,8},{8,12},{12,0},{1,5},{5,9},{9,13},{13,1},{2,6},{6,10},{... | collective-permute-start | bytes 2359304 | tf_op jit(solution)/shard_map/ppermute | solution.py:279
  50.9 5.5 %copy-start.11 = (bf16[8,128,128]{2,1,0:T(8,128)(2,1)}, bf16[8,128,128]{2,1,0:T(8,128)(2,1)S(1)}, u32[]{:S(2)}) copy-start(bf16[8,128,128]{2,1,0:T(8,128)(2,1)S(1)} %collective-permute-done.14.refs_10_) | copy-start | bytes 786436
  50.9 20.9 %collective-permute-start.9 = (bf16[12,2,128,128]{3,2,1,0:T(8,128)(2,1)S(1)}, bf16[12,2,128,128]{3,2,1,0:T(8,128)(2,1)S(1)}, u32[]{:S(2)}, u32[]{:S(2)}) collective-permute-start(bf16[12,2,128,128]{3,2,1,0:T(8,128)(2,1)S(1)} %slice.61), channel_id=1, source_target_pairs={{0,12},{4,0},{8,4},{12,8},{1,13},{5,1},{9,5},{13,9},{2,14},{6,2},{... | collective-permute-start | bytes 2359304 | tf_op jit(solution)/shard_map/ppermute | solution.py:280
  53.6 2.7 %copy-start.12 = (bf16[8,128,128]{2,1,0:T(8,128)(2,1)}, bf16[8,128,128]{2,1,0:T(8,128)(2,1)S(1)}, u32[]{:S(2)}) copy-start(bf16[8,128,128]{2,1,0:T(8,128)(2,1)S(1)} %collective-permute-done.15.refs_11_) | copy-start | bytes 786436
  53.6 19.9 %collective-permute-start.12 = (bf16[12,2,128,128]{3,2,1,0:T(8,128)(2,1)S(1)}, bf16[12,2,128,128]{3,2,1,0:T(8,128)(2,1)}, u32[]{:S(2)}, u32[]{:S(2)}) collective-permute-start(bf16[12,2,128,128]{3,2,1,0:T(8,128)(2,1)S(1)} %slice.80), channel_id=1, source_target_pairs={{0,1},{1,2},{2,3},{3,0},{4,5},{5,6},{6,7},{7,4},{8,9},{9,10},{10,1... | collective-permute-start | bytes 2359304 | tf_op jit(solution)/shard_map/ppermute | solution.py:279
  53.7 2.7 %copy-start.13 = (bf16[8,128,128]{2,1,0:T(8,128)(2,1)}, bf16[8,128,128]{2,1,0:T(8,128)(2,1)S(1)}, u32[]{:S(2)}) copy-start(bf16[8,128,128]{2,1,0:T(8,128)(2,1)S(1)} %collective-permute-done.16.refs_12_) | copy-start | bytes 786436
  53.7 19.8 %collective-permute-start.13 = (bf16[12,2,128,128]{3,2,1,0:T(8,128)(2,1)S(1)}, bf16[12,2,128,128]{3,2,1,0:T(8,128)(2,1)}, u32[]{:S(2)}, u32[]{:S(2)}) collective-permute-start(bf16[12,2,128,128]{3,2,1,0:T(8,128)(2,1)S(1)} %slice.81), channel_id=1, source_target_pairs={{0,3},{1,0},{2,1},{3,2},{4,7},{5,4},{6,5},{7,6},{8,11},{9,8},{10,9... | collective-permute-start | bytes 2359304 | tf_op jit(solution)/shard_map/ppermute | solution.py:280
  71.7 1.8 %copy-start.6 = (bf16[12,2,128,128]{3,2,1,0:T(8,128)(2,1)}, bf16[12,2,128,128]{3,2,1,0:T(8,128)(2,1)S(1)}, u32[]{:S(2)}) copy-start(bf16[12,2,128,128]{3,2,1,0:T(8,128)(2,1)S(1)} %collective-permute-done.8.refs_3_) | copy-start | bytes 2359300
  71.8 1.7 %copy-start.7 = (bf16[12,2,128,128]{3,2,1,0:T(8,128)(2,1)}, bf16[12,2,128,128]{3,2,1,0:T(8,128)(2,1)S(1)}, u32[]{:S(2)}) copy-start(bf16[12,2,128,128]{3,2,1,0:T(8,128)(2,1)S(1)} %collective-permute-done.9.refs_4_) | copy-start | bytes 2359300
  73.5 14.9 %copy-start.14 = (s32[32]{0:T(128)S(1)}, s32[32]{0:T(128)}, u32[]{:S(2)}) copy-start(s32[32]{0:T(128)} %units.3) | copy-start | bytes 388
  86.8 6.9 %copy-start = (bf16[4,2,2,128,128]{4,3,2,1,0:T(8,128)(2,1)S(1)}, bf16[4,2,2,128,128]{4,3,2,1,0:T(8,128)(2,1)}, u32[]{:S(2)}) copy-start(bf16[4,2,2,128,128]{4,3,2,1,0:T(8,128)(2,1)} %get-tuple-element.52) | copy-start | bytes 1572868
  86.8 3.2 %collective-permute-start.22 = (bf16[4,2,2,128,128]{4,3,2,1,0:T(8,128)(2,1)}, bf16[4,2,2,128,128]{4,3,2,1,0:T(8,128)(2,1)S(1)}, u32[]{:S(2)}, u32[]{:S(2)}) collective-permute-start(bf16[4,2,2,128,128]{4,3,2,1,0:T(8,128)(2,1)} %get-tuple-element.55), channel_id=1, source_target_pairs={{0,16},{16,0},{1,17},{17,1},{2,18},{18,2},{3,19},{19,3},{4,20},{20... | collective-permute-start | bytes 1572872 | tf_op jit(solution)/shard_map/ppermute | solution.py:307
  88.3 5.4 %collective-permute-start.18 = (bf16[4,2,2,128,128]{4,3,2,1,0:T(8,128)(2,1)}, bf16[4,2,2,128,128]{4,3,2,1,0:T(8,128)(2,1)S(1)}, u32[]{:S(2)}, u32[]{:S(2)}) collective-permute-start(bf16[4,2,2,128,128]{4,3,2,1,0:T(8,128)(2,1)} %get-tuple-element.53), channel_id=1, source_target_pairs={{0,16},{16,0},{1,17},{17,1},{2,18},{18,2},{3,19},{19,3},{4,20},{20... | collective-permute-start | bytes 1572872 | tf_op jit(solution)/shard_map/ppermute | solution.py:307
  91.3 5.4 %collective-permute-start.23 = (bf16[2,2,128,128]{3,2,1,0:T(8,128)(2,1)S(1)}, bf16[2,2,128,128]{3,2,1,0:T(8,128)(2,1)S(1)}, u32[]{:S(2)}, u32[]{:S(2)}) collective-permute-start(bf16[2,2,128,128]{3,2,1,0:T(8,128)(2,1)S(1)} %get-tuple-element.71), channel_id=1, source_target_pairs={{0,32},{32,64},{64,96},{96,0},{1,33},{33,65},{65,97},{97,1},{2,34}... | collective-permute-start | bytes 393224 | tf_op jit(solution)/shard_map/ppermute | solution.py:313
  91.5 5.9 %collective-permute-start.24 = (bf16[2,2,128,128]{3,2,1,0:T(8,128)(2,1)S(1)}, bf16[2,2,128,128]{3,2,1,0:T(8,128)(2,1)S(1)}, u32[]{:S(2)}, u32[]{:S(2)}) collective-permute-start(bf16[2,2,128,128]{3,2,1,0:T(8,128)(2,1)S(1)} %get-tuple-element.70), channel_id=1, source_target_pairs={{0,64},{32,96},{64,0},{96,32},{1,65},{33,97},{65,1},{97,33},{2,66}... | collective-permute-start | bytes 393224 | tf_op jit(solution)/shard_map/ppermute | solution.py:313
  93.7 6.9 %collective-permute-start.25 = (bf16[2,2,128,128]{3,2,1,0:T(8,128)(2,1)S(1)}, bf16[2,2,128,128]{3,2,1,0:T(8,128)(2,1)S(1)}, u32[]{:S(2)}, u32[]{:S(2)}) collective-permute-start(bf16[2,2,128,128]{3,2,1,0:T(8,128)(2,1)S(1)} %get-tuple-element.69), channel_id=1, source_target_pairs={{0,96},{32,0},{64,32},{96,64},{1,97},{33,1},{65,33},{97,65},{2,98}... | collective-permute-start | bytes 393224 | tf_op jit(solution)/shard_map/ppermute | solution.py:313
  93.8 16.1 %collective-permute-start.19 = (bf16[2,2,128,128]{3,2,1,0:T(8,128)(2,1)S(1)}, bf16[2,2,128,128]{3,2,1,0:T(8,128)(2,1)S(1)}, u32[]{:S(2)}, u32[]{:S(2)}) collective-permute-start(bf16[2,2,128,128]{3,2,1,0:T(8,128)(2,1)S(1)} %get-tuple-element.75), channel_id=1, source_target_pairs={{0,32},{32,64},{64,96},{96,0},{1,33},{33,65},{65,97},{97,1},{2,34}... | collective-permute-start | bytes 393224 | tf_op jit(solution)/shard_map/ppermute | solution.py:313
  96.6 13.3 %collective-permute-start.20 = (bf16[2,2,128,128]{3,2,1,0:T(8,128)(2,1)S(1)}, bf16[2,2,128,128]{3,2,1,0:T(8,128)(2,1)S(1)}, u32[]{:S(2)}, u32[]{:S(2)}) collective-permute-start(bf16[2,2,128,128]{3,2,1,0:T(8,128)(2,1)S(1)} %get-tuple-element.74), channel_id=1, source_target_pairs={{0,64},{32,96},{64,0},{96,32},{1,65},{33,97},{65,1},{97,33},{2,66}... | collective-permute-start | bytes 393224 | tf_op jit(solution)/shard_map/ppermute | solution.py:313
  96.7 13.2 %collective-permute-start.21 = (bf16[2,2,128,128]{3,2,1,0:T(8,128)(2,1)S(1)}, bf16[2,2,128,128]{3,2,1,0:T(8,128)(2,1)S(1)}, u32[]{:S(2)}, u32[]{:S(2)}) collective-permute-start(bf16[2,2,128,128]{3,2,1,0:T(8,128)(2,1)S(1)} %get-tuple-element.73), channel_id=1, source_target_pairs={{0,96},{32,0},{64,32},{96,64},{1,97},{33,1},{65,33},{97,65},{2,98}... | collective-permute-start | bytes 393224 | tf_op jit(solution)/shard_map/ppermute | solution.py:313
  100.7 12.1 %collective-permute-start.26 = (bf16[2,2,128,128]{3,2,1,0:T(8,128)(2,1)S(1)}, bf16[2,2,128,128]{3,2,1,0:T(8,128)(2,1)S(1)}, u32[]{:S(2)}, u32[]{:S(2)}) collective-permute-start(bf16[2,2,128,128]{3,2,1,0:T(8,128)(2,1)S(1)} %add_convert_fusion.1), channel_id=1, source_target_pairs={{0,0},{1,1},{2,16},{3,17},{16,2},{17,3},{18,18},{19,19},{4,4},{5,5... | collective-permute-start | bytes 393224 | tf_op jit(solution)/shard_map/ppermute | solution.py:347
  112.8 5.7 %collective-permute-start.27 = (bf16[2,2,128,128]{3,2,1,0:T(8,128)(2,1)S(1)}, bf16[2,2,128,128]{3,2,1,0:T(8,128)(2,1)S(1)}, u32[]{:S(2)}, u32[]{:S(2)}) collective-permute-start(bf16[2,2,128,128]{3,2,1,0:T(8,128)(2,1)S(1)} %add_convert_fusion), channel_id=1, source_target_pairs={{0,1},{1,0},{2,17},{3,16},{16,3},{17,2},{18,19},{19,18},{4,5},{5,4... | collective-permute-start | bytes 393224 | tf_op jit(solution)/shard_map/ppermute | solution.py:347
